TPU v7x, 256 devices: a whole 4x4x8 slice. The times are simulated.
256 devices in a mesh: blk: 64 (over z, y_lo, x), col: 4 (over y_hi, core).
Axes of the slice: x: 4, y: 4 (y_hi: 2, y_lo: 2; y = y_hi * 2 + y_lo), z: 8, core: 2. Of those that a mesh axis runs over, the one named last changes fastest.
Arguments:
- slab: float32 [131072, 1024], P('blk', 'col'), may hold values from -6 to 6
- angles: float32 [4, 65536], P(None, 'blk'), may hold values from -3.140625 to 3.140625
- pairing: int32 [4], replicated, may hold values from 0 to 1, as said below
- band_offsets: int32 [8], replicated, may hold values from 1 to 512, as said below
- band_weights: float32 [8], replicated, may hold values from -0.0625 to 0.0625
Outputs:
- evolved: float32 [131072, 1024], P('blk', 'col')
- angle_gradient: float32 [4, 65536], P(None, 'blk')
Inputs may be any that keep to these rules, and one draw needn't show every extreme that they name: `pairing`: the entries alternate between 0 and 1 from one layer to the next. `band_offsets`: exactly one entry equals 512.
All inputs are finite; a program needn't handle non-finite values.
Results may differ from a plain program's by a relative error of at most 0.0001.
Values sent between devices are 32-bit elements; how exact they have to be, the bound alone decides.
No kernel may reach another device: no remote copies, remote signals or barrier semaphores. Data moves between devices by JAX's collectives and lax.ppermute only.
A program may use at most 128 MiB of HBM per device.

v0:
```python
import jax
import jax.numpy as jnp
from jax import lax
from jax.experimental import pallas as pl
from jax.experimental.pallas import tpu as pltpu
from jax.sharding import PartitionSpec as P

LAYERS = 4
REACH = 512
BANDS = 8
ROWS = 2048
PAIRS = 1024
HALO = 520
STEP = 32
FRONT = 8
GFRONT = 112
INNER = 1024
EDGE = 800


def turn_table(cos_sin, table, tile_of, tiles):
    for tile in range(tiles):
        angle = tile_of(tile)
        both = jnp.concatenate([jnp.cos(angle), jnp.sin(angle)], 0)
        tall = jnp.transpose(both)
        for lane in range(2 * LAYERS):
            cos_sin[table, lane, pl.ds(128 * tile, 128), :] = jnp.broadcast_to(tall[:, lane : lane + 1], (128, 128))


def forward(raw, states, cos_sin, table, shift, lead, pairs):
    for layer in range(LAYERS):
        odd = layer % 2

        def block(i, carry, layer=layer, odd=odd):
            at = pl.multiple_of(i * STEP, STEP)
            angle_at = at + shift + lead if odd else at + shift
            cosine = cos_sin[table, layer, pl.ds(angle_at, STEP), :]
            sine = cos_sin[table, LAYERS + layer, pl.ds(angle_at, STEP), :]
            for half in range(2):
                if layer == 0:
                    first = raw[half, pl.ds(2 * at + lead, STEP, stride=2), :]
                    second = raw[half, pl.ds(2 * at + lead + 1, STEP, stride=2), :]
                elif odd:
                    first = states[layer - 1, 1, half, pl.ds(at + FRONT, STEP), :]
                    second = states[layer - 1, 0, half, pl.ds(at + FRONT + 1, STEP), :]
                else:
                    first = states[layer - 1, 0, half, pl.ds(at + FRONT - 1, STEP), :]
                    second = states[layer - 1, 1, half, pl.ds(at + FRONT, STEP), :]
                new_first = cosine * first - sine * second
                new_second = sine * first + cosine * second
                states[layer, odd, half, pl.ds(at + FRONT, STEP), :] = new_first
                states[layer, 1 - odd, half, pl.ds(at + FRONT, STEP), :] = new_second
            return carry

        lax.fori_loop(0, pairs // STEP, block, 0)


def band(states, adjoints, offsets, weights, start, pairs):
    where = []
    for parity in range(2):
        for k in range(BANDS):
            for sign in (1, -1):
                row = parity + sign * offsets[k]
                side = lax.bitwise_and(row, 1)
                where.append((side, lax.shift_right_arithmetic(row, 1) - 1 + side + FRONT + start))

    def block(i, carry):
        at = pl.multiple_of(i * STEP, STEP)
        for parity in range(2):
            for half in range(2):
                total = jnp.zeros((STEP, 128), jnp.float32)
                for k in range(BANDS):
                    side, shift = where[(parity * BANDS + k) * 2]
                    upper = states[LAYERS - 1, side, half, pl.ds(at + shift, STEP), :]
                    side, shift = where[(parity * BANDS + k) * 2 + 1]
                    lower = states[LAYERS - 1, side, half, pl.ds(at + shift, STEP), :]
                    total = total + weights[k] * (upper + lower)
                adjoints[LAYERS - 1, parity, half, pl.ds(at + FRONT, STEP), :] = total
        return carry

    lax.fori_loop(0, pairs // STEP, block, 0)


def backward(states, adjoints, products, cos_sin, table, shift, lead, start, pairs):
    for layer in reversed(range(LAYERS)):
        odd = layer % 2

        def block(i, carry, layer=layer, odd=odd):
            at = pl.multiple_of(i * STEP, STEP)
            angle_at = at + (start + shift) + lead if odd else at + (start + shift)
            cosine = cos_sin[table, layer, pl.ds(angle_at, STEP), :]
            sine = cos_sin[table, LAYERS + layer, pl.ds(angle_at, STEP), :]
            product = None
            for half in range(2):
                if odd:
                    first = adjoints[layer, 1, half, pl.ds(at + FRONT, STEP), :]
                    second = adjoints[layer, 0, half, pl.ds(at + FRONT + 1, STEP), :]
                else:
                    first = adjoints[layer, 0, half, pl.ds(at + FRONT - 1, STEP), :]
                    second = adjoints[layer, 1, half, pl.ds(at + FRONT, STEP), :]
                state_first = states[layer, odd, half, pl.ds(at + start + FRONT, STEP), :]
                state_second = states[layer, 1 - odd, half, pl.ds(at + start + FRONT, STEP), :]
                part = second * state_first - first * state_second
                product = part if product is None else product + part
                if layer:
                    adjoints[layer - 1, odd, half, pl.ds(at + FRONT, STEP), :] = cosine * first + sine * second
                    adjoints[layer - 1, 1 - odd, half, pl.ds(at + FRONT, STEP), :] = cosine * second - sine * first
            products[layer, pl.ds(at + GFRONT, STEP), :] = product
            return carry

        lax.fori_loop(0, pairs // STEP, block, 0)


def summed(products, lead, at):
    rows = []
    for layer in range(LAYERS):
        block = products[layer, pl.ds(at + GFRONT - lead if layer % 2 else at + GFRONT, 128), :]
        rows.append(jnp.sum(jnp.transpose(block), axis=0, keepdims=True))
    return jnp.concatenate(rows, 0)


def inner_kernel(pairing, offsets, weights, slab, angles, evolved, gradient, raw, states, adjoints, products, cos_sin, out, sems):
    loads = []
    for half in range(2):
        loads.append(pltpu.make_async_copy(slab.at[:, pl.ds(128 * half, 128)], raw.at[half, pl.ds(0, ROWS), :], sems.at[half]))
        loads[-1].start()
    lead = pairing[0]
    turn_table(cos_sin, 0, lambda tile: angles[:, 128 * tile : 128 * (tile + 1)], 8)
    for load in loads:
        load.wait()
    forward(raw, states, cos_sin, 0, 0, lead, INNER)

    def weave(i, carry):
        at = pl.multiple_of(i * STEP, STEP)
        for half in range(2):
            out[half, pl.ds(2 * at + lead + FRONT, STEP, stride=2), :] = states[3, 0, half, pl.ds(at + FRONT - 1, STEP), :]
            out[half, pl.ds(2 * at + lead + FRONT + 1, STEP, stride=2), :] = states[3, 1, half, pl.ds(at + FRONT, STEP), :]
        return carry

    lax.fori_loop(0, INNER // STEP, weave, 0)
    stores = []
    for half in range(2):
        stores.append(
            pltpu.make_async_copy(out.at[half, pl.ds(FRONT, ROWS), :], evolved.at[:, pl.ds(128 * half, 128)], sems.at[2 + half])
        )
        stores[-1].start()
    band(states, adjoints, offsets, weights, 256, 512)
    backward(states, adjoints, products, cos_sin, 0, 0, lead, 256, 512)
    for tile in range(4):
        gradient[:, 128 * tile : 128 * (tile + 1)] = summed(products, lead, 128 * tile)
    for store in stores:
        store.wait()


def edge_kernel(
    pairing, offsets, weights, slab, angles, before, after, before_angles, after_angles, inner, evolved_in,
    evolved, gradient, raw, states, adjoints, products, cos_sin, out, sems,
):
    loads = []
    for side in range(2):
        for half in range(2):
            lanes = pl.ds(128 * half, 128)
            if side == 0:
                pieces = [(before, 0, 8, HALO), (slab, 0, 8 + HALO, 2 * EDGE - HALO - 8)]
            else:
                own = 2 * EDGE - HALO - 8
                pieces = [(slab, ROWS - own, 0, own), (after, 0, own, HALO)]
            for source, source_at, at, rows in pieces:
                load = pltpu.make_async_copy(
                    source.at[pl.ds(source_at, rows), lanes],
                    raw.at[side, half, pl.ds(at, rows), :],
                    sems.at[len(loads)],
                )
                load.start()
                loads.append(load)
    lead = pairing[0]

    def left_angles(tile):
        if tile < 3:
            t = tile + 1
            return before_angles[4 * (t // 2) : 4 * (t // 2) + 4, 128 * (t % 2) : 128 * (t % 2) + 128]
        return angles[:, 128 * (tile - 3) : 128 * (tile - 2)]

    def right_angles(tile):
        if tile < 5:
            return angles[:, 128 * (tile + 3) : 128 * (tile + 4)]
        t = tile - 5
        return after_angles[4 * (t // 2) : 4 * (t // 2) + 4, 128 * (t % 2) : 128 * (t % 2) + 128]

    turn_table(cos_sin, 0, left_angles, 8)
    turn_table(cos_sin, 1, right_angles, 8)
    for load in loads:
        load.wait()
    stores = []
    for side in range(2):
        shift = (120, 104)[side]
        forward(raw.at[side], states, cos_sin, side, shift, lead, EDGE)
        at = (256, 528)[side]
        for half in range(2):
            out[side, half, pl.ds(lead, 16, stride=2), :] = states[3, 0, half, pl.ds(at + FRONT - 1, 16), :]
            out[side, half, pl.ds(lead + 1, 16, stride=2), :] = states[3, 1, half, pl.ds(at + FRONT, 16), :]
            store = pltpu.make_async_copy(
                out.at[side, half, pl.ds((16, 8)[side], 8), :],
                evolved.at[pl.ds((0, ROWS - 8)[side], 8), pl.ds(128 * half, 128)],
                sems.at[8 + 2 * side + half],
            )
            store.start()
            stores.append(store)
        band(states, adjoints, offsets, weights, 256, 288)
        backward(states, adjoints, products, cos_sin, side, shift, lead, 256, 288)
        lane = lax.broadcasted_iota(jnp.int32, (LAYERS, 128), 1)
        if side == 0:
            gradient[:, 0:128] = summed(products, lead, 8)
            gradient[:, 128:256] = summed(products, lead, 136)
            gradient[:, 256:384] = jnp.where(lane < 16, summed(products, lead, 264), inner[:, 0:128])
            gradient[:, 384:640] = inner[:, 128:384]
        else:
            gradient[:, 640:768] = jnp.where(lane < 112, inner[:, 384:512], summed(products, lead, -104))
            gradient[:, 768:896] = summed(products, lead, 24)
            gradient[:, 896:1024] = summed(products, lead, 152)
    for store in stores:
        store.wait()


SMALL = pl.BlockSpec(memory_space=pltpu.SMEM)
WHOLE = pl.BlockSpec(memory_space=pltpu.VMEM)
FAR = pl.BlockSpec(memory_space=pl.ANY)


def scratch(sides, rows, pairs, range_pairs, tables, out_shape, sems):
    raw = (2, rows, 128) if sides == 1 else (sides, 2, rows, 128)
    return [
        pltpu.VMEM(raw, jnp.float32),
        pltpu.VMEM((LAYERS, 2, 2, pairs + 2 * FRONT, 128), jnp.float32),
        pltpu.VMEM((LAYERS, 2, 2, range_pairs + 2 * FRONT, 128), jnp.float32),
        pltpu.VMEM((LAYERS, GFRONT + max(range_pairs, 392) + 8, 128), jnp.float32),
        pltpu.VMEM((tables, 2 * LAYERS, 1024 + 8, 128), jnp.float32),
        pltpu.VMEM(out_shape, jnp.float32),
        pltpu.SemaphoreType.DMA((sems,)),
    ]


def inner_call(pairing, offsets, weights, slab, angles):
    return pl.pallas_call(
        inner_kernel,
        out_shape=(jax.ShapeDtypeStruct((ROWS, 256), jnp.float32), jax.ShapeDtypeStruct((LAYERS, 512), jnp.float32)),
        in_specs=[SMALL, SMALL, SMALL, FAR, WHOLE],
        out_specs=(FAR, WHOLE),
        scratch_shapes=scratch(1, ROWS + 8, INNER, 512, 1, (2, ROWS + 2 * FRONT, 128), 4),
        compiler_params=pltpu.CompilerParams(vmem_limit_bytes=40 * 2**20),
        cost_estimate=pl.CostEstimate(flops=40_000_000, bytes_accessed=16 * 2**20, transcendentals=8192),
        name="inner",
    )(pairing, offsets, weights, slab, angles)


def edge_call(pairing, offsets, weights, slab, angles, before, after, before_angles, after_angles, inner, evolved):
    return pl.pallas_call(
        edge_kernel,
        out_shape=(jax.ShapeDtypeStruct((ROWS, 256), jnp.float32), jax.ShapeDtypeStruct((LAYERS, PAIRS), jnp.float32)),
        in_specs=[SMALL, SMALL, SMALL, FAR, WHOLE, FAR, FAR, WHOLE, WHOLE, WHOLE, FAR],
        out_specs=(FAR, WHOLE),
        scratch_shapes=scratch(2, 2 * EDGE + 8, EDGE, 288, 2, (2, 2, 40, 128), 12),
        input_output_aliases={10: 0},
        compiler_params=pltpu.CompilerParams(vmem_limit_bytes=40 * 2**20),
        cost_estimate=pl.CostEstimate(flops=40_000_000, bytes_accessed=16 * 2**20, transcendentals=8192),
        name="edges",
    )(pairing, offsets, weights, slab, angles, before, after, before_angles, after_angles, inner, evolved)


def on_device(slab, angles, pairing, band_offsets, band_weights):
    count = lax.axis_size("blk")
    tail = jnp.concatenate([slab[ROWS - HALO :], angles[:, 512:768], angles[:, 768:]], 0)
    before = lax.ppermute(tail, "blk", [(i, (i + 1) % count) for i in range(count)])
    head = jnp.concatenate([slab[:HALO], angles[:, :256], angles[:, 256:512]], 0)
    after = lax.ppermute(head, "blk", [((i + 1) % count, i) for i in range(count)])
    evolved, inner = inner_call(pairing, band_offsets, band_weights, slab, angles)
    evolved, gradient = edge_call(
        pairing, band_offsets, band_weights, slab, angles, before, after, before[HALO:], after[HALO:], inner, evolved
    )
    columns = lax.axis_size("col")
    step = 1
    while step < columns:
        gradient = gradient + lax.ppermute(gradient, "col", [(i, i ^ step) for i in range(columns)])
        step *= 2
    return (evolved, gradient)


def solution(mesh):
    in_specs = (P("blk", "col"), P(None, "blk"), P(), P(), P())
    out_specs = (P("blk", "col"), P(None, "blk"))
    return jax.shard_map(
        on_device, mesh=mesh, in_specs=in_specs, out_specs=out_specs, check_vma=False
    )
```

profile of v0, /device:TPU:1, one launch (start us, length us, event | category | flops | bytes accessed | tf_op | source)
XLA Modules:
  0.0 41.3 jit_solution(14248579760302223514)
XLA Ops:
  0.6 0.7 %fusion.1 = (f32[4,256]{1,0:T(4,128)S(1)}, f32[4,256]{1,0:T(4,128)S(1)}, f32[4,256]{1,0:T(4,128)S(1)}, f32[4,256]{1,0:T(4,128)S(1)}) fusion(f32[4,1024]{1,0:T(4,128)} %angles.3), kind=kLoop, calls=%fused_computation.3 | loop fusion | bytes 32768 | tf_op jit(solution)/shard_map/slice | solution.py:274
  1.4 0.0 copy-start
  1.4 0.0 copy-start.1
  1.4 0.0 copy-start.2
  1.4 0.0 copy-start.3
  1.4 0.0 copy-start.4
  1.4 1.4 %fusion = (f32[520,256]{1,0:T(8,128)S(1)}, f32[520,256]{1,0:T(8,128)S(1)}) fusion(f32[2048,256]{1,0:T(8,128)} %slab.3), kind=kLoop, calls=%fused_computation.2 | loop fusion | bytes 2129920 | tf_op jit(solution)/shard_map/slice | solution.py:274
  2.9 2.1 %collective-permute-start = (f32[528,256]{1,0:T(8,128)S(1)}, f32[528,256]{1,0:T(8,128)S(1)}, u32[]{:S(2)}, u32[]{:S(2)}) collective-permute-start(f32[528,256]{1,0:T(8,128)S(1)} %pad_maximum_fusion), channel_id=1, source_target_pairs={{0,4},{4,8},{8,12},{12,16},{16,20},{20,24},{24,28},{28,32},{32,36}... | collective-permute-start | bytes 1622024 | tf_op jit(solution)/shard_map/ppermute | solution.py:273
  5.0 7.7 %collective-permute-start.1 = (f32[528,256]{1,0:T(8,128)S(1)}, f32[528,256]{1,0:T(8,128)S(1)}, u32[]{:S(2)}, u32[]{:S(2)}) collective-permute-start(f32[528,256]{1,0:T(8,128)S(1)} %pad_maximum_fusion.1), channel_id=1, source_target_pairs={{4,0},{8,4},{12,8},{16,12},{20,16},{24,20},{28,24},{32,28},{36,32}... | collective-permute-start | bytes 1622024 | tf_op jit(solution)/shard_map/ppermute | solution.py:275
  12.7 0.0 copy-done
  12.7 0.0 copy-done.1
  12.7 0.0 copy-done.2
  12.7 0.0 copy-done.3
  12.7 0.0 copy-done.4
  12.7 7.1 %inner.1 = (f32[2048,256]{1,0:T(8,128)}, f32[4,512]{1,0:T(4,128)S(1)}) custom-call(s32[4]{0:T(128)S(1)} %copy-done.2, s32[8]{0:T(128)S(1)} %copy-done.3, f32[8]{0:T(128)S(1)} %copy-done.4, f32[2048,256]{1,0:T(8,128)S(1)} %copy-done, f32[4,1024]{1,0:T(4,128)S(1)} %copy-done.1), custom_call_target="tpu_custom_call" | custom-call | flops 40000000 | bytes 16777216 | tf_op jit(solution)/shard_map/inner/pallas_call | solution.py:244
  19.9 4.7 %collective-permute-done.before = f32[528,256]{1,0:T(8,128)S(1)} collective-permute-done((f32[528,256]{1,0:T(8,128)S(1)}, f32[528,256]{1,0:T(8,128)S(1)}, u32[]{:S(2)}, u32[]{:S(2)}) %collective-permute-start) | collective-permute-done | bytes 540704 | tf_op jit(solution)/shard_map/ppermute | solution.py:273
  24.6 0.0 collective-permute-done.1.after
  24.6 9.9 %edges.1 = (f32[2048,256]{1,0:T(8,128)}, f32[4,1024]{1,0:T(4,128)S(1)}) custom-call(s32[4]{0:T(128)S(1)} %copy-done.2, s32[8]{0:T(128)S(1)} %copy-done.3, f32[8]{0:T(128)S(1)} %copy-done.4, f32[2048,256]{1,0:T(8,128)S(1)} %copy-done, f32[4,1024]{1,0:T(4,128)S(1)} %copy-done.1, ...), custom_call_target="tpu_custom_call", output_to_operand_aliasing={{0}: (10, {})} | custom-call | flops 40000000 | bytes 16777216 | tf_op jit(solution)/shard_map/edges/pallas_call | solution.py:257
  34.4 1.3 %collective-permute-start.2 = (f32[4,1024]{1,0:T(4,128)S(1)}, f32[4,1024]{1,0:T(4,128)S(1)}, u32[]{:S(2)}, u32[]{:S(2)}) collective-permute-start(f32[4,1024]{1,0:T(4,128)S(1)} %get-tuple-element.9), channel_id=1, source_target_pairs={{0,1},{1,0},{2,3},{3,2},{4,5},{5,4},{6,7},{7,6},{8,9},{9,8},{10,11... | collective-permute-start | bytes 49160 | tf_op jit(solution)/shard_map/ppermute | solution.py:283
  35.8 0.8 %collective-permute-done.2 = f32[4,1024]{1,0:T(4,128)S(1)} collective-permute-done((f32[4,1024]{1,0:T(4,128)S(1)}, f32[4,1024]{1,0:T(4,128)S(1)}, u32[]{:S(2)}, u32[]{:S(2)}) %collective-permute-start.2) | collective-permute-done | bytes 16416 | tf_op jit(solution)/shard_map/ppermute | solution.py:283
  36.6 2.6 %collective-permute-start.3 = (f32[4,1024]{1,0:T(4,128)S(1)}, f32[4,1024]{1,0:T(4,128)S(1)}, u32[]{:S(2)}, u32[]{:S(2)}) collective-permute-start(f32[4,1024]{1,0:T(4,128)S(1)} %add.6), channel_id=1, source_target_pairs={{0,2},{1,3},{2,0},{3,1},{4,6},{5,7},{6,4},{7,5},{8,10},{9,11},{10,... | collective-permute-start | bytes 49160 | tf_op jit(solution)/shard_map/ppermute | solution.py:283
  39.2 1.5 %collective-permute-done.3 = f32[4,1024]{1,0:T(4,128)S(1)} collective-permute-done((f32[4,1024]{1,0:T(4,128)S(1)}, f32[4,1024]{1,0:T(4,128)S(1)}, u32[]{:S(2)}, u32[]{:S(2)}) %collective-permute-start.3) | collective-permute-done | bytes 16416 | tf_op jit(solution)/shard_map/ppermute | solution.py:283
  40.7 0.6 %add.7 = f32[4,1024]{1,0:T(4,128)} add(f32[4,1024]{1,0:T(4,128)S(1)} %add.6, f32[4,1024]{1,0:T(4,128)S(1)} %collective-permute-done.3) | non-fusion elementwise | flops 4096 | bytes 49152 | tf_op jit(solution)/shard_map/add | solution.py:283
  (5 shorter events, 0.1 us)
Async XLA Ops:
  1.4 11.3 %copy-start = (f32[2048,256]{1,0:T(8,128)S(1)}, f32[2048,256]{1,0:T(8,128)}, u32[]{:S(2)}) copy-start(f32[2048,256]{1,0:T(8,128)} %slab.3) | copy-start | bytes 6291460
  1.4 11.3 %copy-start.1 = (f32[4,1024]{1,0:T(4,128)S(1)}, f32[4,1024]{1,0:T(4,128)}, u32[]{:S(2)}) copy-start(f32[4,1024]{1,0:T(4,128)} %angles.3) | copy-start | bytes 49156
  1.4 11.3 %copy-start.2 = (s32[4]{0:T(128)S(1)}, s32[4]{0:T(128)}, u32[]{:S(2)}) copy-start(s32[4]{0:T(128)} %pairing.3) | copy-start | bytes 52
  1.4 11.3 %copy-start.3 = (s32[8]{0:T(128)S(1)}, s32[8]{0:T(128)}, u32[]{:S(2)}) copy-start(s32[8]{0:T(128)} %offsets.3) | copy-start | bytes 100
  1.4 11.3 %copy-start.4 = (f32[8]{0:T(128)S(1)}, f32[8]{0:T(128)}, u32[]{:S(2)}) copy-start(f32[8]{0:T(128)} %weights.3) | copy-start | bytes 100
  2.9 21.7 %collective-permute-start = (f32[528,256]{1,0:T(8,128)S(1)}, f32[528,256]{1,0:T(8,128)S(1)}, u32[]{:S(2)}, u32[]{:S(2)}) collective-permute-start(f32[528,256]{1,0:T(8,128)S(1)} %pad_maximum_fusion), channel_id=1, source_target_pairs={{0,4},{4,8},{8,12},{12,16},{16,20},{20,24},{24,28},{28,32},{32,36}... | collective-permute-start | bytes 1622024 | tf_op jit(solution)/shard_map/ppermute | solution.py:273
  5.0 19.5 %collective-permute-start.1 = (f32[528,256]{1,0:T(8,128)S(1)}, f32[528,256]{1,0:T(8,128)S(1)}, u32[]{:S(2)}, u32[]{:S(2)}) collective-permute-start(f32[528,256]{1,0:T(8,128)S(1)} %pad_maximum_fusion.1), channel_id=1, source_target_pairs={{4,0},{8,4},{12,8},{16,12},{20,16},{24,20},{28,24},{32,28},{36,32}... | collective-permute-start | bytes 1622024 | tf_op jit(solution)/shard_map/ppermute | solution.py:275
  34.4 2.2 %collective-permute-start.2 = (f32[4,1024]{1,0:T(4,128)S(1)}, f32[4,1024]{1,0:T(4,128)S(1)}, u32[]{:S(2)}, u32[]{:S(2)}) collective-permute-start(f32[4,1024]{1,0:T(4,128)S(1)} %get-tuple-element.9), channel_id=1, source_target_pairs={{0,1},{1,0},{2,3},{3,2},{4,5},{5,4},{6,7},{7,6},{8,9},{9,8},{10,11... | collective-permute-start | bytes 49160 | tf_op jit(solution)/shard_map/ppermute | solution.py:283
  36.6 4.1 %collective-permute-start.3 = (f32[4,1024]{1,0:T(4,128)S(1)}, f32[4,1024]{1,0:T(4,128)S(1)}, u32[]{:S(2)}, u32[]{:S(2)}) collective-permute-start(f32[4,1024]{1,0:T(4,128)S(1)} %add.6), channel_id=1, source_target_pairs={{0,2},{1,3},{2,0},{3,1},{4,6},{5,7},{6,4},{7,5},{8,10},{9,11},{10,... | collective-permute-start | bytes 49160 | tf_op jit(solution)/shard_map/ppermute | solution.py:283
where the time goes:
time: 41.4 us; the launch traced here: 41.3 us
  Pallas kernels  17 us (41%)
  starting transfers between devices  13.7 us (33%)
  waiting for transfers between devices  7.02 us (17%)
  local copies, waits for them, and re-layouts  2.19 us (5%)
  between operations  0.7 us (2%)
  other arithmetic  0.69 us (2%)
    pallas_call x1, Pallas kernels, edge_call(): pl.pallas_call(edge_kernel, out_shape=(jax.ShapeDtypeStruct((ROWS, 256),...  9.86 us
    ppermute x1, starting transfers between devices, on_device(): lax.ppermute(head, 'blk', [((i + 1) % count, i) for i in range(count)])  7.67 us
    pallas_call x1, Pallas kernels, inner_call(): pl.pallas_call(inner_kernel, out_shape=(jax.ShapeDtypeStruct((ROWS, 256),...  7.13 us
    ppermute x1, waiting for transfers between devices, on_device(): lax.ppermute(tail, 'blk', [(i, (i + 1) % count) for i in range(count)])  4.71 us
    ppermute x2, starting transfers between devices, on_device(): lax.ppermute(gradient, 'col', [(i, i ^ step) for i in range(columns)])  3.94 us
    ppermute x2, waiting for transfers between devices, on_device(): lax.ppermute(gradient, 'col', [(i, i ^ step) for i in range(columns)])  2.31 us
    ppermute x1, starting transfers between devices, on_device(): lax.ppermute(tail, 'blk', [(i, (i + 1) % count) for i in range(count)])  2.12 us
    slice x1, local copies, waits for them, and re-layouts, on_device(): slab[:HALO]  1.42 us
  transfers between devices with their start and end apart: 4, of which 3 were waited for; matrix products, arithmetic and copies ran while one was open for 0% of the time, Pallas kernels for 17%

commit v1 on v0

v1 whole, which is shorter than its diff:
```python
import jax
import jax.numpy as jnp
from jax import lax
from jax.experimental import pallas as pl
from jax.experimental.pallas import tpu as pltpu
from jax.sharding import PartitionSpec as P

LAYERS = 4
REACH = 512
BANDS = 8
ROWS = 2048
PAIRS = 1024
NEAR = 280
FAR_ROWS = 240
THIRD = 176
PAD = 272
LENGTH = PAD + PAIRS + PAD
WINDOW = 160
FAR_WINDOW = 136
FRONT = 8
GFRONT = 8
RANGE = 304


def fill_table(table, at, angle, low=0, high=128):
    both = jnp.concatenate([jnp.cos(angle), jnp.sin(angle)], 0)
    tall = jnp.transpose(both)
    for lane in range(2 * LAYERS):
        table[lane, pl.ds(at, high - low), :] = jnp.broadcast_to(tall[low:high, lane : lane + 1], (high - low, 128))


def forward(raw, states, start, table, table_start, lead, pairs, step):
    for layer in range(LAYERS):
        odd = layer % 2

        def block(i, carry, layer=layer, odd=odd):
            at = pl.multiple_of(i * step, 8)
            angle_at = at + table_start + lead if odd else at + table_start
            cosine = table[layer, pl.ds(angle_at, step), :]
            sine = table[LAYERS + layer, pl.ds(angle_at, step), :]
            for half in range(2):
                if layer == 0:
                    first = raw[half, pl.ds(2 * at + lead, step, stride=2), :]
                    second = raw[half, pl.ds(2 * at + lead + 1, step, stride=2), :]
                elif odd:
                    first = states[layer - 1, 1, half, pl.ds(at + start, step), :]
                    second = states[layer - 1, 0, half, pl.ds(at + start + 1, step), :]
                else:
                    first = states[layer - 1, 0, half, pl.ds(at + start - 1, step), :]
                    second = states[layer - 1, 1, half, pl.ds(at + start, step), :]
                states[layer, odd, half, pl.ds(at + start, step), :] = cosine * first - sine * second
                states[layer, 1 - odd, half, pl.ds(at + start, step), :] = sine * first + cosine * second
            return carry

        lax.fori_loop(0, pairs // step, block, 0)


def band(source, source_start, total, total_start, offsets, weights, pairs, step, signs, add):
    where = []
    for parity in range(2):
        for k in range(BANDS):
            for sign in signs:
                row = parity + sign * offsets[k]
                side = lax.bitwise_and(row, 1)
                where.append((side, lax.shift_right_arithmetic(row, 1) - 1 + side + source_start))

    def block(i, carry):
        at = pl.multiple_of(i * step, 8)
        for parity in range(2):
            for half in range(2):
                place = (parity, half, pl.ds(at + total_start, step), slice(None))
                value = total[place] if add else None
                for k in range(BANDS):
                    term = None
                    for n in range(len(signs)):
                        side, shift = where[(parity * BANDS + k) * len(signs) + n]
                        row = source[side, half, pl.ds(at + shift, step), :]
                        term = row if term is None else term + row
                    term = weights[k] * term
                    value = term if value is None else value + term
                total[place] = value
        return carry

    lax.fori_loop(0, pairs // step, block, 0)


def backward(states, start, adjoint, adjoint_start, turned, products, table, table_start, lead, pairs, step):
    for layer in reversed(range(LAYERS)):
        odd = layer % 2

        def block(i, carry, layer=layer, odd=odd):
            at = pl.multiple_of(i * step, 8)
            angle_at = at + table_start + lead if odd else at + table_start
            cosine = table[layer, pl.ds(angle_at, step), :]
            sine = table[LAYERS + layer, pl.ds(angle_at, step), :]
            product = None
            for half in range(2):
                source = adjoint if layer == LAYERS - 1 else turned.at[layer]
                begin = adjoint_start if layer == LAYERS - 1 else FRONT
                if odd:
                    first = source[1, half, pl.ds(at + begin, step), :]
                    second = source[0, half, pl.ds(at + begin + 1, step), :]
                else:
                    first = source[0, half, pl.ds(at + begin - 1, step), :]
                    second = source[1, half, pl.ds(at + begin, step), :]
                state_first = states[layer, odd, half, pl.ds(at + start, step), :]
                state_second = states[layer, 1 - odd, half, pl.ds(at + start, step), :]
                part = second * state_first - first * state_second
                product = part if product is None else product + part
                if layer:
                    turned[layer - 1, odd, half, pl.ds(at + FRONT, step), :] = cosine * first + sine * second
                    turned[layer - 1, 1 - odd, half, pl.ds(at + FRONT, step), :] = cosine * second - sine * first
            products[layer, pl.ds(at + GFRONT, step), :] = product
            return carry

        lax.fori_loop(0, pairs // step, block, 0)


def summed(products, lead, at):
    rows = []
    for layer in range(LAYERS):
        block = products[layer, pl.ds(at + GFRONT - lead if layer % 2 else at + GFRONT, 128), :]
        rows.append(jnp.sum(jnp.transpose(block), axis=0, keepdims=True))
    return jnp.concatenate(rows, 0)


def inner_kernel(
    pairing, offsets, weights, slab, angles,
    evolved, states, adjoint, table, gradient, raw, turned, products, out, sems,
):
    loads = []
    for half in range(2):
        loads.append(pltpu.make_async_copy(slab.at[:, pl.ds(128 * half, 128)], raw.at[half, pl.ds(0, ROWS), :], sems.at[half]))
        loads[-1].start()
    lead = pairing[0]
    for tile in range(8):
        fill_table(table, FRONT + 128 * tile, angles[:, 128 * tile : 128 * (tile + 1)])
    for load in loads:
        load.wait()
    forward(raw, states, PAD, table, FRONT, lead, PAIRS, 128)

    def weave(i, carry):
        at = pl.multiple_of(i * 128, 128)
        for half in range(2):
            out[half, pl.ds(2 * at + lead + FRONT, 128, stride=2), :] = states[3, 0, half, pl.ds(at + PAD - 1, 128), :]
            out[half, pl.ds(2 * at + lead + FRONT + 1, 128, stride=2), :] = states[3, 1, half, pl.ds(at + PAD, 128), :]
        return carry

    lax.fori_loop(0, PAIRS // 128, weave, 0)
    stores = []
    for half in range(2):
        stores.append(
            pltpu.make_async_copy(out.at[half, pl.ds(FRONT, ROWS), :], evolved.at[:, pl.ds(128 * half, 128)], sems.at[2 + half])
        )
        stores[-1].start()
    blank = jnp.zeros((PAD + 8, 128), jnp.float32)
    last = states.at[LAYERS - 1]
    for parity in range(2):
        for half in range(2):
            last[parity, half, pl.ds(0, PAD + 8), :] = blank
            last[parity, half, pl.ds(PAD + PAIRS - 8, PAD + 8), :] = blank
    band(last, PAD - 8, adjoint, FRONT, offsets, weights, PAIRS + 16, 104, (1, -1), False)
    backward(states, PAD + 256, adjoint, FRONT + 8 + 256, turned, products, table, FRONT + 256, lead, 512, 128)
    for tile in range(4):
        gradient[:, 128 * tile : 128 * (tile + 1)] = summed(products, lead, 128 * tile)
    for store in stores:
        store.wait()


def halo_angles(halo, at, tile):
    return halo[at + 4 * (tile // 2) : at + 4 * (tile // 2) + 4, 128 * (tile % 2) : 128 * (tile % 2) + 128]


def started(pieces, raw, sems):
    loads = []
    for half in range(2):
        for piece, piece_at, at, rows in pieces:
            load = pltpu.make_async_copy(
                piece.at[pl.ds(piece_at, rows), pl.ds(128 * half, 128)], raw.at[half, pl.ds(at, rows), :], sems.at[len(loads)]
            )
            load.start()
            loads.append(load)
    return loads


def near_tables(side, halo, at, table, halo_table):
    if side == 0:
        fill_table(halo_table, 0, halo_angles(halo, at, 1), 120, 128)
        fill_table(halo_table, 8, halo_angles(halo, at, 2))
        fill_table(halo_table, 136, halo_angles(halo, at, 3))
    else:
        fill_table(halo_table, 16, halo_angles(halo, at, 0))
        fill_table(halo_table, 144, halo_angles(halo, at, 1))
        fill_table(halo_table, 272, halo_angles(halo, at, 2), 0, 16)
    for lane in range(2 * LAYERS):
        if side == 0:
            halo_table[lane, pl.ds(264, 24), :] = table[lane, pl.ds(FRONT, 24), :]
            table[lane, pl.ds(0, FRONT), :] = halo_table[lane, pl.ds(256, 8), :]
        else:
            halo_table[lane, pl.ds(0, 16), :] = table[lane, pl.ds(FRONT + PAIRS - 16, 16), :]
            table[lane, pl.ds(FRONT + PAIRS, 16), :] = halo_table[lane, pl.ds(16, 16), :]


def near_side(
    side, lead, offsets, weights, raw, window, source, states, adjoint, table, halo_table, turned, products, out, evolved, sems
):
    forward(raw, window, FRONT, halo_table, (120, 0)[side], lead, WINDOW, 80)
    stores = []
    blank = jnp.zeros((272, 128), jnp.float32)
    at = FRONT + (144, 8)[side]
    for half in range(2):
        out[half, pl.ds(lead, 16, stride=2), :] = window[3, 0, half, pl.ds(at - 9, 16), :]
        out[half, pl.ds(lead + 1, 16, stride=2), :] = window[3, 1, half, pl.ds(at - 8, 16), :]
        store = pltpu.make_async_copy(
            out.at[half, pl.ds(16, 16), :],
            evolved.at[pl.ds((0, ROWS - 16)[side], 16), pl.ds(128 * half, 128)],
            sems.at[half],
        )
        store.start()
        stores.append(store)
        for parity in range(2):
            for layer in range(LAYERS):
                states[layer, parity, half, pl.ds(PAD + (-8, PAIRS - 8)[side], 16), :] = window[
                    layer, parity, half, pl.ds(at + (-8, 0)[side], 16), :
                ]
            if side == 0:
                source[parity, half, pl.ds(0, 136), :] = blank[:136]
                source[parity, half, pl.ds(136, 144), :] = window[3, parity, half, pl.ds(FRONT + 8, 144), :]
                source[parity, half, pl.ds(280, 272), :] = blank
            else:
                source[parity, half, pl.ds(0, 272), :] = blank
                source[parity, half, pl.ds(272, 144), :] = window[3, parity, half, pl.ds(FRONT + 8, 144), :]
                source[parity, half, pl.ds(416, 128), :] = blank[:128]
    band(source, (264, 0)[side], adjoint, FRONT + (0, 752)[side], offsets, weights, 288, 96, ((-1,), (1,))[side], True)
    band(source, (264, 272)[side], adjoint, FRONT + (0, PAIRS)[side], offsets, weights, 16, 16, ((1,), (-1,))[side], True)
    begin = (120, 744)[side]
    backward(states, PAD + begin, adjoint, FRONT + 8 + begin, turned, products, table, FRONT + begin, lead, 160, 80)
    return stores


def far_side(side, lead, offsets, weights, raw, window, source, states, adjoint, table, halo_table, turned, products):
    forward(raw, window, FRONT, halo_table, (0, 144)[side], lead, FAR_WINDOW, 136)
    blank = jnp.zeros((272, 128), jnp.float32)
    for parity in range(2):
        for half in range(2):
            value = window[3, parity, half, pl.ds(FRONT + (0, 8)[side], 128), :]
            if side == 0:
                source[parity, half, pl.ds(8, 128), :] = value
                source[parity, half, pl.ds(136, 272), :] = blank
            else:
                source[parity, half, pl.ds(0, 272), :] = blank
                source[parity, half, pl.ds(272, 128), :] = value
    band(source, (264, 0)[side], adjoint, FRONT + (0, 896)[side], offsets, weights, 144, 144, ((-1,), (1,))[side], True)
    begin = (-8, 888)[side]
    backward(states, PAD + begin, adjoint, FRONT + 8 + begin, turned, products, table, FRONT + begin, lead, 144, 144)


def left_kernel(
    pairing, offsets, weights, slab, before, evolved_in, states_in, adjoint_in, table_in, inner,
    evolved, states, adjoint, table, halo_table, gradient, raw, window, source, turned, products, out, sems,
):
    loads = started(((before, 0, 8, NEAR), (slab, 0, 8 + NEAR, 40)), raw, sems)
    lead = pairing[0]
    near_tables(0, before, NEAR, table, halo_table)
    for load in loads:
        load.wait()
    stores = near_side(
        0, lead, offsets, weights, raw, window, source, states, adjoint, table, halo_table, turned, products, out, evolved,
        sems.at[pl.ds(4, 2)],
    )
    lane = lax.broadcasted_iota(jnp.int32, (LAYERS, 128), 1)
    gradient[:, 0:128] = summed(products, lead, 8)
    gradient[:, 128:256] = jnp.where(lane < 16, summed(products, lead, 136), inner[:, 0:128])
    gradient[:, 256:512] = inner[:, 128:384]
    for store in stores:
        store.wait()


def rest_kernel(
    pairing, offsets, weights, slab, before, before_far, after, after_next, after_last, left_table, inner, left,
    evolved_in, states_in, adjoint_in, table_in,
    evolved, states, adjoint, table, gradient, raw, raw_left, raw_right, window, source, turned, products, right_table, out, sems,
):
    loads = started(
        ((slab, ROWS - 32, 0, 32), (after, 0, 32, THIRD), (after_next, 0, 32 + THIRD, NEAR - THIRD)), raw, sems
    )
    loads_left = started(((before_far, 0, 8, FAR_ROWS), (before, 0, 8 + FAR_ROWS, 32)), raw_left, sems.at[pl.ds(6, 4)])
    loads_right = started(
        ((after_next, NEAR - 24 - THIRD, 0, 2 * THIRD + 24 - NEAR), (after_last, 0, 2 * THIRD + 24 - NEAR, THIRD - 8)),
        raw_right,
        sems.at[pl.ds(10, 4)],
    )
    lead = pairing[0]
    near_tables(1, after_last, THIRD - 8, table, right_table)
    for load in loads:
        load.wait()
    common = (window, source, states, adjoint, table)
    stores = near_side(
        1, lead, offsets, weights, raw, *common, right_table, turned, products, out, evolved, sems.at[pl.ds(14, 2)]
    )
    lane = lax.broadcasted_iota(jnp.int32, (LAYERS, 128), 1)
    gradient[:, 128:640] = left[...]
    gradient[:, 640:768] = jnp.where(lane < 112, inner[:, 384:512], pltpu.roll(summed(products, lead, 8), 112, 1))
    gradient[:, 768:896] = summed(products, lead, 24)
    for load in loads_left:
        load.wait()
    far_side(0, lead, offsets, weights, raw_left, *common, left_table, turned, products)
    gradient[:, 0:128] = summed(products, lead, 8)
    for load in loads_right:
        load.wait()
    far_side(1, lead, offsets, weights, raw_right, *common, right_table, turned, products)
    gradient[:, 896:1024] = summed(products, lead, 8)
    for store in stores:
        store.wait()


SMALL = pl.BlockSpec(memory_space=pltpu.SMEM)
WHOLE = pl.BlockSpec(memory_space=pltpu.VMEM)
FAR = pl.BlockSpec(memory_space=pl.ANY)

EVOLVED = jax.ShapeDtypeStruct((ROWS, 256), jnp.float32)
STATES = jax.ShapeDtypeStruct((LAYERS, 2, 2, LENGTH, 128), jnp.float32)
ADJOINT = jax.ShapeDtypeStruct((2, 2, PAIRS + 32, 128), jnp.float32)
TABLE = jax.ShapeDtypeStruct((2 * LAYERS, PAIRS + 32, 128), jnp.float32)
HALO_TABLE = jax.ShapeDtypeStruct((2 * LAYERS, 296, 128), jnp.float32)


def limits(flops, traffic, grant=16):
    return dict(
        compiler_params=pltpu.CompilerParams(vmem_limit_bytes=grant * 2**20),
        cost_estimate=pl.CostEstimate(flops=flops, bytes_accessed=traffic, transcendentals=8192),
    )


def room(*shape):
    return pltpu.VMEM(shape, jnp.float32)


def pack_call(slab, angles, pieces, angle_at, *earlier):
    def kernel(slab, angles, *refs):
        packed, tiles, sems = refs[len(earlier) : len(earlier) + len(pieces)], refs[-2], refs[-1]
        copies = [pltpu.make_async_copy(angles, tiles, sems.at[len(pieces)])]
        for n, (first, rows, _) in enumerate(pieces):
            copies.append(
                pltpu.make_async_copy(slab.at[pl.ds(first, rows), :], packed[n].at[pl.ds(0, rows), :], sems.at[n])
            )
        for copy in copies:
            copy.start()
        copies[0].wait()
        for n, (_, rows, follow) in enumerate(pieces):
            for row in range(2 * follow):
                lanes = slice(angle_at + 256 * row, angle_at + 256 * (row + 1))
                packed[n][rows + 4 * row : rows + 4 * (row + 1), :] = tiles[:, lanes]
        for copy in copies[1:]:
            copy.wait()

    slab = pltpu.with_memory_space_constraint(slab, pltpu.HBM)
    angles = pltpu.with_memory_space_constraint(angles, pltpu.HBM)
    return pl.pallas_call(
        kernel,
        out_shape=[jax.ShapeDtypeStruct((rows + 8 * follow, 256), jnp.float32) for _, rows, follow in pieces],
        in_specs=[pl.BlockSpec(memory_space=pltpu.HBM)] * 2 + [FAR] * len(earlier),
        out_specs=[WHOLE] * len(pieces),
        scratch_shapes=[room(LAYERS, PAIRS), pltpu.SemaphoreType.DMA((len(pieces) + 1,))],
        name="pack",
        **limits(1000, 2**20),
    )(slab, angles, *earlier)


def inner_call(pairing, offsets, weights, slab, angles):
    return pl.pallas_call(
        inner_kernel,
        out_shape=(EVOLVED, STATES, ADJOINT, TABLE, jax.ShapeDtypeStruct((LAYERS, 512), jnp.float32)),
        in_specs=[SMALL, SMALL, SMALL, FAR, WHOLE],
        out_specs=(FAR, WHOLE, WHOLE, WHOLE, WHOLE),
        scratch_shapes=[
            room(2, ROWS + 8, 128),
            room(LAYERS - 1, 2, 2, 512 + 16, 128),
            room(LAYERS, 512 + 16, 128),
            room(2, ROWS + 16, 128),
            pltpu.SemaphoreType.DMA((4,)),
        ],
        name="inner",
        **limits(60_000_000, 24 * 2**20),
    )(pairing, offsets, weights, slab, angles)


def left_call(pairing, offsets, weights, slab, before, evolved, states, adjoint, table, inner):
    return pl.pallas_call(
        left_kernel,
        out_shape=(EVOLVED, STATES, ADJOINT, TABLE, HALO_TABLE, jax.ShapeDtypeStruct((LAYERS, 512), jnp.float32)),
        in_specs=[SMALL, SMALL, SMALL, FAR, WHOLE, FAR, WHOLE, WHOLE, WHOLE, WHOLE],
        out_specs=(FAR, WHOLE, WHOLE, WHOLE, WHOLE, WHOLE),
        scratch_shapes=[
            room(2, 328, 128),
            room(LAYERS, 2, 2, WINDOW + 16, 128),
            room(2, 2, 552, 128),
            room(LAYERS - 1, 2, 2, 160 + 16, 128),
            room(LAYERS, 280, 128),
            room(2, 40, 128),
            pltpu.SemaphoreType.DMA((6,)),
        ],
        input_output_aliases={5: 0, 6: 1, 7: 2, 8: 3},
        name="left",
        **limits(15_000_000, 8 * 2**20),
    )(pairing, offsets, weights, slab, before, evolved, states, adjoint, table, inner)


def rest_call(*operands):
    return pl.pallas_call(
        rest_kernel,
        out_shape=(EVOLVED, STATES, ADJOINT, TABLE, jax.ShapeDtypeStruct((LAYERS, PAIRS), jnp.float32)),
        in_specs=[SMALL, SMALL, SMALL, FAR] + [WHOLE] * 8 + [FAR, WHOLE, WHOLE, WHOLE],
        out_specs=(FAR, WHOLE, WHOLE, WHOLE, WHOLE),
        scratch_shapes=[
            room(2, 328, 128),
            room(2, 280, 128),
            room(2, 280, 128),
            room(LAYERS, 2, 2, WINDOW + 16, 128),
            room(2, 2, 552, 128),
            room(LAYERS - 1, 2, 2, 160 + 16, 128),
            room(LAYERS, 280, 128),
            room(2 * LAYERS, 296, 128),
            room(2, 40, 128),
            pltpu.SemaphoreType.DMA((16,)),
        ],
        input_output_aliases={12: 0, 13: 1, 14: 2, 15: 3},
        name="rest",
        **limits(30_000_000, 8 * 2**20),
    )(*operands)


def on_device(slab, angles, pairing, band_offsets, band_weights):
    count = lax.axis_size("blk")
    onward = [(i, (i + 1) % count) for i in range(count)]
    back = [((i + 1) % count, i) for i in range(count)]
    tail, far_tail = pack_call(
        slab, angles, ((ROWS - NEAR, NEAR, 1), (ROWS - NEAR - FAR_ROWS, FAR_ROWS, 0)), 512
    )
    before = lax.ppermute(tail, "blk", onward)
    before_far = lax.ppermute(far_tail, "blk", onward)
    heads = pack_call(slab, angles, ((0, THIRD, 0), (THIRD, THIRD, 0), (2 * THIRD, THIRD - 8, 1)), 0, far_tail)
    after = [lax.ppermute(head, "blk", back) for head in heads]
    scalars = (pairing, band_offsets, band_weights)
    evolved, states, adjoint, table, gradient = inner_call(*scalars, slab, angles)
    evolved, states, adjoint, table, left_table, left = left_call(
        *scalars, slab, before, evolved, states, adjoint, table, gradient
    )
    evolved, _, _, _, gradient = rest_call(
        *scalars, slab, before, before_far, *after, left_table, gradient, left, evolved, states, adjoint, table
    )
    columns = lax.axis_size("col")
    step = 1
    while step < columns:
        gradient = gradient + lax.ppermute(gradient, "col", [(i, i ^ step) for i in range(columns)])
        step *= 2
    return (evolved, gradient)


def solution(mesh):
    in_specs = (P("blk", "col"), P(None, "blk"), P(), P(), P())
    out_specs = (P("blk", "col"), P(None, "blk"))
    return jax.shard_map(
        on_device, mesh=mesh, in_specs=in_specs, out_specs=out_specs, check_vma=False
    )
```

time: 41.4 us -> 38.8 us (0.937)
  waiting for transfers between devices: 7.02 us -> 2.33 us
  starting transfers between devices: 13.7 us -> 17.5 us
  local copies, waits for them, and re-layouts: 2.19 us -> 0.03 us
    ppermute x2 -> x5, waiting for transfers between devices: 4.71 us -> 0.01 us  [the longest x3 0.01 us: on_device(): after = [lax.ppermute(head, 'blk', back) for head in heads]]
    ppermute x2 -> x5, starting transfers between devices: 9.78 us -> 12.7 us  [the longest x3 9.37 us: on_device(): after = [lax.ppermute(head, 'blk', back) for head in heads]]
    slice x4 -> x0, local copies, waits for them, and re-layouts: 2.16 us -> none  [the longest x1 1.42 us: on_device(): slab[:HALO]]
    ppermute x2, starting transfers between devices: 3.94 us -> 4.78 us  [on_device(): lax.ppermute(gradient, 'col', [(i, i ^ step) for i in range(columns)])]
    pallas_call x2 -> x5, Pallas kernels: 17 us -> 17.3 us  [the longest x1 8.01 us: inner_call(): pl.pallas_call(inner_kernel, out_shape=(EVOLVED, STATES, ADJOINT, TABLE,...]
  transfers between devices with their start and end apart: 4 -> 7, of which waited for: 3 -> 2; matrix products, arithmetic and copies ran while one was open for 0% -> 0% of each run, Pallas kernels for 17% -> 30%
where the time goes in v1:
time: 38.8 us; the launch traced here: 38.6 us
  starting transfers between devices  17.5 us (45%)
  Pallas kernels  17.3 us (45%)
  waiting for transfers between devices  2.33 us (6%)
  between operations  0.77 us (2%)
  other arithmetic  0.62 us (2%)
    ppermute x3, starting transfers between devices, on_device(): after = [lax.ppermute(head, 'blk', back) for head in heads]  9.37 us
    pallas_call x1, Pallas kernels, inner_call(): pl.pallas_call(inner_kernel, out_shape=(EVOLVED, STATES, ADJOINT, TABLE,...  8.01 us
    ppermute x2, starting transfers between devices, on_device(): lax.ppermute(gradient, 'col', [(i, i ^ step) for i in range(columns)])  4.78 us
    pallas_call x1, Pallas kernels, rest_call(): pl.pallas_call(rest_kernel, out_shape=(EVOLVED, STATES, ADJOINT, TABLE, j...  4.52 us
    pallas_call x1, Pallas kernels, left_call(): pl.pallas_call(left_kernel, out_shape=(EVOLVED, STATES, ADJOINT, TABLE, H...  2.46 us
    pallas_call x2, Pallas kernels, pack_call(): pl.pallas_call(kernel, out_shape=[jax.ShapeDtypeStruct((rows + 8 * follow...  2.35 us
    ppermute x2, waiting for transfers between devices, on_device(): lax.ppermute(gradient, 'col', [(i, i ^ step) for i in range(columns)])  2.31 us
    ppermute x1, starting transfers between devices, on_device(): before = lax.ppermute(tail, 'blk', onward)  2.12 us
  transfers between devices with their start and end apart: 7, of which 2 were waited for; matrix products, arithmetic and copies ran while one was open for 0% of the time, Pallas kernels for 30%

profile of v1, /device:TPU:1, one launch (start us, length us, event | category | flops | bytes accessed | tf_op | source)
XLA Modules:
  0.0 38.6 jit_solution(1660645456982617271)
XLA Ops:
  0.6 0.0 copy-start
  0.6 0.0 copy-start.1
  0.7 0.0 copy-start.4
  0.7 0.0 copy-start.3
  0.7 0.0 copy-start.2
  0.7 1.2 %pack.2 = (f32[288,256]{1,0:T(8,128)S(1)}, f32[240,256]{1,0:T(8,128)S(1)}) custom-call(f32[2048,256]{1,0:T(8,128)} %slab.9, f32[4,1024]{1,0:T(4,128)} %angles.5), custom_call_target="tpu_custom_call" | custom-call | flops 1000 | bytes 1048576 | tf_op jit(solution)/shard_map/pack/pallas_call | solution.py:359
  1.9 2.1 %collective-permute-start = (f32[288,256]{1,0:T(8,128)S(1)}, f32[288,256]{1,0:T(8,128)S(1)}, u32[]{:S(2)}, u32[]{:S(2)}) collective-permute-start(f32[288,256]{1,0:T(8,128)S(1)} %get-tuple-element.20), channel_id=1, source_target_pairs={{0,4},{4,8},{8,12},{12,16},{16,20},{20,24},{24,28},{28,32},{32,36}... | collective-permute-start | bytes 884744 | tf_op jit(solution)/shard_map/ppermute | solution.py:440
  4.0 1.2 %collective-permute-start.1 = (f32[240,256]{1,0:T(8,128)S(1)}, f32[240,256]{1,0:T(8,128)S(1)}, u32[]{:S(2)}, u32[]{:S(2)}) collective-permute-start(f32[240,256]{1,0:T(8,128)S(1)} %get-tuple-element.21.refs_0_), channel_id=1, source_target_pairs={{0,4},{4,8},{8,12},{12,16},{16,20},{20,24},{24,28},{28,32},{32,36}... | collective-permute-start | bytes 737288 | tf_op jit(solution)/shard_map/ppermute | solution.py:441
  5.2 1.1 %pack.3 = (f32[176,256]{1,0:T(8,128)S(1)}, f32[176,256]{1,0:T(8,128)S(1)}, f32[176,256]{1,0:T(8,128)S(1)}) custom-call(f32[2048,256]{1,0:T(8,128)} %slab.9, f32[4,1024]{1,0:T(4,128)} %angles.5, f32[240,256]{1,0:T(8,128)S(1)} %get-tuple-element.21.refs_0_), custom_call_target="tpu_custom_call" | custom-call | flops 1000 | bytes 1048576 | tf_op jit(solution)/shard_map/pack/pallas_call | solution.py:359
  6.4 6.5 %collective-permute-start.2 = (f32[176,256]{1,0:T(8,128)S(1)}, f32[176,256]{1,0:T(8,128)S(1)}, u32[]{:S(2)}, u32[]{:S(2)}) collective-permute-start(f32[176,256]{1,0:T(8,128)S(1)} %get-tuple-element.22), channel_id=1, source_target_pairs={{4,0},{8,4},{12,8},{16,12},{20,16},{24,20},{28,24},{32,28},{36,32}... | collective-permute-start | bytes 540680 | tf_op jit(solution)/shard_map/ppermute | solution.py:443
  12.9 1.4 %collective-permute-start.3 = (f32[176,256]{1,0:T(8,128)S(1)}, f32[176,256]{1,0:T(8,128)S(1)}, u32[]{:S(2)}, u32[]{:S(2)}) collective-permute-start(f32[176,256]{1,0:T(8,128)S(1)} %get-tuple-element.23), channel_id=1, source_target_pairs={{4,0},{8,4},{12,8},{16,12},{20,16},{24,20},{28,24},{32,28},{36,32}... | collective-permute-start | bytes 540680 | tf_op jit(solution)/shard_map/ppermute | solution.py:443
  14.4 1.4 %collective-permute-start.4 = (f32[176,256]{1,0:T(8,128)S(1)}, f32[176,256]{1,0:T(8,128)S(1)}, u32[]{:S(2)}, u32[]{:S(2)}) collective-permute-start(f32[176,256]{1,0:T(8,128)S(1)} %get-tuple-element.24), channel_id=1, source_target_pairs={{4,0},{8,4},{12,8},{16,12},{20,16},{24,20},{28,24},{32,28},{36,32}... | collective-permute-start | bytes 540680 | tf_op jit(solution)/shard_map/ppermute | solution.py:443
  15.8 0.0 copy-done
  15.8 0.0 copy-done.1
  15.8 0.0 copy-done.4
  15.8 0.0 copy-done.3
  15.8 0.0 copy-done.2
  15.8 8.0 %inner.1 = (f32[2048,256]{1,0:T(8,128)}, f32[4,2,2,1568,128]{4,3,2,1,0:T(8,128)S(1)}, f32[2,2,1056,128]{3,2,1,0:T(8,128)S(1)}, f32[8,1056,128]{2,1,0:T(8,128)S(1)}, f32[4,512]{1,0:T(4,128)S(1)}) custom-call(s32[4]{0:T(128)S(1)} %copy-done.2, s32[8]{0:T(128)S(1)} %copy-done.3, f32[8]{0:T(128)S(1)} %copy-done.4, f32[2048,256]{1,0:T(8,128)S(1)} %copy-done, ...), custom_call_target="tpu_custom_call" | custom-call | flops 60000000 | bytes 25165824 | tf_op jit(solution)/shard_map/inner/pallas_call | solution.py:371
  23.8 0.0 collective-permute-done.before
  23.8 2.5 %left.1 = (f32[2048,256]{1,0:T(8,128)}, f32[4,2,2,1568,128]{4,3,2,1,0:T(8,128)S(1)}, f32[2,2,1056,128]{3,2,1,0:T(8,128)S(1)}, f32[8,1056,128]{2,1,0:T(8,128)S(1)...) custom-call(s32[4]{0:T(128)S(1)} %copy-done.2, ...), custom_call_target="tpu_custom_call", output_to_operand_aliasing={{0}: (5, {}), {1}: (6, {}), {2}: (7, {}), {3}: (8, {})} | custom-call | flops 15000000 | bytes 8388608 | tf_op jit(solution)/shard_map/left/pallas_call | solution.py:389
  26.3 0.0 collective-permute-done.2.after
  26.3 0.0 collective-permute-done.3.after_next
  26.3 0.0 collective-permute-done.4.after_last
  26.3 0.0 collective-permute-done.1.before_far
  26.3 4.5 %rest.1 = (f32[2048,256]{1,0:T(8,128)}, f32[4,2,2,1568,128]{4,3,2,1,0:T(8,128)S(1)}, f32[2,2,1056,128]{3,2,1,0:T(8,128)S(1)}, f32[8,1056,128]{2,1,0:T(8,128)S(1)}, f32[4,1024]{1,0:T(4,128)S(1)}) custom-call(s32[4]{0:T(128)S(1)} %copy-done.2, s32[8]{0:T(128)S(1)} %copy-done.3, ...), custom_call_target="tpu_custom_call", output_to_operand_aliasing={{0}: (12, {}), {1}: (13, {}), {2}: (14, {}), {3}: (15, {})} | custom-call | flops 30000000 | bytes 8388608 | tf_op jit(solution)/shard_map/rest/pallas_call | solution.py:410
  30.8 2.2 %collective-permute-start.5 = (f32[4,1024]{1,0:T(4,128)S(1)}, f32[4,1024]{1,0:T(4,128)S(1)}, u32[]{:S(2)}, u32[]{:S(2)}) collective-permute-start(f32[4,1024]{1,0:T(4,128)S(1)} %get-tuple-element.37), channel_id=1, source_target_pairs={{0,1},{1,0},{2,3},{3,2},{4,5},{5,4},{6,7},{7,6},{8,9},{9,8},{10,11... | collective-permute-start | bytes 49160 | tf_op jit(solution)/shard_map/ppermute | solution.py:455
  33.0 0.8 %collective-permute-done.5 = f32[4,1024]{1,0:T(4,128)S(1)} collective-permute-done((f32[4,1024]{1,0:T(4,128)S(1)}, f32[4,1024]{1,0:T(4,128)S(1)}, u32[]{:S(2)}, u32[]{:S(2)}) %collective-permute-start.5) | collective-permute-done | bytes 16416 | tf_op jit(solution)/shard_map/ppermute | solution.py:455
  33.9 2.6 %collective-permute-start.6 = (f32[4,1024]{1,0:T(4,128)S(1)}, f32[4,1024]{1,0:T(4,128)S(1)}, u32[]{:S(2)}, u32[]{:S(2)}) collective-permute-start(f32[4,1024]{1,0:T(4,128)S(1)} %add.6), channel_id=1, source_target_pairs={{0,2},{1,3},{2,0},{3,1},{4,6},{5,7},{6,4},{7,5},{8,10},{9,11},{10,... | collective-permute-start | bytes 49160 | tf_op jit(solution)/shard_map/ppermute | solution.py:455
  36.5 1.5 %collective-permute-done.6 = f32[4,1024]{1,0:T(4,128)S(1)} collective-permute-done((f32[4,1024]{1,0:T(4,128)S(1)}, f32[4,1024]{1,0:T(4,128)S(1)}, u32[]{:S(2)}, u32[]{:S(2)}) %collective-permute-start.6) | collective-permute-done | bytes 16416 | tf_op jit(solution)/shard_map/ppermute | solution.py:455
  37.9 0.6 %add.7 = f32[4,1024]{1,0:T(4,128)} add(f32[4,1024]{1,0:T(4,128)S(1)} %add.6, f32[4,1024]{1,0:T(4,128)S(1)} %collective-permute-done.6) | non-fusion elementwise | flops 4096 | bytes 49152 | tf_op jit(solution)/shard_map/add | solution.py:455
  (1 shorter events, 0.0 us)
Async XLA Ops:
  0.6 15.1 %copy-start = (f32[2048,256]{1,0:T(8,128)S(1)}, f32[2048,256]{1,0:T(8,128)}, u32[]{:S(2)}) copy-start(f32[2048,256]{1,0:T(8,128)} %slab.9) | copy-start | bytes 6291460
  0.6 15.1 %copy-start.1 = (f32[4,1024]{1,0:T(4,128)S(1)}, f32[4,1024]{1,0:T(4,128)}, u32[]{:S(2)}) copy-start(f32[4,1024]{1,0:T(4,128)} %angles.5) | copy-start | bytes 49156
  0.7 15.1 %copy-start.4 = (f32[8]{0:T(128)S(1)}, f32[8]{0:T(128)}, u32[]{:S(2)}) copy-start(f32[8]{0:T(128)} %weights.5) | copy-start | bytes 100
  0.7 15.1 %copy-start.3 = (s32[8]{0:T(128)S(1)}, s32[8]{0:T(128)}, u32[]{:S(2)}) copy-start(s32[8]{0:T(128)} %offsets.5) | copy-start | bytes 100
  0.7 15.1 %copy-start.2 = (s32[4]{0:T(128)S(1)}, s32[4]{0:T(128)}, u32[]{:S(2)}) copy-start(s32[4]{0:T(128)} %pairing.5) | copy-start | bytes 52
  1.9 21.9 %collective-permute-start = (f32[288,256]{1,0:T(8,128)S(1)}, f32[288,256]{1,0:T(8,128)S(1)}, u32[]{:S(2)}, u32[]{:S(2)}) collective-permute-start(f32[288,256]{1,0:T(8,128)S(1)} %get-tuple-element.20), channel_id=1, source_target_pairs={{0,4},{4,8},{8,12},{12,16},{16,20},{20,24},{24,28},{28,32},{32,36}... | collective-permute-start | bytes 884744 | tf_op jit(solution)/shard_map/ppermute | solution.py:440
  4.0 22.3 %collective-permute-start.1 = (f32[240,256]{1,0:T(8,128)S(1)}, f32[240,256]{1,0:T(8,128)S(1)}, u32[]{:S(2)}, u32[]{:S(2)}) collective-permute-start(f32[240,256]{1,0:T(8,128)S(1)} %get-tuple-element.21.refs_0_), channel_id=1, source_target_pairs={{0,4},{4,8},{8,12},{12,16},{16,20},{20,24},{24,28},{28,32},{32,36}... | collective-permute-start | bytes 737288 | tf_op jit(solution)/shard_map/ppermute | solution.py:441
  6.4 19.9 %collective-permute-start.2 = (f32[176,256]{1,0:T(8,128)S(1)}, f32[176,256]{1,0:T(8,128)S(1)}, u32[]{:S(2)}, u32[]{:S(2)}) collective-permute-start(f32[176,256]{1,0:T(8,128)S(1)} %get-tuple-element.22), channel_id=1, source_target_pairs={{4,0},{8,4},{12,8},{16,12},{20,16},{24,20},{28,24},{32,28},{36,32}... | collective-permute-start | bytes 540680 | tf_op jit(solution)/shard_map/ppermute | solution.py:443
  12.9 13.4 %collective-permute-start.3 = (f32[176,256]{1,0:T(8,128)S(1)}, f32[176,256]{1,0:T(8,128)S(1)}, u32[]{:S(2)}, u32[]{:S(2)}) collective-permute-start(f32[176,256]{1,0:T(8,128)S(1)} %get-tuple-element.23), channel_id=1, source_target_pairs={{4,0},{8,4},{12,8},{16,12},{20,16},{24,20},{28,24},{32,28},{36,32}... | collective-permute-start | bytes 540680 | tf_op jit(solution)/shard_map/ppermute | solution.py:443
  14.4 11.9 %collective-permute-start.4 = (f32[176,256]{1,0:T(8,128)S(1)}, f32[176,256]{1,0:T(8,128)S(1)}, u32[]{:S(2)}, u32[]{:S(2)}) collective-permute-start(f32[176,256]{1,0:T(8,128)S(1)} %get-tuple-element.24), channel_id=1, source_target_pairs={{4,0},{8,4},{12,8},{16,12},{20,16},{24,20},{28,24},{32,28},{36,32}... | collective-permute-start | bytes 540680 | tf_op jit(solution)/shard_map/ppermute | solution.py:443
  30.8 3.0 %collective-permute-start.5 = (f32[4,1024]{1,0:T(4,128)S(1)}, f32[4,1024]{1,0:T(4,128)S(1)}, u32[]{:S(2)}, u32[]{:S(2)}) collective-permute-start(f32[4,1024]{1,0:T(4,128)S(1)} %get-tuple-element.37), channel_id=1, source_target_pairs={{0,1},{1,0},{2,3},{3,2},{4,5},{5,4},{6,7},{7,6},{8,9},{9,8},{10,11... | collective-permute-start | bytes 49160 | tf_op jit(solution)/shard_map/ppermute | solution.py:455
  33.9 4.1 %collective-permute-start.6 = (f32[4,1024]{1,0:T(4,128)S(1)}, f32[4,1024]{1,0:T(4,128)S(1)}, u32[]{:S(2)}, u32[]{:S(2)}) collective-permute-start(f32[4,1024]{1,0:T(4,128)S(1)} %add.6), channel_id=1, source_target_pairs={{0,2},{1,3},{2,0},{3,1},{4,6},{5,7},{6,4},{7,5},{8,10},{9,11},{10,... | collective-permute-start | bytes 49160 | tf_op jit(solution)/shard_map/ppermute | solution.py:455

commit v2 on v1

--- a/solution.py
+++ b/solution.py
@@ -12,14 +12,15 @@
 PAIRS = 1024
 NEAR = 280
 FAR_ROWS = 240
-THIRD = 176
+HALO = NEAR + FAR_ROWS
+SENT = NEAR + 8
 PAD = 272
 LENGTH = PAD + PAIRS + PAD
 WINDOW = 160
 FAR_WINDOW = 136
+FULL_WINDOW = 288
 FRONT = 8
 GFRONT = 8
-RANGE = 304
 
 
 def fill_table(table, at, angle, low=0, high=128):
@@ -201,13 +202,8 @@
             table[lane, pl.ds(FRONT + PAIRS, 16), :] = halo_table[lane, pl.ds(16, 16), :]
 
 
-def near_side(
-    side, lead, offsets, weights, raw, window, source, states, adjoint, table, halo_table, turned, products, out, evolved, sems
-):
-    forward(raw, window, FRONT, halo_table, (120, 0)[side], lead, WINDOW, 80)
+def boundary(side, at, lead, window, states, out, evolved, sems):
     stores = []
-    blank = jnp.zeros((272, 128), jnp.float32)
-    at = FRONT + (144, 8)[side]
     for half in range(2):
         out[half, pl.ds(lead, 16, stride=2), :] = window[3, 0, half, pl.ds(at - 9, 16), :]
         out[half, pl.ds(lead + 1, 16, stride=2), :] = window[3, 1, half, pl.ds(at - 8, 16), :]
@@ -223,36 +219,7 @@
                 states[layer, parity, half, pl.ds(PAD + (-8, PAIRS - 8)[side], 16), :] = window[
                     layer, parity, half, pl.ds(at + (-8, 0)[side], 16), :
                 ]
-            if side == 0:
-                source[parity, half, pl.ds(0, 136), :] = blank[:136]
-                source[parity, half, pl.ds(136, 144), :] = window[3, parity, half, pl.ds(FRONT + 8, 144), :]
-                source[parity, half, pl.ds(280, 272), :] = blank
-            else:
-                source[parity, half, pl.ds(0, 272), :] = blank
-                source[parity, half, pl.ds(272, 144), :] = window[3, parity, half, pl.ds(FRONT + 8, 144), :]
-                source[parity, half, pl.ds(416, 128), :] = blank[:128]
-    band(source, (264, 0)[side], adjoint, FRONT + (0, 752)[side], offsets, weights, 288, 96, ((-1,), (1,))[side], True)
-    band(source, (264, 272)[side], adjoint, FRONT + (0, PAIRS)[side], offsets, weights, 16, 16, ((1,), (-1,))[side], True)
-    begin = (120, 744)[side]
-    backward(states, PAD + begin, adjoint, FRONT + 8 + begin, turned, products, table, FRONT + begin, lead, 160, 80)
     return stores
-
-
-def far_side(side, lead, offsets, weights, raw, window, source, states, adjoint, table, halo_table, turned, products):
-    forward(raw, window, FRONT, halo_table, (0, 144)[side], lead, FAR_WINDOW, 136)
-    blank = jnp.zeros((272, 128), jnp.float32)
-    for parity in range(2):
-        for half in range(2):
-            value = window[3, parity, half, pl.ds(FRONT + (0, 8)[side], 128), :]
-            if side == 0:
-                source[parity, half, pl.ds(8, 128), :] = value
-                source[parity, half, pl.ds(136, 272), :] = blank
-            else:
-                source[parity, half, pl.ds(0, 272), :] = blank
-                source[parity, half, pl.ds(272, 128), :] = value
-    band(source, (264, 0)[side], adjoint, FRONT + (0, 896)[side], offsets, weights, 144, 144, ((-1,), (1,))[side], True)
-    begin = (-8, 888)[side]
-    backward(states, PAD + begin, adjoint, FRONT + 8 + begin, turned, products, table, FRONT + begin, lead, 144, 144)
 
 
 def left_kernel(
@@ -264,10 +231,17 @@
     near_tables(0, before, NEAR, table, halo_table)
     for load in loads:
         load.wait()
-    stores = near_side(
-        0, lead, offsets, weights, raw, window, source, states, adjoint, table, halo_table, turned, products, out, evolved,
-        sems.at[pl.ds(4, 2)],
-    )
+    forward(raw, window, FRONT, halo_table, 120, lead, WINDOW, 80)
+    stores = boundary(0, FRONT + 144, lead, window, states, out, evolved, sems.at[pl.ds(4, 2)])
+    blank = jnp.zeros((272, 128), jnp.float32)
+    for half in range(2):
+        for parity in range(2):
+            source[parity, half, pl.ds(0, 136), :] = blank[:136]
+            source[parity, half, pl.ds(136, 144), :] = window[3, parity, half, pl.ds(FRONT + 8, 144), :]
+            source[parity, half, pl.ds(280, 272), :] = blank
+    band(source, 264, adjoint, FRONT, offsets, weights, 288, 96, (-1,), True)
+    band(source, 264, adjoint, FRONT, offsets, weights, 16, 16, (1,), True)
+    backward(states, PAD + 120, adjoint, FRONT + 8 + 120, turned, products, table, FRONT + 120, lead, 160, 80)
     lane = lax.broadcasted_iota(jnp.int32, (LAYERS, 128), 1)
     gradient[:, 0:128] = summed(products, lead, 8)
     gradient[:, 128:256] = jnp.where(lane < 16, summed(products, lead, 136), inner[:, 0:128])
@@ -276,40 +250,56 @@
         store.wait()
 
 
-def rest_kernel(
-    pairing, offsets, weights, slab, before, before_far, after, after_next, after_last, left_table, inner, left,
-    evolved_in, states_in, adjoint_in, table_in,
-    evolved, states, adjoint, table, gradient, raw, raw_left, raw_right, window, source, turned, products, right_table, out, sems,
+def left_far_kernel(
+    pairing, offsets, weights, before, before_far, states, table, halo_table, rest, adjoint_in,
+    adjoint, gradient, raw, window, source, turned, products, sems,
+):
+    loads = started(((before_far, SENT - FAR_ROWS, 8, FAR_ROWS), (before, 0, 8 + FAR_ROWS, 32)), raw, sems)
+    lead = pairing[0]
+    blank = jnp.zeros((272, 128), jnp.float32)
+    for half in range(2):
+        for parity in range(2):
+            source[parity, half, pl.ds(136, 272), :] = blank
+    gradient[:, 128:1024] = rest[...]
+    for load in loads:
+        load.wait()
+    forward(raw, window, FRONT, halo_table, 0, lead, FAR_WINDOW, 136)
+    for half in range(2):
+        for parity in range(2):
+            source[parity, half, pl.ds(8, 128), :] = window[3, parity, half, pl.ds(FRONT, 128), :]
+    band(source, 264, adjoint, FRONT, offsets, weights, 144, 144, (-1,), True)
+    backward(states, PAD - 8, adjoint, FRONT, turned, products, table, FRONT - 8, lead, 144, 144)
+    gradient[:, 0:128] = summed(products, lead, 8)
+
+
+def right_kernel(
+    pairing, offsets, weights, slab, after, after_far, inner, left, evolved_in, states_in, adjoint_in, table_in,
+    evolved, states, adjoint, table, gradient, raw, window, source, turned, products, halo_table, out, sems,
 ):
     loads = started(
-        ((slab, ROWS - 32, 0, 32), (after, 0, 32, THIRD), (after_next, 0, 32 + THIRD, NEAR - THIRD)), raw, sems
-    )
-    loads_left = started(((before_far, 0, 8, FAR_ROWS), (before, 0, 8 + FAR_ROWS, 32)), raw_left, sems.at[pl.ds(6, 4)])
-    loads_right = started(
-        ((after_next, NEAR - 24 - THIRD, 0, 2 * THIRD + 24 - NEAR), (after_last, 0, 2 * THIRD + 24 - NEAR, THIRD - 8)),
-        raw_right,
-        sems.at[pl.ds(10, 4)],
+        ((slab, ROWS - 32, 0, 32), (after, 0, 32, NEAR), (after_far, 0, 32 + NEAR, FAR_ROWS)), raw, sems
     )
     lead = pairing[0]
-    near_tables(1, after_last, THIRD - 8, table, right_table)
+    near_tables(1, after, NEAR, table, halo_table)
+    blank = jnp.zeros((272, 128), jnp.float32)
+    for half in range(2):
+        for parity in range(2):
+            source[parity, half, pl.ds(0, 272), :] = blank
+    gradient[:, 0:512] = left[...]
     for load in loads:
         load.wait()
-    common = (window, source, states, adjoint, table)
-    stores = near_side(
-        1, lead, offsets, weights, raw, *common, right_table, turned, products, out, evolved, sems.at[pl.ds(14, 2)]
-    )
+    forward(raw, window, FRONT, halo_table, 0, lead, FULL_WINDOW, 144)
+    stores = boundary(1, FRONT + 8, lead, window, states, out, evolved, sems.at[pl.ds(6, 2)])
+    for half in range(2):
+        for parity in range(2):
+            source[parity, half, pl.ds(272, 280), :] = window[3, parity, half, pl.ds(FRONT + 8, 280), :]
+    band(source, 0, adjoint, FRONT + 752, offsets, weights, 288, 144, (1,), True)
+    band(source, 272, adjoint, FRONT + PAIRS, offsets, weights, 16, 16, (-1,), True)
+    backward(states, PAD + 744, adjoint, FRONT + 8 + 744, turned, products, table, FRONT + 744, lead, 288, 144)
     lane = lax.broadcasted_iota(jnp.int32, (LAYERS, 128), 1)
-    gradient[:, 128:640] = left[...]
-    gradient[:, 640:768] = jnp.where(lane < 112, inner[:, 384:512], pltpu.roll(summed(products, lead, 8), 112, 1))
-    gradient[:, 768:896] = summed(products, lead, 24)
-    for load in loads_left:
-        load.wait()
-    far_side(0, lead, offsets, weights, raw_left, *common, left_table, turned, products)
-    gradient[:, 0:128] = summed(products, lead, 8)
-    for load in loads_right:
-        load.wait()
-    far_side(1, lead, offsets, weights, raw_right, *common, right_table, turned, products)
-    gradient[:, 896:1024] = summed(products, lead, 8)
+    gradient[:, 512:640] = jnp.where(lane < 112, inner[:, 384:512], pltpu.roll(summed(products, lead, 8), 112, 1))
+    gradient[:, 640:768] = summed(products, lead, 24)
+    gradient[:, 768:896] = summed(products, lead, 152)
     for store in stores:
         store.wait()
 
@@ -322,7 +312,7 @@
 STATES = jax.ShapeDtypeStruct((LAYERS, 2, 2, LENGTH, 128), jnp.float32)
 ADJOINT = jax.ShapeDtypeStruct((2, 2, PAIRS + 32, 128), jnp.float32)
 TABLE = jax.ShapeDtypeStruct((2 * LAYERS, PAIRS + 32, 128), jnp.float32)
-HALO_TABLE = jax.ShapeDtypeStruct((2 * LAYERS, 296, 128), jnp.float32)
+HALO_TABLE = jax.ShapeDtypeStruct((2 * LAYERS, 304, 128), jnp.float32)
 
 
 def limits(flops, traffic, grant=16):
@@ -336,7 +326,9 @@
     return pltpu.VMEM(shape, jnp.float32)
 
 
-def pack_call(slab, angles, pieces, angle_at, *earlier):
+def pack_call(slab, angles, pieces, *earlier):
+    shapes = [(rows + (0 if lane is None else 8), 256) for _, rows, lane in pieces]
+
     def kernel(slab, angles, *refs):
         packed, tiles, sems = refs[len(earlier) : len(earlier) + len(pieces)], refs[-2], refs[-1]
         copies = [pltpu.make_async_copy(angles, tiles, sems.at[len(pieces)])]
@@ -347,10 +339,11 @@
         for copy in copies:
             copy.start()
         copies[0].wait()
-        for n, (_, rows, follow) in enumerate(pieces):
-            for row in range(2 * follow):
-                lanes = slice(angle_at + 256 * row, angle_at + 256 * (row + 1))
-                packed[n][rows + 4 * row : rows + 4 * (row + 1), :] = tiles[:, lanes]
+        for n, (_, rows, lane) in enumerate(pieces):
+            if lane is not None:
+                for row in range(2):
+                    lanes = slice(lane + 256 * row, lane + 256 * (row + 1))
+                    packed[n][rows + 4 * row : rows + 4 * (row + 1), :] = tiles[:, lanes]
         for copy in copies[1:]:
             copy.wait()
 
@@ -358,10 +351,10 @@
     angles = pltpu.with_memory_space_constraint(angles, pltpu.HBM)
     return pl.pallas_call(
         kernel,
-        out_shape=[jax.ShapeDtypeStruct((rows + 8 * follow, 256), jnp.float32) for _, rows, follow in pieces],
+        out_shape=[jax.ShapeDtypeStruct(shape, jnp.float32) for shape in [*shapes, (LAYERS, PAIRS)]],
         in_specs=[pl.BlockSpec(memory_space=pltpu.HBM)] * 2 + [FAR] * len(earlier),
-        out_specs=[WHOLE] * len(pieces),
-        scratch_shapes=[room(LAYERS, PAIRS), pltpu.SemaphoreType.DMA((len(pieces) + 1,))],
+        out_specs=[WHOLE] * (len(pieces) + 1),
+        scratch_shapes=[pltpu.SemaphoreType.DMA((len(pieces) + 1,))],
         name="pack",
         **limits(1000, 2**20),
     )(slab, angles, *earlier)
@@ -406,27 +399,45 @@
     )(pairing, offsets, weights, slab, before, evolved, states, adjoint, table, inner)
 
 
-def rest_call(*operands):
+def left_far_call(pairing, offsets, weights, before, before_far, states, table, halo_table, rest, adjoint):
     return pl.pallas_call(
-        rest_kernel,
-        out_shape=(EVOLVED, STATES, ADJOINT, TABLE, jax.ShapeDtypeStruct((LAYERS, PAIRS), jnp.float32)),
-        in_specs=[SMALL, SMALL, SMALL, FAR] + [WHOLE] * 8 + [FAR, WHOLE, WHOLE, WHOLE],
+        left_far_kernel,
+        out_shape=(ADJOINT, jax.ShapeDtypeStruct((LAYERS, PAIRS), jnp.float32)),
+        in_specs=[SMALL, SMALL, SMALL] + [WHOLE] * 7,
+        out_specs=(WHOLE, WHOLE),
+        scratch_shapes=[
+            room(2, 280, 128),
+            room(LAYERS, 2, 2, FAR_WINDOW + 16, 128),
+            room(2, 2, 408, 128),
+            room(LAYERS - 1, 2, 2, 144 + 16, 128),
+            room(LAYERS, 160, 128),
+            pltpu.SemaphoreType.DMA((4,)),
+        ],
+        input_output_aliases={9: 0},
+        name="left_far",
+        **limits(10_000_000, 8 * 2**20),
+    )(pairing, offsets, weights, before, before_far, states, table, halo_table, rest, adjoint)
+
+
+def right_call(*operands):
+    return pl.pallas_call(
+        right_kernel,
+        out_shape=(EVOLVED, STATES, ADJOINT, TABLE, jax.ShapeDtypeStruct((LAYERS, 896), jnp.float32)),
+        in_specs=[SMALL, SMALL, SMALL, FAR] + [WHOLE] * 4 + [FAR, WHOLE, WHOLE, WHOLE],
         out_specs=(FAR, WHOLE, WHOLE, WHOLE, WHOLE),
         scratch_shapes=[
-            room(2, 328, 128),
-            room(2, 280, 128),
-            room(2, 280, 128),
-            room(LAYERS, 2, 2, WINDOW + 16, 128),
-            room(2, 2, 552, 128),
-            room(LAYERS - 1, 2, 2, 160 + 16, 128),
-            room(LAYERS, 280, 128),
-            room(2 * LAYERS, 296, 128),
+            room(2, 2 * FULL_WINDOW + 8, 128),
+            room(LAYERS, 2, 2, FULL_WINDOW + 16, 128),
+            room(2, 2, 560, 128),
+            room(LAYERS - 1, 2, 2, 288 + 16, 128),
+            room(LAYERS, 304, 128),
+            room(2 * LAYERS, 304, 128),
             room(2, 40, 128),
-            pltpu.SemaphoreType.DMA((16,)),
+            pltpu.SemaphoreType.DMA((8,)),
         ],
-        input_output_aliases={12: 0, 13: 1, 14: 2, 15: 3},
-        name="rest",
-        **limits(30_000_000, 8 * 2**20),
+        input_output_aliases={8: 0, 9: 1, 10: 2, 11: 3},
+        name="right",
+        **limits(20_000_000, 8 * 2**20),
     )(*operands)
 
 
@@ -434,21 +445,22 @@
     count = lax.axis_size("blk")
     onward = [(i, (i + 1) % count) for i in range(count)]
     back = [((i + 1) % count, i) for i in range(count)]
-    tail, far_tail = pack_call(
-        slab, angles, ((ROWS - NEAR, NEAR, 1), (ROWS - NEAR - FAR_ROWS, FAR_ROWS, 0)), 512
+    tail, far_tail, head, far_head, angles_near = pack_call(
+        slab, angles, ((ROWS - NEAR, NEAR, 512), (ROWS - NEAR - SENT, SENT, None), (0, NEAR, 0), (NEAR, SENT, None))
     )
     before = lax.ppermute(tail, "blk", onward)
     before_far = lax.ppermute(far_tail, "blk", onward)
-    heads = pack_call(slab, angles, ((0, THIRD, 0), (THIRD, THIRD, 0), (2 * THIRD, THIRD - 8, 1)), 0, far_tail)
-    after = [lax.ppermute(head, "blk", back) for head in heads]
-    scalars = (pairing, band_offsets, band_weights)
-    evolved, states, adjoint, table, gradient = inner_call(*scalars, slab, angles)
+    after = lax.ppermute(head, "blk", back)
+    after_far = lax.ppermute(far_head, "blk", back)
+    scalars = [pltpu.with_memory_space_constraint(x, pltpu.HBM) for x in (pairing, band_offsets, band_weights)]
+    evolved, states, adjoint, table, inner = inner_call(*scalars, slab, angles_near)
     evolved, states, adjoint, table, left_table, left = left_call(
-        *scalars, slab, before, evolved, states, adjoint, table, gradient
-    )
-    evolved, _, _, _, gradient = rest_call(
-        *scalars, slab, before, before_far, *after, left_table, gradient, left, evolved, states, adjoint, table
-    )
+        *scalars, slab, before, evolved, states, adjoint, table, inner
+    )
+    evolved, states, adjoint, table, rest = right_call(
+        *scalars, slab, after, after_far, inner, left, evolved, states, adjoint, table
+    )
+    _, gradient = left_far_call(*scalars, before, before_far, states, table, left_table, rest, adjoint)
     columns = lax.axis_size("col")
     step = 1
     while step < columns:

time: 38.8 us -> 36.3 us (0.936)
  starting transfers between devices: 17.5 us -> 15.5 us
  Pallas kernels: 17.3 us -> 16.9 us
    ppermute x1, starting transfers between devices: 1.21 us -> 0.09 us  [on_device(): before_far = lax.ppermute(far_tail, 'blk', onward)]
    pallas_call x3, Pallas kernels: 6.87 us -> 6.12 us  [the longest x1 3.08 us: right_call(): pl.pallas_call(right_kernel, out_shape=(EVOLVED, STATES, ADJOINT, TABLE,...]
    ppermute x2, starting transfers between devices: 4.78 us -> 4.22 us  [on_device(): lax.ppermute(gradient, 'col', [(i, i ^ step) for i in range(columns)])]
    ppermute x3 -> x2, starting transfers between devices: 9.37 us -> 9.04 us  [the longest x1 7.66 us: on_device(): after = lax.ppermute(head, 'blk', back)]
  transfers between devices with their start and end apart: 7 -> 6, of which waited for: 2 -> 2; matrix products, arithmetic and copies ran while one was open for 0% -> 0% of each run, Pallas kernels for 30% -> 38%
where the time goes in v2:
time: 36.3 us; the launch traced here: 36 us
  Pallas kernels  16.9 us (47%)
  starting transfers between devices  15.5 us (43%)
  waiting for transfers between devices  2.32 us (6%)
  between operations  0.71 us (2%)
  other arithmetic  0.62 us (2%)
    pallas_call x1, Pallas kernels, inner_call(): pl.pallas_call(inner_kernel, out_shape=(EVOLVED, STATES, ADJOINT, TABLE,...  8.17 us
    ppermute x1, starting transfers between devices, on_device(): after = lax.ppermute(head, 'blk', back)  7.66 us
    ppermute x2, starting transfers between devices, on_device(): lax.ppermute(gradient, 'col', [(i, i ^ step) for i in range(columns)])  4.22 us
    pallas_call x1, Pallas kernels, right_call(): pl.pallas_call(right_kernel, out_shape=(EVOLVED, STATES, ADJOINT, TABLE,...  3.08 us
    pallas_call x1, Pallas kernels, left_call(): pl.pallas_call(left_kernel, out_shape=(EVOLVED, STATES, ADJOINT, TABLE, H...  2.58 us
    ppermute x2, waiting for transfers between devices, on_device(): lax.ppermute(gradient, 'col', [(i, i ^ step) for i in range(columns)])  2.31 us
    ppermute x1, starting transfers between devices, on_device(): before = lax.ppermute(tail, 'blk', onward)  2.12 us
    pallas_call x1, Pallas kernels, left_far_call(): pl.pallas_call(left_far_kernel, out_shape=(ADJOINT, jax.ShapeDtypeStruct(...  1.61 us
  transfers between devices with their start and end apart: 6, of which 2 were waited for; matrix products, arithmetic and copies ran while one was open for 0% of the time, Pallas kernels for 38%

profile of v2, /device:TPU:1, one launch (start us, length us, event | category | flops | bytes accessed | tf_op | source)
XLA Modules:
  0.0 36.0 jit_solution(6059063117643417754)
XLA Ops:
  0.6 0.0 copy-start
  0.6 1.4 %pack.1 = (f32[288,256]{1,0:T(8,128)S(1)}, f32[288,256]{1,0:T(8,128)S(1)}, f32[288,256]{1,0:T(8,128)S(1)}, f32[288,256]{1,0:T(8,128)S(1)}, f32[4,1024]{1,0:T(4,128)S(1)}) custom-call(f32[2048,256]{1,0:T(8,128)} %slab.7, f32[4,1024]{1,0:T(4,128)} %angles.1), custom_call_target="tpu_custom_call" | custom-call | flops 1000 | bytes 1048576 | tf_op jit(solution)/shard_map/pack/pallas_call | solution.py:352
  2.1 2.1 %collective-permute-start.2 = (f32[288,256]{1,0:T(8,128)S(1)}, f32[288,256]{1,0:T(8,128)S(1)}, u32[]{:S(2)}, u32[]{:S(2)}) collective-permute-start(f32[288,256]{1,0:T(8,128)S(1)} %get-tuple-element.28), channel_id=1, source_target_pairs={{0,4},{4,8},{8,12},{12,16},{16,20},{20,24},{24,28},{28,32},{32,36}... | collective-permute-start | bytes 884744 | tf_op jit(solution)/shard_map/ppermute | solution.py:451
  4.2 7.7 %collective-permute-start = (f32[288,256]{1,0:T(8,128)S(1)}, f32[288,256]{1,0:T(8,128)S(1)}, u32[]{:S(2)}, u32[]{:S(2)}) collective-permute-start(f32[288,256]{1,0:T(8,128)S(1)} %get-tuple-element.24), channel_id=1, source_target_pairs={{4,0},{8,4},{12,8},{16,12},{20,16},{24,20},{28,24},{32,28},{36,32}... | collective-permute-start | bytes 884744 | tf_op jit(solution)/shard_map/ppermute | solution.py:453
  11.9 1.4 %collective-permute-start.1 = (f32[288,256]{1,0:T(8,128)S(1)}, f32[288,256]{1,0:T(8,128)S(1)}, u32[]{:S(2)}, u32[]{:S(2)}) collective-permute-start(f32[288,256]{1,0:T(8,128)S(1)} %get-tuple-element.25), channel_id=1, source_target_pairs={{4,0},{8,4},{12,8},{16,12},{20,16},{24,20},{28,24},{32,28},{36,32}... | collective-permute-start | bytes 884744 | tf_op jit(solution)/shard_map/ppermute | solution.py:454
  13.2 0.1 collective-permute-start.3
  13.3 0.0 copy-done
  13.3 8.2 %inner.1 = (f32[2048,256]{1,0:T(8,128)}, f32[4,2,2,1568,128]{4,3,2,1,0:T(8,128)S(1)}, f32[2,2,1056,128]{3,2,1,0:T(8,128)S(1)}, f32[8,1056,128]{2,1,0:T(8,128)S(1)}, f32[4,512]{1,0:T(4,128)S(1)}) custom-call(s32[4]{0:T(128)} %pairing.7, s32[8]{0:T(128)} %offsets.7, f32[8]{0:T(128)} %weights.7, f32[2048,256]{1,0:T(8,128)S(1)} %copy-done, ...), custom_call_target="tpu_custom_call" | custom-call | flops 60000000 | bytes 25165824 | tf_op jit(solution)/shard_map/inner/pallas_call | solution.py:364
  21.5 0.0 collective-permute-done.2.before
  21.5 2.6 %left.1 = (f32[2048,256]{1,0:T(8,128)}, f32[4,2,2,1568,128]{4,3,2,1,0:T(8,128)S(1)}, f32[2,2,1056,128]{3,2,1,0:T(8,128)S(1)}, f32[8,1056,128]{2,1,0:T(8,128)S(1)...) custom-call(s32[4]{0:T(128)} %pairing.7, ...), custom_call_target="tpu_custom_call", output_to_operand_aliasing={{0}: (5, {}), {1}: (6, {}), {2}: (7, {}), {3}: (8, {})} | custom-call | flops 15000000 | bytes 8388608 | tf_op jit(solution)/shard_map/left/pallas_call | solution.py:382
  24.1 0.0 collective-permute-done.after
  24.1 0.0 collective-permute-done.1.after_far
  24.1 3.1 %right.1 = (f32[2048,256]{1,0:T(8,128)}, f32[4,2,2,1568,128]{4,3,2,1,0:T(8,128)S(1)}, f32[2,2,1056,128]{3,2,1,0:T(8,128)S(1)}, f32[8,1056,128]{2,1,0:T(8,128)S(1)}, f32[4,896]{1,0:T(4,128)S(1)}) custom-call(s32[4]{0:T(128)} %pairing.7, s32[8]{0:T(128)} %offsets.7, ...), custom_call_target="tpu_custom_call", output_to_operand_aliasing={{0}: (8, {}), {1}: (9, {}), {2}: (10, {}), {3}: (11, {})} | custom-call | flops 20000000 | bytes 8388608 | tf_op jit(solution)/shard_map/right/pallas_call | solution.py:423
  27.2 0.0 collective-permute-done.3.before_far
  27.2 1.6 %left_far.1 = (f32[2,2,1056,128]{3,2,1,0:T(8,128)S(1)}, f32[4,1024]{1,0:T(4,128)S(1)}) custom-call(s32[4]{0:T(128)} %pairing.7, s32[8]{0:T(128)} %offsets.7, f32[8]{0:T(128)} %weights.7, f32[288,256]{1,0:T(8,128)S(1)} %collective-permute-done.2.before, f32[288,256]{1,0:T(8,128)S(1)} %collective-permute-done.3.before_far, ...), custom_call_target="tpu_custom_call", output_to_operand_aliasing={{0}: (9, {})} | custom-call | flops 10000000 | bytes 8388608 | tf_op jit(solution)/shard_map/left_far/pallas_call | solution.py:403
  28.8 1.6 %collective-permute-start.4 = (f32[4,1024]{1,0:T(4,128)S(1)}, f32[4,1024]{1,0:T(4,128)S(1)}, u32[]{:S(2)}, u32[]{:S(2)}) collective-permute-start(f32[4,1024]{1,0:T(4,128)S(1)} %get-tuple-element.45), channel_id=1, source_target_pairs={{0,1},{1,0},{2,3},{3,2},{4,5},{5,4},{6,7},{7,6},{8,9},{9,8},{10,11... | collective-permute-start | bytes 49160 | tf_op jit(solution)/shard_map/ppermute | solution.py:467
  30.4 0.8 %collective-permute-done.4 = f32[4,1024]{1,0:T(4,128)S(1)} collective-permute-done((f32[4,1024]{1,0:T(4,128)S(1)}, f32[4,1024]{1,0:T(4,128)S(1)}, u32[]{:S(2)}, u32[]{:S(2)}) %collective-permute-start.4) | collective-permute-done | bytes 16416 | tf_op jit(solution)/shard_map/ppermute | solution.py:467
  31.3 2.6 %collective-permute-start.5 = (f32[4,1024]{1,0:T(4,128)S(1)}, f32[4,1024]{1,0:T(4,128)S(1)}, u32[]{:S(2)}, u32[]{:S(2)}) collective-permute-start(f32[4,1024]{1,0:T(4,128)S(1)} %add.6), channel_id=1, source_target_pairs={{0,2},{1,3},{2,0},{3,1},{4,6},{5,7},{6,4},{7,5},{8,10},{9,11},{10,... | collective-permute-start | bytes 49160 | tf_op jit(solution)/shard_map/ppermute | solution.py:467
  33.9 1.5 %collective-permute-done.5 = f32[4,1024]{1,0:T(4,128)S(1)} collective-permute-done((f32[4,1024]{1,0:T(4,128)S(1)}, f32[4,1024]{1,0:T(4,128)S(1)}, u32[]{:S(2)}, u32[]{:S(2)}) %collective-permute-start.5) | collective-permute-done | bytes 16416 | tf_op jit(solution)/shard_map/ppermute | solution.py:467
  35.4 0.6 %add.7 = f32[4,1024]{1,0:T(4,128)} add(f32[4,1024]{1,0:T(4,128)S(1)} %add.6, f32[4,1024]{1,0:T(4,128)S(1)} %collective-permute-done.5) | non-fusion elementwise | flops 4096 | bytes 49152 | tf_op jit(solution)/shard_map/add | solution.py:467
  (1 shorter events, 0.0 us)
Async XLA Ops:
  0.6 12.7 %copy-start = (f32[2048,256]{1,0:T(8,128)S(1)}, f32[2048,256]{1,0:T(8,128)}, u32[]{:S(2)}) copy-start(f32[2048,256]{1,0:T(8,128)} %slab.7) | copy-start | bytes 6291460
  2.1 19.4 %collective-permute-start.2 = (f32[288,256]{1,0:T(8,128)S(1)}, f32[288,256]{1,0:T(8,128)S(1)}, u32[]{:S(2)}, u32[]{:S(2)}) collective-permute-start(f32[288,256]{1,0:T(8,128)S(1)} %get-tuple-element.28), channel_id=1, source_target_pairs={{0,4},{4,8},{8,12},{12,16},{16,20},{20,24},{24,28},{28,32},{32,36}... | collective-permute-start | bytes 884744 | tf_op jit(solution)/shard_map/ppermute | solution.py:451
  4.2 19.9 %collective-permute-start = (f32[288,256]{1,0:T(8,128)S(1)}, f32[288,256]{1,0:T(8,128)S(1)}, u32[]{:S(2)}, u32[]{:S(2)}) collective-permute-start(f32[288,256]{1,0:T(8,128)S(1)} %get-tuple-element.24), channel_id=1, source_target_pairs={{4,0},{8,4},{12,8},{16,12},{20,16},{24,20},{28,24},{32,28},{36,32}... | collective-permute-start | bytes 884744 | tf_op jit(solution)/shard_map/ppermute | solution.py:453
  11.9 12.3 %collective-permute-start.1 = (f32[288,256]{1,0:T(8,128)S(1)}, f32[288,256]{1,0:T(8,128)S(1)}, u32[]{:S(2)}, u32[]{:S(2)}) collective-permute-start(f32[288,256]{1,0:T(8,128)S(1)} %get-tuple-element.25), channel_id=1, source_target_pairs={{4,0},{8,4},{12,8},{16,12},{20,16},{24,20},{28,24},{32,28},{36,32}... | collective-permute-start | bytes 884744 | tf_op jit(solution)/shard_map/ppermute | solution.py:454
  13.2 14.0 %collective-permute-start.3 = (f32[288,256]{1,0:T(8,128)S(1)}, f32[288,256]{1,0:T(8,128)S(1)}, u32[]{:S(2)}, u32[]{:S(2)}) collective-permute-start(f32[288,256]{1,0:T(8,128)S(1)} %get-tuple-element.39), channel_id=1, source_target_pairs={{0,4},{4,8},{8,12},{12,16},{16,20},{20,24},{24,28},{28,32},{32,36}... | collective-permute-start | bytes 884744 | tf_op jit(solution)/shard_map/ppermute | solution.py:452
  28.8 2.4 %collective-permute-start.4 = (f32[4,1024]{1,0:T(4,128)S(1)}, f32[4,1024]{1,0:T(4,128)S(1)}, u32[]{:S(2)}, u32[]{:S(2)}) collective-permute-start(f32[4,1024]{1,0:T(4,128)S(1)} %get-tuple-element.45), channel_id=1, source_target_pairs={{0,1},{1,0},{2,3},{3,2},{4,5},{5,4},{6,7},{7,6},{8,9},{9,8},{10,11... | collective-permute-start | bytes 49160 | tf_op jit(solution)/shard_map/ppermute | solution.py:467
  31.3 4.1 %collective-permute-start.5 = (f32[4,1024]{1,0:T(4,128)S(1)}, f32[4,1024]{1,0:T(4,128)S(1)}, u32[]{:S(2)}, u32[]{:S(2)}) collective-permute-start(f32[4,1024]{1,0:T(4,128)S(1)} %add.6), channel_id=1, source_target_pairs={{0,2},{1,3},{2,0},{3,1},{4,6},{5,7},{6,4},{7,5},{8,10},{9,11},{10,... | collective-permute-start | bytes 49160 | tf_op jit(solution)/shard_map/ppermute | solution.py:467

commit v3 on v2

--- a/solution.py
+++ b/solution.py
@@ -13,12 +13,15 @@
 NEAR = 280
 FAR_ROWS = 240
 HALO = NEAR + FAR_ROWS
-SENT = NEAR + 8
+SENT = 272
+HEAD = 256
+EARLY = 2
 PAD = 272
 LENGTH = PAD + PAIRS + PAD
 WINDOW = 160
 FAR_WINDOW = 136
-FULL_WINDOW = 288
+RIGHT_WINDOW = 144
+RIGHT_FAR_WINDOW = 152
 FRONT = 8
 GFRONT = 8
 
@@ -125,20 +128,51 @@
     return jnp.concatenate(rows, 0)
 
 
-def inner_kernel(
-    pairing, offsets, weights, slab, angles,
-    evolved, states, adjoint, table, gradient, raw, turned, products, out, sems,
-):
+def fetching(sources, scalars):
+    copies = [pltpu.make_async_copy(source, scalars[n], scalars[3].at[n]) for n, source in enumerate(sources)]
+    for copy in copies:
+        copy.start()
+    return copies
+
+
+def fetched(sources, scalars):
+    for copy in fetching(sources, scalars):
+        copy.wait()
+    return scalars[:3]
+
+
+def evolve(pairing, slab, angles, states, table, raw, flags, sems):
+    scalar = pltpu.make_async_copy(pairing, flags, sems.at[2])
+    scalar.start()
     loads = []
     for half in range(2):
         loads.append(pltpu.make_async_copy(slab.at[:, pl.ds(128 * half, 128)], raw.at[half, pl.ds(0, ROWS), :], sems.at[half]))
         loads[-1].start()
-    lead = pairing[0]
     for tile in range(8):
         fill_table(table, FRONT + 128 * tile, angles[:, 128 * tile : 128 * (tile + 1)])
     for load in loads:
         load.wait()
-    forward(raw, states, PAD, table, FRONT, lead, PAIRS, 128)
+    scalar.wait()
+    forward(raw, states, PAD, table, FRONT, flags[0], PAIRS, 128)
+
+
+def early_kernel(pairing, slab, angles, head_in, far_head_in, states, table, head, far_head, raw, flags, sems):
+    @pl.when(lax.axis_index("blk") < EARLY)
+    def _():
+        evolve(pairing, slab, angles, states, table, raw, flags, sems)
+
+
+def later_kernel(pairing, slab, angles, states_in, table_in, states, table, raw, flags, sems):
+    @pl.when(lax.axis_index("blk") >= EARLY)
+    def _():
+        evolve(pairing, slab, angles, states, table, raw, flags, sems)
+
+
+def inner_kernel(
+    pairing, offsets, weights, states_in, table, evolved, states, adjoint, gradient, turned, products, out, sems, *scalars
+):
+    pairing, offsets, weights = fetched((pairing, offsets, weights), scalars)
+    lead = pairing[0]
 
     def weave(i, carry):
         at = pl.multiple_of(i * 128, 128)
@@ -151,15 +185,15 @@
     stores = []
     for half in range(2):
         stores.append(
-            pltpu.make_async_copy(out.at[half, pl.ds(FRONT, ROWS), :], evolved.at[:, pl.ds(128 * half, 128)], sems.at[2 + half])
+            pltpu.make_async_copy(out.at[half, pl.ds(FRONT, ROWS), :], evolved.at[:, pl.ds(128 * half, 128)], sems.at[half])
         )
         stores[-1].start()
     blank = jnp.zeros((PAD + 8, 128), jnp.float32)
-    last = states.at[LAYERS - 1]
     for parity in range(2):
         for half in range(2):
-            last[parity, half, pl.ds(0, PAD + 8), :] = blank
-            last[parity, half, pl.ds(PAD + PAIRS - 8, PAD + 8), :] = blank
+            states[LAYERS - 1, parity, half, pl.ds(0, PAD + 8), :] = blank
+            states[LAYERS - 1, parity, half, pl.ds(PAD + PAIRS - 8, PAD + 8), :] = blank
+    last = states.at[LAYERS - 1]
     band(last, PAD - 8, adjoint, FRONT, offsets, weights, PAIRS + 16, 104, (1, -1), False)
     backward(states, PAD + 256, adjoint, FRONT + 8 + 256, turned, products, table, FRONT + 256, lead, 512, 128)
     for tile in range(4):
@@ -224,13 +258,15 @@
 
 def left_kernel(
     pairing, offsets, weights, slab, before, evolved_in, states_in, adjoint_in, table_in, inner,
-    evolved, states, adjoint, table, halo_table, gradient, raw, window, source, turned, products, out, sems,
+    evolved, states, adjoint, table, halo_table, gradient, raw, window, source, turned, products, out, sems, *scalars,
 ):
+    copies = fetching((pairing, offsets, weights), scalars)
     loads = started(((before, 0, 8, NEAR), (slab, 0, 8 + NEAR, 40)), raw, sems)
+    near_tables(0, before, NEAR, table, halo_table)
+    for load in loads + copies:
+        load.wait()
+    pairing, offsets, weights = scalars[:3]
     lead = pairing[0]
-    near_tables(0, before, NEAR, table, halo_table)
-    for load in loads:
-        load.wait()
     forward(raw, window, FRONT, halo_table, 120, lead, WINDOW, 80)
     stores = boundary(0, FRONT + 144, lead, window, states, out, evolved, sems.at[pl.ds(4, 2)])
     blank = jnp.zeros((272, 128), jnp.float32)
@@ -252,17 +288,19 @@
 
 def left_far_kernel(
     pairing, offsets, weights, before, before_far, states, table, halo_table, rest, adjoint_in,
-    adjoint, gradient, raw, window, source, turned, products, sems,
+    adjoint, gradient, raw, window, source, turned, products, sems, *scalars,
 ):
+    copies = fetching((pairing, offsets, weights), scalars)
     loads = started(((before_far, SENT - FAR_ROWS, 8, FAR_ROWS), (before, 0, 8 + FAR_ROWS, 32)), raw, sems)
+    blank = jnp.zeros((272, 128), jnp.float32)
+    for half in range(2):
+        for parity in range(2):
+            source[parity, half, pl.ds(136, 272), :] = blank
+    gradient[:, 128:896] = rest[...]
+    for load in loads + copies:
+        load.wait()
+    pairing, offsets, weights = scalars[:3]
     lead = pairing[0]
-    blank = jnp.zeros((272, 128), jnp.float32)
-    for half in range(2):
-        for parity in range(2):
-            source[parity, half, pl.ds(136, 272), :] = blank
-    gradient[:, 128:1024] = rest[...]
-    for load in loads:
-        load.wait()
     forward(raw, window, FRONT, halo_table, 0, lead, FAR_WINDOW, 136)
     for half in range(2):
         for parity in range(2):
@@ -273,38 +311,63 @@
 
 
 def right_kernel(
-    pairing, offsets, weights, slab, after, after_far, inner, left, evolved_in, states_in, adjoint_in, table_in,
-    evolved, states, adjoint, table, gradient, raw, window, source, turned, products, halo_table, out, sems,
+    pairing, offsets, weights, slab, after, inner, left, evolved_in, states_in, adjoint_in, table_in,
+    evolved, states, adjoint, table, halo_table, gradient, raw, window, source, turned, products, out, sems, *scalars,
 ):
-    loads = started(
-        ((slab, ROWS - 32, 0, 32), (after, 0, 32, NEAR), (after_far, 0, 32 + NEAR, FAR_ROWS)), raw, sems
-    )
+    copies = fetching((pairing, offsets, weights), scalars)
+    loads = started(((slab, ROWS - 32, 0, 32), (after, 0, 32, HEAD)), raw, sems)
+    near_tables(1, after, HEAD, table, halo_table)
+    blank = jnp.zeros((272, 128), jnp.float32)
+    for half in range(2):
+        for parity in range(2):
+            source[parity, half, pl.ds(0, 272), :] = blank
+            source[parity, half, pl.ds(400, 152), :] = blank[:152]
+    gradient[:, 0:512] = left[...]
+    for load in loads + copies:
+        load.wait()
+    pairing, offsets, weights = scalars[:3]
     lead = pairing[0]
-    near_tables(1, after, NEAR, table, halo_table)
-    blank = jnp.zeros((272, 128), jnp.float32)
-    for half in range(2):
-        for parity in range(2):
-            source[parity, half, pl.ds(0, 272), :] = blank
-    gradient[:, 0:512] = left[...]
-    for load in loads:
-        load.wait()
-    forward(raw, window, FRONT, halo_table, 0, lead, FULL_WINDOW, 144)
-    stores = boundary(1, FRONT + 8, lead, window, states, out, evolved, sems.at[pl.ds(6, 2)])
-    for half in range(2):
-        for parity in range(2):
-            source[parity, half, pl.ds(272, 280), :] = window[3, parity, half, pl.ds(FRONT + 8, 280), :]
+    forward(raw, window, FRONT, halo_table, 0, lead, RIGHT_WINDOW, 72)
+    stores = boundary(1, FRONT + 8, lead, window, states, out, evolved, sems.at[pl.ds(4, 2)])
+    for half in range(2):
+        for parity in range(2):
+            source[parity, half, pl.ds(272, 128), :] = window[3, parity, half, pl.ds(FRONT + 8, 128), :]
     band(source, 0, adjoint, FRONT + 752, offsets, weights, 288, 144, (1,), True)
     band(source, 272, adjoint, FRONT + PAIRS, offsets, weights, 16, 16, (-1,), True)
-    backward(states, PAD + 744, adjoint, FRONT + 8 + 744, turned, products, table, FRONT + 744, lead, 288, 144)
+    backward(states, PAD + 744, adjoint, FRONT + 8 + 744, turned, products, table, FRONT + 744, lead, 144, 144)
     lane = lax.broadcasted_iota(jnp.int32, (LAYERS, 128), 1)
     gradient[:, 512:640] = jnp.where(lane < 112, inner[:, 384:512], pltpu.roll(summed(products, lead, 8), 112, 1))
     gradient[:, 640:768] = summed(products, lead, 24)
-    gradient[:, 768:896] = summed(products, lead, 152)
     for store in stores:
         store.wait()
 
 
-SMALL = pl.BlockSpec(memory_space=pltpu.SMEM)
+def right_far_kernel(
+    pairing, offsets, weights, after, after_far, states, table, halo_table, rest, adjoint_in,
+    adjoint, gradient, raw, window, source, turned, products, sems, *scalars,
+):
+    copies = fetching((pairing, offsets, weights), scalars)
+    loads = started(((after, HEAD - 32, 0, 32), (after_far, 0, 32, HALO - HEAD)), raw, sems)
+    blank = jnp.zeros((272, 128), jnp.float32)
+    for half in range(2):
+        for parity in range(2):
+            source[parity, half, pl.ds(0, 272), :] = blank
+    gradient[:, 0:768] = rest[:, 0:768]
+    for load in loads + copies:
+        load.wait()
+    pairing, offsets, weights = scalars[:3]
+    lead = pairing[0]
+    forward(raw, window, FRONT, halo_table, 128, lead, RIGHT_FAR_WINDOW, 152)
+    for half in range(2):
+        for parity in range(2):
+            source[parity, half, pl.ds(272, 144), :] = window[3, parity, half, pl.ds(FRONT + 8, 144), :]
+    band(source, 0, adjoint, FRONT + 880, offsets, weights, 160, 160, (1,), True)
+    backward(states, PAD + 872, adjoint, FRONT + 8 + 872, turned, products, table, FRONT + 872, lead, 160, 160)
+    lane = lax.broadcasted_iota(jnp.int32, (LAYERS, 128), 1)
+    gradient[:, 768:896] = jnp.where(lane < 112, rest[:, 768:896], pltpu.roll(summed(products, lead, 8), 112, 1))
+    gradient[:, 896:1024] = summed(products, lead, 24)
+
+
 WHOLE = pl.BlockSpec(memory_space=pltpu.VMEM)
 FAR = pl.BlockSpec(memory_space=pl.ANY)
 
@@ -360,29 +423,65 @@
     )(slab, angles, *earlier)
 
 
-def inner_call(pairing, offsets, weights, slab, angles):
+SCALARS = [
+    pltpu.SMEM((LAYERS,), jnp.int32),
+    pltpu.SMEM((BANDS,), jnp.int32),
+    pltpu.SMEM((BANDS,), jnp.float32),
+    pltpu.SemaphoreType.DMA((3,)),
+]
+EVOLVE_ROOM = [room(2, ROWS + 8, 128), pltpu.SMEM((LAYERS,), jnp.int32), pltpu.SemaphoreType.DMA((3,))]
+
+
+def early_call(pairing, slab, angles, head, far_head):
+    return pl.pallas_call(
+        early_kernel,
+        out_shape=(STATES, TABLE) + tuple(jax.ShapeDtypeStruct(x.shape, x.dtype) for x in (head, far_head)),
+        in_specs=[FAR, FAR, WHOLE, FAR, FAR],
+        out_specs=(WHOLE, WHOLE, FAR, FAR),
+        scratch_shapes=EVOLVE_ROOM,
+        input_output_aliases={3: 2, 4: 3},
+        name="early",
+        **limits(12_000_000, 8 * 2**20),
+    )(pairing, slab, angles, head, far_head)
+
+
+def later_call(pairing, slab, angles, states, table):
+    return pl.pallas_call(
+        later_kernel,
+        out_shape=(STATES, TABLE),
+        in_specs=[FAR, FAR, WHOLE, WHOLE, WHOLE],
+        out_specs=(WHOLE, WHOLE),
+        scratch_shapes=EVOLVE_ROOM,
+        input_output_aliases={3: 0, 4: 1},
+        name="later",
+        **limits(12_000_000, 8 * 2**20),
+    )(pairing, slab, angles, states, table)
+
+
+def inner_call(pairing, offsets, weights, states, table):
     return pl.pallas_call(
         inner_kernel,
-        out_shape=(EVOLVED, STATES, ADJOINT, TABLE, jax.ShapeDtypeStruct((LAYERS, 512), jnp.float32)),
-        in_specs=[SMALL, SMALL, SMALL, FAR, WHOLE],
-        out_specs=(FAR, WHOLE, WHOLE, WHOLE, WHOLE),
+        out_shape=(EVOLVED, STATES, ADJOINT, jax.ShapeDtypeStruct((LAYERS, 512), jnp.float32)),
+        in_specs=[FAR, FAR, FAR, WHOLE, WHOLE],
+        out_specs=(FAR, WHOLE, WHOLE, WHOLE),
         scratch_shapes=[
-            room(2, ROWS + 8, 128),
             room(LAYERS - 1, 2, 2, 512 + 16, 128),
             room(LAYERS, 512 + 16, 128),
             room(2, ROWS + 16, 128),
-            pltpu.SemaphoreType.DMA((4,)),
+            pltpu.SemaphoreType.DMA((2,)),
+            *SCALARS,
         ],
+        input_output_aliases={3: 1},
         name="inner",
-        **limits(60_000_000, 24 * 2**20),
-    )(pairing, offsets, weights, slab, angles)
+        **limits(50_000_000, 16 * 2**20),
+    )(pairing, offsets, weights, states, table)
 
 
 def left_call(pairing, offsets, weights, slab, before, evolved, states, adjoint, table, inner):
     return pl.pallas_call(
         left_kernel,
         out_shape=(EVOLVED, STATES, ADJOINT, TABLE, HALO_TABLE, jax.ShapeDtypeStruct((LAYERS, 512), jnp.float32)),
-        in_specs=[SMALL, SMALL, SMALL, FAR, WHOLE, FAR, WHOLE, WHOLE, WHOLE, WHOLE],
+        in_specs=[FAR, FAR, FAR, FAR, WHOLE, FAR, WHOLE, WHOLE, WHOLE, WHOLE],
         out_specs=(FAR, WHOLE, WHOLE, WHOLE, WHOLE, WHOLE),
         scratch_shapes=[
             room(2, 328, 128),
@@ -392,6 +491,7 @@
             room(LAYERS, 280, 128),
             room(2, 40, 128),
             pltpu.SemaphoreType.DMA((6,)),
+            *SCALARS,
         ],
         input_output_aliases={5: 0, 6: 1, 7: 2, 8: 3},
         name="left",
@@ -402,8 +502,8 @@
 def left_far_call(pairing, offsets, weights, before, before_far, states, table, halo_table, rest, adjoint):
     return pl.pallas_call(
         left_far_kernel,
-        out_shape=(ADJOINT, jax.ShapeDtypeStruct((LAYERS, PAIRS), jnp.float32)),
-        in_specs=[SMALL, SMALL, SMALL] + [WHOLE] * 7,
+        out_shape=(ADJOINT, jax.ShapeDtypeStruct((LAYERS, 896), jnp.float32)),
+        in_specs=[FAR, FAR, FAR] + [WHOLE] * 7,
         out_specs=(WHOLE, WHOLE),
         scratch_shapes=[
             room(2, 280, 128),
@@ -412,6 +512,7 @@
             room(LAYERS - 1, 2, 2, 144 + 16, 128),
             room(LAYERS, 160, 128),
             pltpu.SemaphoreType.DMA((4,)),
+            *SCALARS,
         ],
         input_output_aliases={9: 0},
         name="left_far",
@@ -422,22 +523,43 @@
 def right_call(*operands):
     return pl.pallas_call(
         right_kernel,
-        out_shape=(EVOLVED, STATES, ADJOINT, TABLE, jax.ShapeDtypeStruct((LAYERS, 896), jnp.float32)),
-        in_specs=[SMALL, SMALL, SMALL, FAR] + [WHOLE] * 4 + [FAR, WHOLE, WHOLE, WHOLE],
-        out_specs=(FAR, WHOLE, WHOLE, WHOLE, WHOLE),
+        out_shape=(EVOLVED, STATES, ADJOINT, TABLE, HALO_TABLE, jax.ShapeDtypeStruct((LAYERS, 768), jnp.float32)),
+        in_specs=[FAR, FAR, FAR, FAR] + [WHOLE] * 3 + [FAR, WHOLE, WHOLE, WHOLE],
+        out_specs=(FAR, WHOLE, WHOLE, WHOLE, WHOLE, WHOLE),
         scratch_shapes=[
-            room(2, 2 * FULL_WINDOW + 8, 128),
-            room(LAYERS, 2, 2, FULL_WINDOW + 16, 128),
+            room(2, 2 * RIGHT_WINDOW + 8, 128),
+            room(LAYERS, 2, 2, RIGHT_WINDOW + 16, 128),
             room(2, 2, 560, 128),
-            room(LAYERS - 1, 2, 2, 288 + 16, 128),
-            room(LAYERS, 304, 128),
-            room(2 * LAYERS, 304, 128),
+            room(LAYERS - 1, 2, 2, 144 + 16, 128),
+            room(LAYERS, 168, 128),
             room(2, 40, 128),
-            pltpu.SemaphoreType.DMA((8,)),
+            pltpu.SemaphoreType.DMA((6,)),
+            *SCALARS,
         ],
-        input_output_aliases={8: 0, 9: 1, 10: 2, 11: 3},
+        input_output_aliases={7: 0, 8: 1, 9: 2, 10: 3},
         name="right",
-        **limits(20_000_000, 8 * 2**20),
+        **limits(15_000_000, 8 * 2**20),
+    )(*operands)
+
+
+def right_far_call(*operands):
+    return pl.pallas_call(
+        right_far_kernel,
+        out_shape=(ADJOINT, jax.ShapeDtypeStruct((LAYERS, PAIRS), jnp.float32)),
+        in_specs=[FAR, FAR, FAR] + [WHOLE] * 7,
+        out_specs=(WHOLE, WHOLE),
+        scratch_shapes=[
+            room(2, 2 * RIGHT_FAR_WINDOW + 8, 128),
+            room(LAYERS, 2, 2, RIGHT_FAR_WINDOW + 16, 128),
+            room(2, 2, 440, 128),
+            room(LAYERS - 1, 2, 2, 160 + 16, 128),
+            room(LAYERS, 176, 128),
+            pltpu.SemaphoreType.DMA((4,)),
+            *SCALARS,
+        ],
+        input_output_aliases={9: 0},
+        name="right_far",
+        **limits(10_000_000, 8 * 2**20),
     )(*operands)
 
 
@@ -446,21 +568,24 @@
     onward = [(i, (i + 1) % count) for i in range(count)]
     back = [((i + 1) % count, i) for i in range(count)]
     tail, far_tail, head, far_head, angles_near = pack_call(
-        slab, angles, ((ROWS - NEAR, NEAR, 512), (ROWS - NEAR - SENT, SENT, None), (0, NEAR, 0), (NEAR, SENT, None))
+        slab, angles, ((ROWS - NEAR, NEAR, 512), (ROWS - NEAR - SENT, SENT, None), (0, HEAD, 0), (HEAD, HALO - HEAD, None))
     )
     before = lax.ppermute(tail, "blk", onward)
     before_far = lax.ppermute(far_tail, "blk", onward)
+    scalars = [pltpu.with_memory_space_constraint(x, pltpu.HBM) for x in (pairing, band_offsets, band_weights)]
+    states, table, head, far_head = early_call(scalars[0], slab, angles_near, head, far_head)
     after = lax.ppermute(head, "blk", back)
     after_far = lax.ppermute(far_head, "blk", back)
-    scalars = [pltpu.with_memory_space_constraint(x, pltpu.HBM) for x in (pairing, band_offsets, band_weights)]
-    evolved, states, adjoint, table, inner = inner_call(*scalars, slab, angles_near)
+    states, table = later_call(scalars[0], slab, angles_near, states, table)
+    evolved, states, adjoint, inner = inner_call(*scalars, states, table)
     evolved, states, adjoint, table, left_table, left = left_call(
         *scalars, slab, before, evolved, states, adjoint, table, inner
     )
-    evolved, states, adjoint, table, rest = right_call(
-        *scalars, slab, after, after_far, inner, left, evolved, states, adjoint, table
+    evolved, states, adjoint, table, right_table, rest = right_call(
+        *scalars, slab, after, inner, left, evolved, states, adjoint, table
     )
-    _, gradient = left_far_call(*scalars, before, before_far, states, table, left_table, rest, adjoint)
+    adjoint, rest = left_far_call(*scalars, before, before_far, states, table, left_table, rest, adjoint)
+    _, gradient = right_far_call(*scalars, after, after_far, states, table, right_table, rest, adjoint)
     columns = lax.axis_size("col")
     step = 1
     while step < columns:

time: 36.3 us -> 34.8 us (0.959)
  starting transfers between devices: 15.5 us -> 12.5 us
  waiting for transfers between devices: 2.32 us -> 3.9 us
    ppermute x1, starting transfers between devices: 7.66 us -> 4.15 us  [on_device(): after = lax.ppermute(head, 'blk', back)]
    pallas_call x1 -> x4, Pallas kernels: 8.17 us -> 9.86 us  [the longest x1 5.31 us: inner_call(): pl.pallas_call(inner_kernel, out_shape=(EVOLVED, STATES, ADJOINT, jax.Sha...]
    ppermute x1, waiting for transfers between devices: 0.01 us -> 1.58 us  [on_device(): before_far = lax.ppermute(far_tail, 'blk', onward)]
    ppermute x1, starting transfers between devices: 0.09 us -> 1.21 us  [on_device(): before_far = lax.ppermute(far_tail, 'blk', onward)]
    pallas_call x1, Pallas kernels: 3.08 us -> 1.98 us  [right_call(): pl.pallas_call(right_kernel, out_shape=(EVOLVED, STATES, ADJOINT, TABLE,...]
    pallas_call x1, Pallas kernels: 2.58 us -> 2.08 us  [left_call(): pl.pallas_call(left_kernel, out_shape=(EVOLVED, STATES, ADJOINT, TABLE, H...]
  transfers between devices with their start and end apart: 6 -> 6, of which waited for: 2 -> 3; matrix products, arithmetic and copies ran while one was open for 0% -> 0% of each run, Pallas kernels for 38% -> 39%
where the time goes in v3:
time: 34.8 us; the launch traced here: 34.7 us
  Pallas kernels  16.9 us (49%)
  starting transfers between devices  12.5 us (36%)
  waiting for transfers between devices  3.9 us (11%)
  between operations  0.73 us (2%)
  other arithmetic  0.62 us (2%)
    pallas_call x1, Pallas kernels, inner_call(): pl.pallas_call(inner_kernel, out_shape=(EVOLVED, STATES, ADJOINT, jax.Sha...  5.31 us
    ppermute x1, starting transfers between devices, on_device(): after = lax.ppermute(head, 'blk', back)  4.15 us
    ppermute x2, starting transfers between devices, on_device(): lax.ppermute(gradient, 'col', [(i, i ^ step) for i in range(columns)])  3.94 us
    pallas_call x1, Pallas kernels, early_call(): pl.pallas_call(early_kernel, out_shape=(STATES, TABLE) + tuple((jax.Shape...  2.74 us
    ppermute x2, waiting for transfers between devices, on_device(): lax.ppermute(gradient, 'col', [(i, i ^ step) for i in range(columns)])  2.31 us
    ppermute x1, starting transfers between devices, on_device(): before = lax.ppermute(tail, 'blk', onward)  2.12 us
    pallas_call x1, Pallas kernels, left_call(): pl.pallas_call(left_kernel, out_shape=(EVOLVED, STATES, ADJOINT, TABLE, H...  2.08 us
    pallas_call x1, Pallas kernels, right_call(): pl.pallas_call(right_kernel, out_shape=(EVOLVED, STATES, ADJOINT, TABLE,...  1.98 us
  transfers between devices with their start and end apart: 6, of which 3 were waited for; matrix products, arithmetic and copies ran while one was open for 0% of the time, Pallas kernels for 39%

profile of v3, /device:TPU:1, one launch (start us, length us, event | category | flops | bytes accessed | tf_op | source)
XLA Modules:
  0.0 34.7 jit_solution(5253147289314722472)
XLA Ops:
  0.6 0.0 copy-start
  0.6 1.4 %pack.1 = (f32[288,256]{1,0:T(8,128)S(1)}, f32[272,256]{1,0:T(8,128)S(1)}, f32[264,256]{1,0:T(8,128)S(1)}, f32[264,256]{1,0:T(8,128)S(1)}, f32[4,1024]{1,0:T(4,128)S(1)}) custom-call(f32[2048,256]{1,0:T(8,128)} %slab.9, f32[4,1024]{1,0:T(4,128)} %angles.1), custom_call_target="tpu_custom_call" | custom-call | flops 1000 | bytes 1048576 | tf_op jit(solution)/shard_map/pack/pallas_call | solution.py:415
  2.1 2.1 %collective-permute-start.1 = (f32[288,256]{1,0:T(8,128)S(1)}, f32[288,256]{1,0:T(8,128)S(1)}, u32[]{:S(2)}, u32[]{:S(2)}) collective-permute-start(f32[288,256]{1,0:T(8,128)S(1)} %get-tuple-element.41), channel_id=1, source_target_pairs={{0,4},{4,8},{8,12},{12,16},{16,20},{20,24},{24,28},{28,32},{32,36}... | collective-permute-start | bytes 884744 | tf_op jit(solution)/shard_map/ppermute | solution.py:573
  4.2 1.2 %collective-permute-start.3 = (f32[272,256]{1,0:T(8,128)S(1)}, f32[272,256]{1,0:T(8,128)S(1)}, u32[]{:S(2)}, u32[]{:S(2)}) collective-permute-start(f32[272,256]{1,0:T(8,128)S(1)} %get-tuple-element.55), channel_id=1, source_target_pairs={{0,4},{4,8},{8,12},{12,16},{16,20},{20,24},{24,28},{28,32},{32,36}... | collective-permute-start | bytes 835592 | tf_op jit(solution)/shard_map/ppermute | solution.py:574
  5.4 0.0 copy-done
  5.4 2.7 %early.1 = (f32[4,2,2,1568,128]{4,3,2,1,0:T(8,128)S(1)}, f32[8,1056,128]{2,1,0:T(8,128)S(1)}, f32[264,256]{1,0:T(8,128)S(1)}, f32[264,256]{1,0:T(8,128)S(1)}) custom-call(s32[4]{0:T(128)} %pairing.13, f32[2048,256]{1,0:T(8,128)S(1)} %copy-done, f32[4,1024]{1,0:T(4,128)S(1)} %get-tuple-element.32.angles, ...), custom_call_target="tpu_custom_call", output_to_operand_aliasing={{2}: (3, {}), {3}: (4, {})} | custom-call | flops 12000000 | bytes 8388608 | tf_op jit(solution)/shard_map/early/pallas_call | solution.py:436
  8.1 4.1 %collective-permute-start = (f32[264,256]{1,0:T(8,128)S(1)}, f32[264,256]{1,0:T(8,128)S(1)}, u32[]{:S(2)}, u32[]{:S(2)}) collective-permute-start(f32[264,256]{1,0:T(8,128)S(1)} %get-tuple-element.35), channel_id=1, source_target_pairs={{4,0},{8,4},{12,8},{16,12},{20,16},{24,20},{28,24},{32,28},{36,32}... | collective-permute-start | bytes 811016 | tf_op jit(solution)/shard_map/ppermute | solution.py:577
  12.3 1.1 %collective-permute-start.2 = (f32[264,256]{1,0:T(8,128)S(1)}, f32[264,256]{1,0:T(8,128)S(1)}, u32[]{:S(2)}, u32[]{:S(2)}) collective-permute-start(f32[264,256]{1,0:T(8,128)S(1)} %get-tuple-element.51), channel_id=1, source_target_pairs={{4,0},{8,4},{12,8},{16,12},{20,16},{24,20},{28,24},{32,28},{36,32}... | collective-permute-start | bytes 811016 | tf_op jit(solution)/shard_map/ppermute | solution.py:578
  13.5 5.3 %inner.1 = (f32[2048,256]{1,0:T(8,128)}, f32[4,2,2,1568,128]{4,3,2,1,0:T(8,128)S(1)}, f32[2,2,1056,128]{3,2,1,0:T(8,128)S(1)}, f32[4,512]{1,0:T(4,128)S(1)}) custom-call(s32[4]{0:T(128)} %pairing.13, s32[8]{0:T(128)} %offsets.9, f32[8]{0:T(128)} %weights.9, f32[4,2,2,1568,128]{4,3,2,1,0:T(8,128)S(1)} %get-tuple-element.38.states_in, ...), custom_call_target="tpu_custom_call", output_to_operand_aliasing={{1}: (3, {})} | custom-call | flops 50000000 | bytes 16777216 | tf_op jit(solution)/shard_map/inner/pallas_call | solution.py:462
  18.8 0.0 collective-permute-done.1.before
  18.8 2.1 %left.1 = (f32[2048,256]{1,0:T(8,128)}, f32[4,2,2,1568,128]{4,3,2,1,0:T(8,128)S(1)}, f32[2,2,1056,128]{3,2,1,0:T(8,128)S(1)}, f32[8,1056,128]{2,1,0:T(8,128)S(1)...) custom-call(s32[4]{0:T(128)} %pairing.13, ...), custom_call_target="tpu_custom_call", output_to_operand_aliasing={{0}: (5, {}), {1}: (6, {}), {2}: (7, {}), {3}: (8, {})} | custom-call | flops 15000000 | bytes 8388608 | tf_op jit(solution)/shard_map/left/pallas_call | solution.py:481
  20.9 0.0 collective-permute-done.after
  20.9 2.0 %right.1 = (f32[2048,256]{1,0:T(8,128)}, f32[4,2,2,1568,128]{4,3,2,1,0:T(8,128)S(1)}, f32[2,2,1056,128]{3,2,1,0:T(8,128)S(1)}, f32[8,1056,128]{2,1,0:T(8,128)S(1...) custom-call(s32[4]{0:T(128)} %pairing.13, ...), custom_call_target="tpu_custom_call", output_to_operand_aliasing={{0}: (7, {}), {1}: (8, {}), {2}: (9, {}), {3}: (10, {})} | custom-call | flops 15000000 | bytes 8388608 | tf_op jit(solution)/shard_map/right/pallas_call | solution.py:524
  22.9 1.6 %collective-permute-done.3.before_far = f32[272,256]{1,0:T(8,128)S(1)} collective-permute-done((f32[272,256]{1,0:T(8,128)S(1)}, f32[272,256]{1,0:T(8,128)S(1)}, u32[]{:S(2)}, u32[]{:S(2)}) %collective-permute-start.3) | collective-permute-done | bytes 278560 | tf_op jit(solution)/shard_map/ppermute | solution.py:574
  24.5 1.5 %left_far.1 = (f32[2,2,1056,128]{3,2,1,0:T(8,128)S(1)}, f32[4,896]{1,0:T(4,128)S(1)}) custom-call(s32[4]{0:T(128)} %pairing.13, s32[8]{0:T(128)} %offsets.9, f32[8]{0:T(128)} %weights.9, f32[288,256]{1,0:T(8,128)S(1)} %collective-permute-done.1.before, f32[272,256]{1,0:T(8,128)S(1)} %collective-permute-done.3.before_far, ...), custom_call_target="tpu_custom_call", output_to_operand_aliasing={{0}: (9, {})} | custom-call | flops 10000000 | bytes 8388608 | tf_op jit(solution)/shard_map/left_far/pallas_call | solution.py:503
  26.0 0.0 collective-permute-done.2.after_far
  26.0 1.8 %right_far.1 = (f32[2,2,1056,128]{3,2,1,0:T(8,128)S(1)}, f32[4,1024]{1,0:T(4,128)S(1)}) custom-call(s32[4]{0:T(128)} %pairing.13, s32[8]{0:T(128)} %offsets.9, f32[8]{0:T(128)} %weights.9, f32[264,256]{1,0:T(8,128)S(1)} %collective-permute-done.after, f32[264,256]{1,0:T(8,128)S(1)} %collective-permute-done.2.after_far, ...), custom_call_target="tpu_custom_call", output_to_operand_aliasing={{0}: (9, {})} | custom-call | flops 10000000 | bytes 8388608 | tf_op jit(solution)/shard_map/right_far/pallas_call | solution.py:546
  27.8 1.3 %collective-permute-start.4 = (f32[4,1024]{1,0:T(4,128)S(1)}, f32[4,1024]{1,0:T(4,128)S(1)}, u32[]{:S(2)}, u32[]{:S(2)}) collective-permute-start(f32[4,1024]{1,0:T(4,128)S(1)} %get-tuple-element.61), channel_id=1, source_target_pairs={{0,1},{1,0},{2,3},{3,2},{4,5},{5,4},{6,7},{7,6},{8,9},{9,8},{10,11... | collective-permute-start | bytes 49160 | tf_op jit(solution)/shard_map/ppermute | solution.py:592
  29.1 0.8 %collective-permute-done.4 = f32[4,1024]{1,0:T(4,128)S(1)} collective-permute-done((f32[4,1024]{1,0:T(4,128)S(1)}, f32[4,1024]{1,0:T(4,128)S(1)}, u32[]{:S(2)}, u32[]{:S(2)}) %collective-permute-start.4) | collective-permute-done | bytes 16416 | tf_op jit(solution)/shard_map/ppermute | solution.py:592
  30.0 2.6 %collective-permute-start.5 = (f32[4,1024]{1,0:T(4,128)S(1)}, f32[4,1024]{1,0:T(4,128)S(1)}, u32[]{:S(2)}, u32[]{:S(2)}) collective-permute-start(f32[4,1024]{1,0:T(4,128)S(1)} %add.6), channel_id=1, source_target_pairs={{0,2},{1,3},{2,0},{3,1},{4,6},{5,7},{6,4},{7,5},{8,10},{9,11},{10,... | collective-permute-start | bytes 49160 | tf_op jit(solution)/shard_map/ppermute | solution.py:592
  32.6 1.5 %collective-permute-done.5 = f32[4,1024]{1,0:T(4,128)S(1)} collective-permute-done((f32[4,1024]{1,0:T(4,128)S(1)}, f32[4,1024]{1,0:T(4,128)S(1)}, u32[]{:S(2)}, u32[]{:S(2)}) %collective-permute-start.5) | collective-permute-done | bytes 16416 | tf_op jit(solution)/shard_map/ppermute | solution.py:592
  34.1 0.6 %add.7 = f32[4,1024]{1,0:T(4,128)} add(f32[4,1024]{1,0:T(4,128)S(1)} %add.6, f32[4,1024]{1,0:T(4,128)S(1)} %collective-permute-done.5) | non-fusion elementwise | flops 4096 | bytes 49152 | tf_op jit(solution)/shard_map/add | solution.py:592
  (2 shorter events, 0.0 us)
Async XLA Ops:
  0.6 4.8 %copy-start = (f32[2048,256]{1,0:T(8,128)S(1)}, f32[2048,256]{1,0:T(8,128)}, u32[]{:S(2)}) copy-start(f32[2048,256]{1,0:T(8,128)} %slab.9) | copy-start | bytes 6291460
  2.1 16.7 %collective-permute-start.1 = (f32[288,256]{1,0:T(8,128)S(1)}, f32[288,256]{1,0:T(8,128)S(1)}, u32[]{:S(2)}, u32[]{:S(2)}) collective-permute-start(f32[288,256]{1,0:T(8,128)S(1)} %get-tuple-element.41), channel_id=1, source_target_pairs={{0,4},{4,8},{8,12},{12,16},{16,20},{20,24},{24,28},{28,32},{32,36}... | collective-permute-start | bytes 884744 | tf_op jit(solution)/shard_map/ppermute | solution.py:573
  4.2 20.3 %collective-permute-start.3 = (f32[272,256]{1,0:T(8,128)S(1)}, f32[272,256]{1,0:T(8,128)S(1)}, u32[]{:S(2)}, u32[]{:S(2)}) collective-permute-start(f32[272,256]{1,0:T(8,128)S(1)} %get-tuple-element.55), channel_id=1, source_target_pairs={{0,4},{4,8},{8,12},{12,16},{16,20},{20,24},{24,28},{28,32},{32,36}... | collective-permute-start | bytes 835592 | tf_op jit(solution)/shard_map/ppermute | solution.py:574
  8.1 12.7 %collective-permute-start = (f32[264,256]{1,0:T(8,128)S(1)}, f32[264,256]{1,0:T(8,128)S(1)}, u32[]{:S(2)}, u32[]{:S(2)}) collective-permute-start(f32[264,256]{1,0:T(8,128)S(1)} %get-tuple-element.35), channel_id=1, source_target_pairs={{4,0},{8,4},{12,8},{16,12},{20,16},{24,20},{28,24},{32,28},{36,32}... | collective-permute-start | bytes 811016 | tf_op jit(solution)/shard_map/ppermute | solution.py:577
  12.3 13.7 %collective-permute-start.2 = (f32[264,256]{1,0:T(8,128)S(1)}, f32[264,256]{1,0:T(8,128)S(1)}, u32[]{:S(2)}, u32[]{:S(2)}) collective-permute-start(f32[264,256]{1,0:T(8,128)S(1)} %get-tuple-element.51), channel_id=1, source_target_pairs={{4,0},{8,4},{12,8},{16,12},{20,16},{24,20},{28,24},{32,28},{36,32}... | collective-permute-start | bytes 811016 | tf_op jit(solution)/shard_map/ppermute | solution.py:578
  27.8 2.2 %collective-permute-start.4 = (f32[4,1024]{1,0:T(4,128)S(1)}, f32[4,1024]{1,0:T(4,128)S(1)}, u32[]{:S(2)}, u32[]{:S(2)}) collective-permute-start(f32[4,1024]{1,0:T(4,128)S(1)} %get-tuple-element.61), channel_id=1, source_target_pairs={{0,1},{1,0},{2,3},{3,2},{4,5},{5,4},{6,7},{7,6},{8,9},{9,8},{10,11... | collective-permute-start | bytes 49160 | tf_op jit(solution)/shard_map/ppermute | solution.py:592
  30.0 4.1 %collective-permute-start.5 = (f32[4,1024]{1,0:T(4,128)S(1)}, f32[4,1024]{1,0:T(4,128)S(1)}, u32[]{:S(2)}, u32[]{:S(2)}) collective-permute-start(f32[4,1024]{1,0:T(4,128)S(1)} %add.6), channel_id=1, source_target_pairs={{0,2},{1,3},{2,0},{3,1},{4,6},{5,7},{6,4},{7,5},{8,10},{9,11},{10,... | collective-permute-start | bytes 49160 | tf_op jit(solution)/shard_map/ppermute | solution.py:592

commit v4 on v3

--- a/solution.py
+++ b/solution.py
@@ -206,6 +206,12 @@
     return halo[at + 4 * (tile // 2) : at + 4 * (tile // 2) + 4, 128 * (tile % 2) : 128 * (tile % 2) + 128]
 
 
+def placed(pieces, raw):
+    for piece, piece_at, at, rows in pieces:
+        for half in range(2):
+            raw[half, pl.ds(at, rows), :] = piece[pl.ds(piece_at, rows), 128 * half : 128 * half + 128]
+
+
 def started(pieces, raw, sems):
     loads = []
     for half in range(2):
@@ -261,7 +267,8 @@
     evolved, states, adjoint, table, halo_table, gradient, raw, window, source, turned, products, out, sems, *scalars,
 ):
     copies = fetching((pairing, offsets, weights), scalars)
-    loads = started(((before, 0, 8, NEAR), (slab, 0, 8 + NEAR, 40)), raw, sems)
+    loads = started(((slab, 0, 8 + NEAR, 40),), raw, sems)
+    placed(((before, 0, 8, NEAR),), raw)
     near_tables(0, before, NEAR, table, halo_table)
     for load in loads + copies:
         load.wait()
@@ -288,16 +295,16 @@
 
 def left_far_kernel(
     pairing, offsets, weights, before, before_far, states, table, halo_table, rest, adjoint_in,
-    adjoint, gradient, raw, window, source, turned, products, sems, *scalars,
+    adjoint, gradient, raw, window, source, turned, products, *scalars,
 ):
     copies = fetching((pairing, offsets, weights), scalars)
-    loads = started(((before_far, SENT - FAR_ROWS, 8, FAR_ROWS), (before, 0, 8 + FAR_ROWS, 32)), raw, sems)
+    placed(((before_far, SENT - FAR_ROWS, 8, FAR_ROWS), (before, 0, 8 + FAR_ROWS, 32)), raw)
     blank = jnp.zeros((272, 128), jnp.float32)
     for half in range(2):
         for parity in range(2):
             source[parity, half, pl.ds(136, 272), :] = blank
     gradient[:, 128:896] = rest[...]
-    for load in loads + copies:
+    for load in copies:
         load.wait()
     pairing, offsets, weights = scalars[:3]
     lead = pairing[0]
@@ -315,7 +322,8 @@
     evolved, states, adjoint, table, halo_table, gradient, raw, window, source, turned, products, out, sems, *scalars,
 ):
     copies = fetching((pairing, offsets, weights), scalars)
-    loads = started(((slab, ROWS - 32, 0, 32), (after, 0, 32, HEAD)), raw, sems)
+    loads = started(((slab, ROWS - 32, 0, 32),), raw, sems)
+    placed(((after, 0, 32, HEAD),), raw)
     near_tables(1, after, HEAD, table, halo_table)
     blank = jnp.zeros((272, 128), jnp.float32)
     for half in range(2):
@@ -344,16 +352,16 @@
 
 def right_far_kernel(
     pairing, offsets, weights, after, after_far, states, table, halo_table, rest, adjoint_in,
-    adjoint, gradient, raw, window, source, turned, products, sems, *scalars,
+    adjoint, gradient, raw, window, source, turned, products, *scalars,
 ):
     copies = fetching((pairing, offsets, weights), scalars)
-    loads = started(((after, HEAD - 32, 0, 32), (after_far, 0, 32, HALO - HEAD)), raw, sems)
+    placed(((after, HEAD - 32, 0, 32), (after_far, 0, 32, HALO - HEAD)), raw)
     blank = jnp.zeros((272, 128), jnp.float32)
     for half in range(2):
         for parity in range(2):
             source[parity, half, pl.ds(0, 272), :] = blank
     gradient[:, 0:768] = rest[:, 0:768]
-    for load in loads + copies:
+    for load in copies:
         load.wait()
     pairing, offsets, weights = scalars[:3]
     lead = pairing[0]
@@ -389,12 +397,16 @@
     return pltpu.VMEM(shape, jnp.float32)
 
 
-def pack_call(slab, angles, pieces, *earlier):
+def pack_call(slab, angles, pieces, *scalars):
     shapes = [(rows + (0 if lane is None else 8), 256) for _, rows, lane in pieces]
 
     def kernel(slab, angles, *refs):
-        packed, tiles, sems = refs[len(earlier) : len(earlier) + len(pieces)], refs[-2], refs[-1]
+        count = len(scalars)
+        sources, packed, kept = refs[:count], refs[count : count + len(pieces)], refs[count + len(pieces) : -2]
+        tiles, sems = refs[-2], refs[-1]
         copies = [pltpu.make_async_copy(angles, tiles, sems.at[len(pieces)])]
+        for n, source in enumerate(sources):
+            copies.append(pltpu.make_async_copy(source, kept[n], sems.at[len(pieces) + 1 + n]))
         for n, (first, rows, _) in enumerate(pieces):
             copies.append(
                 pltpu.make_async_copy(slab.at[pl.ds(first, rows), :], packed[n].at[pl.ds(0, rows), :], sems.at[n])
@@ -414,13 +426,14 @@
     angles = pltpu.with_memory_space_constraint(angles, pltpu.HBM)
     return pl.pallas_call(
         kernel,
-        out_shape=[jax.ShapeDtypeStruct(shape, jnp.float32) for shape in [*shapes, (LAYERS, PAIRS)]],
-        in_specs=[pl.BlockSpec(memory_space=pltpu.HBM)] * 2 + [FAR] * len(earlier),
-        out_specs=[WHOLE] * (len(pieces) + 1),
-        scratch_shapes=[pltpu.SemaphoreType.DMA((len(pieces) + 1,))],
+        out_shape=[jax.ShapeDtypeStruct(shape, jnp.float32) for shape in shapes]
+        + [jax.ShapeDtypeStruct(x.shape, x.dtype) for x in (*scalars, angles)],
+        in_specs=[pl.BlockSpec(memory_space=pltpu.HBM)] * (2 + len(scalars)),
+        out_specs=[WHOLE] * (len(pieces) + len(scalars) + 1),
+        scratch_shapes=[pltpu.SemaphoreType.DMA((len(pieces) + len(scalars) + 1,))],
         name="pack",
         **limits(1000, 2**20),
-    )(slab, angles, *earlier)
+    )(slab, angles, *scalars)
 
 
 SCALARS = [
@@ -436,7 +449,7 @@
     return pl.pallas_call(
         early_kernel,
         out_shape=(STATES, TABLE) + tuple(jax.ShapeDtypeStruct(x.shape, x.dtype) for x in (head, far_head)),
-        in_specs=[FAR, FAR, WHOLE, FAR, FAR],
+        in_specs=[WHOLE, FAR, WHOLE, FAR, FAR],
         out_specs=(WHOLE, WHOLE, FAR, FAR),
         scratch_shapes=EVOLVE_ROOM,
         input_output_aliases={3: 2, 4: 3},
@@ -449,7 +462,7 @@
     return pl.pallas_call(
         later_kernel,
         out_shape=(STATES, TABLE),
-        in_specs=[FAR, FAR, WHOLE, WHOLE, WHOLE],
+        in_specs=[WHOLE, FAR, WHOLE, WHOLE, WHOLE],
         out_specs=(WHOLE, WHOLE),
         scratch_shapes=EVOLVE_ROOM,
         input_output_aliases={3: 0, 4: 1},
@@ -462,7 +475,7 @@
     return pl.pallas_call(
         inner_kernel,
         out_shape=(EVOLVED, STATES, ADJOINT, jax.ShapeDtypeStruct((LAYERS, 512), jnp.float32)),
-        in_specs=[FAR, FAR, FAR, WHOLE, WHOLE],
+        in_specs=[WHOLE, WHOLE, WHOLE, WHOLE, WHOLE],
         out_specs=(FAR, WHOLE, WHOLE, WHOLE),
         scratch_shapes=[
             room(LAYERS - 1, 2, 2, 512 + 16, 128),
@@ -481,7 +494,7 @@
     return pl.pallas_call(
         left_kernel,
         out_shape=(EVOLVED, STATES, ADJOINT, TABLE, HALO_TABLE, jax.ShapeDtypeStruct((LAYERS, 512), jnp.float32)),
-        in_specs=[FAR, FAR, FAR, FAR, WHOLE, FAR, WHOLE, WHOLE, WHOLE, WHOLE],
+        in_specs=[WHOLE, WHOLE, WHOLE, FAR, WHOLE, FAR, WHOLE, WHOLE, WHOLE, WHOLE],
         out_specs=(FAR, WHOLE, WHOLE, WHOLE, WHOLE, WHOLE),
         scratch_shapes=[
             room(2, 328, 128),
@@ -503,7 +516,7 @@
     return pl.pallas_call(
         left_far_kernel,
         out_shape=(ADJOINT, jax.ShapeDtypeStruct((LAYERS, 896), jnp.float32)),
-        in_specs=[FAR, FAR, FAR] + [WHOLE] * 7,
+        in_specs=[WHOLE, WHOLE, WHOLE] + [WHOLE] * 7,
         out_specs=(WHOLE, WHOLE),
         scratch_shapes=[
             room(2, 280, 128),
@@ -511,7 +524,6 @@
             room(2, 2, 408, 128),
             room(LAYERS - 1, 2, 2, 144 + 16, 128),
             room(LAYERS, 160, 128),
-            pltpu.SemaphoreType.DMA((4,)),
             *SCALARS,
         ],
         input_output_aliases={9: 0},
@@ -524,7 +536,7 @@
     return pl.pallas_call(
         right_kernel,
         out_shape=(EVOLVED, STATES, ADJOINT, TABLE, HALO_TABLE, jax.ShapeDtypeStruct((LAYERS, 768), jnp.float32)),
-        in_specs=[FAR, FAR, FAR, FAR] + [WHOLE] * 3 + [FAR, WHOLE, WHOLE, WHOLE],
+        in_specs=[WHOLE, WHOLE, WHOLE, FAR] + [WHOLE] * 3 + [FAR, WHOLE, WHOLE, WHOLE],
         out_specs=(FAR, WHOLE, WHOLE, WHOLE, WHOLE, WHOLE),
         scratch_shapes=[
             room(2, 2 * RIGHT_WINDOW + 8, 128),
@@ -546,7 +558,7 @@
     return pl.pallas_call(
         right_far_kernel,
         out_shape=(ADJOINT, jax.ShapeDtypeStruct((LAYERS, PAIRS), jnp.float32)),
-        in_specs=[FAR, FAR, FAR] + [WHOLE] * 7,
+        in_specs=[WHOLE, WHOLE, WHOLE] + [WHOLE] * 7,
         out_specs=(WHOLE, WHOLE),
         scratch_shapes=[
             room(2, 2 * RIGHT_FAR_WINDOW + 8, 128),
@@ -554,7 +566,6 @@
             room(2, 2, 440, 128),
             room(LAYERS - 1, 2, 2, 160 + 16, 128),
             room(LAYERS, 176, 128),
-            pltpu.SemaphoreType.DMA((4,)),
             *SCALARS,
         ],
         input_output_aliases={9: 0},
@@ -567,12 +578,13 @@
     count = lax.axis_size("blk")
     onward = [(i, (i + 1) % count) for i in range(count)]
     back = [((i + 1) % count, i) for i in range(count)]
-    tail, far_tail, head, far_head, angles_near = pack_call(
-        slab, angles, ((ROWS - NEAR, NEAR, 512), (ROWS - NEAR - SENT, SENT, None), (0, HEAD, 0), (HEAD, HALO - HEAD, None))
+    scalars = [pltpu.with_memory_space_constraint(x, pltpu.HBM) for x in (pairing, band_offsets, band_weights)]
+    tail, far_tail, head, far_head, *scalars, angles_near = pack_call(
+        slab, angles, ((ROWS - NEAR, NEAR, 512), (ROWS - NEAR - SENT, SENT, None), (0, HEAD, 0), (HEAD, HALO - HEAD, None)),
+        *scalars,
     )
     before = lax.ppermute(tail, "blk", onward)
     before_far = lax.ppermute(far_tail, "blk", onward)
-    scalars = [pltpu.with_memory_space_constraint(x, pltpu.HBM) for x in (pairing, band_offsets, band_weights)]
     states, table, head, far_head = early_call(scalars[0], slab, angles_near, head, far_head)
     after = lax.ppermute(head, "blk", back)
     after_far = lax.ppermute(far_head, "blk", back)

time: 34.8 us -> 34.6 us (level)
  transfers between devices with their start and end apart: 6 -> 6, of which waited for: 3 -> 3; matrix products, arithmetic and copies ran while one was open for 0% -> 0% of each run, Pallas kernels for 39% -> 40%
where the time goes in v4:
time: 34.6 us; the launch traced here: 34.5 us
  Pallas kernels  16.8 us (49%)
  starting transfers between devices  12.5 us (36%)
  waiting for transfers between devices  3.9 us (11%)
  between operations  0.73 us (2%)
  other arithmetic  0.62 us (2%)
    pallas_call x1, Pallas kernels, inner_call(): pl.pallas_call(inner_kernel, out_shape=(EVOLVED, STATES, ADJOINT, jax.Sha...  5.43 us
    ppermute x1, starting transfers between devices, on_device(): after = lax.ppermute(head, 'blk', back)  4.06 us
    ppermute x2, starting transfers between devices, on_device(): lax.ppermute(gradient, 'col', [(i, i ^ step) for i in range(columns)])  3.94 us
    pallas_call x1, Pallas kernels, early_call(): pl.pallas_call(early_kernel, out_shape=(STATES, TABLE) + tuple((jax.Shape...  2.81 us
    ppermute x2, waiting for transfers between devices, on_device(): lax.ppermute(gradient, 'col', [(i, i ^ step) for i in range(columns)])  2.31 us
    ppermute x1, starting transfers between devices, on_device(): before = lax.ppermute(tail, 'blk', onward)  2.12 us
    pallas_call x1, Pallas kernels, right_call(): pl.pallas_call(right_kernel, out_shape=(EVOLVED, STATES, ADJOINT, TABLE,...  2.01 us
    pallas_call x1, Pallas kernels, left_call(): pl.pallas_call(left_kernel, out_shape=(EVOLVED, STATES, ADJOINT, TABLE, H...  1.94 us
  transfers between devices with their start and end apart: 6, of which 3 were waited for; matrix products, arithmetic and copies ran while one was open for 0% of the time, Pallas kernels for 40%

profile of v4, /device:TPU:1, one launch (start us, length us, event | category | flops | bytes accessed | tf_op | source)
XLA Modules:
  0.0 34.5 jit_solution(26667947571831950)
XLA Ops:
  0.6 0.0 copy-start
  0.6 1.5 %pack.1 = (f32[288,256]{1,0:T(8,128)S(1)}, f32[272,256]{1,0:T(8,128)S(1)}, f32[264,256]{1,0:T(8,128)S(1)}, f32[264,256]{1,0:T(8,128)S(1)}, s32[4]{0:T(128)S(1)},...) custom-call(f32[2048,256]{1,0:T(8,128)} %slab.9, f32[4,1024]{1,0:T(4,128)} %angles.1, s32[4]{0:T(128)} %refs_0_.1, ...), custom_call_target="tpu_custom_call" | custom-call | flops 1000 | bytes 1048576 | tf_op jit(solution)/shard_map/pack/pallas_call | solution.py:427
  2.1 2.1 %collective-permute-start.1 = (f32[288,256]{1,0:T(8,128)S(1)}, f32[288,256]{1,0:T(8,128)S(1)}, u32[]{:S(2)}, u32[]{:S(2)}) collective-permute-start(f32[288,256]{1,0:T(8,128)S(1)} %get-tuple-element.47), channel_id=1, source_target_pairs={{0,4},{4,8},{8,12},{12,16},{16,20},{20,24},{24,28},{28,32},{32,36}... | collective-permute-start | bytes 884744 | tf_op jit(solution)/shard_map/ppermute | solution.py:586
  4.3 1.2 %collective-permute-start.3 = (f32[272,256]{1,0:T(8,128)S(1)}, f32[272,256]{1,0:T(8,128)S(1)}, u32[]{:S(2)}, u32[]{:S(2)}) collective-permute-start(f32[272,256]{1,0:T(8,128)S(1)} %get-tuple-element.61), channel_id=1, source_target_pairs={{0,4},{4,8},{8,12},{12,16},{16,20},{20,24},{24,28},{28,32},{32,36}... | collective-permute-start | bytes 835592 | tf_op jit(solution)/shard_map/ppermute | solution.py:587
  5.5 0.0 copy-done
  5.5 2.8 %early.1 = (f32[4,2,2,1568,128]{4,3,2,1,0:T(8,128)S(1)}, f32[8,1056,128]{2,1,0:T(8,128)S(1)}, f32[264,256]{1,0:T(8,128)S(1)}, f32[264,256]{1,0:T(8,128)S(1)}) custom-call(s32[4]{0:T(128)S(1)} %get-tuple-element.35.pairing, f32[2048,256]{1,0:T(8,128)S(1)} %copy-done, ...), custom_call_target="tpu_custom_call", output_to_operand_aliasing={{2}: (3, {}), {3}: (4, {})} | custom-call | flops 12000000 | bytes 8388608 | tf_op jit(solution)/shard_map/early/pallas_call | solution.py:449
  8.3 4.1 %collective-permute-start = (f32[264,256]{1,0:T(8,128)S(1)}, f32[264,256]{1,0:T(8,128)S(1)}, u32[]{:S(2)}, u32[]{:S(2)}) collective-permute-start(f32[264,256]{1,0:T(8,128)S(1)} %get-tuple-element.41), channel_id=1, source_target_pairs={{4,0},{8,4},{12,8},{16,12},{20,16},{24,20},{28,24},{32,28},{36,32}... | collective-permute-start | bytes 811016 | tf_op jit(solution)/shard_map/ppermute | solution.py:589
  12.3 1.2 %collective-permute-start.2 = (f32[264,256]{1,0:T(8,128)S(1)}, f32[264,256]{1,0:T(8,128)S(1)}, u32[]{:S(2)}, u32[]{:S(2)}) collective-permute-start(f32[264,256]{1,0:T(8,128)S(1)} %get-tuple-element.57), channel_id=1, source_target_pairs={{4,0},{8,4},{12,8},{16,12},{20,16},{24,20},{28,24},{32,28},{36,32}... | collective-permute-start | bytes 811016 | tf_op jit(solution)/shard_map/ppermute | solution.py:590
  13.5 5.4 %inner.1 = (f32[2048,256]{1,0:T(8,128)}, f32[4,2,2,1568,128]{4,3,2,1,0:T(8,128)S(1)}, f32[2,2,1056,128]{3,2,1,0:T(8,128)S(1)}, f32[4,512]{1,0:T(4,128)S(1)}) custom-call(s32[4]{0:T(128)S(1)} %get-tuple-element.35.pairing, s32[8]{0:T(128)S(1)} %get-tuple-element.36.offsets, f32[8]{0:T(128)S(1)} %get-tuple-element.37.weights, ...), custom_call_target="tpu_custom_call", output_to_operand_aliasing={{1}: (3, {})} | custom-call | flops 50000000 | bytes 16777216 | tf_op jit(solution)/shard_map/inner/pallas_call | solution.py:475
  19.0 0.0 collective-permute-done.1.before
  19.0 1.9 %left.1 = (f32[2048,256]{1,0:T(8,128)}, f32[4,2,2,1568,128]{4,3,2,1,0:T(8,128)S(1)}, f32[2,2,1056,128]{3,2,1,0:T(8,128)S(1)}, f32[8,1056,128]{2,1,0:T(8,128)S(1)...) custom-call(s32[4]{0:T(128)S(1)} %get-tuple-element.35.pairing, ...), custom_call_target="tpu_custom_call", output_to_operand_aliasing={{0}: (5, {}), {1}: (6, {}), {2}: (7, {}), {3}: (8, {})} | custom-call | flops 15000000 | bytes 8388608 | tf_op jit(solution)/shard_map/left/pallas_call | solution.py:494
  20.9 0.0 collective-permute-done.after
  20.9 2.0 %right.1 = (f32[2048,256]{1,0:T(8,128)}, f32[4,2,2,1568,128]{4,3,2,1,0:T(8,128)S(1)}, f32[2,2,1056,128]{3,2,1,0:T(8,128)S(1)}, f32[8,1056,128]{2,1,0:T(8,128)S(1...) custom-call(s32[4]{0:T(128)S(1)} %get-tuple-element.35.pairing, ...), custom_call_target="tpu_custom_call", output_to_operand_aliasing={{0}: (7, {}), {1}: (8, {}), {2}: (9, {}), {3}: (10, {})} | custom-call | flops 15000000 | bytes 8388608 | tf_op jit(solution)/shard_map/right/pallas_call | solution.py:536
  23.0 1.6 %collective-permute-done.3.before_far = f32[272,256]{1,0:T(8,128)S(1)} collective-permute-done((f32[272,256]{1,0:T(8,128)S(1)}, f32[272,256]{1,0:T(8,128)S(1)}, u32[]{:S(2)}, u32[]{:S(2)}) %collective-permute-start.3) | collective-permute-done | bytes 278560 | tf_op jit(solution)/shard_map/ppermute | solution.py:587
  24.5 1.4 %left_far.1 = (f32[2,2,1056,128]{3,2,1,0:T(8,128)S(1)}, f32[4,896]{1,0:T(4,128)S(1)}) custom-call(s32[4]{0:T(128)S(1)} %get-tuple-element.35.pairing, s32[8]{0:T(128)S(1)} %get-tuple-element.36.offsets, f32[8]{0:T(128)S(1)} %get-tuple-element.37.weights, f32[288,256]{1,0:T(8,128)S(1)} %collective-permute-done.1.before, ...), custom_call_target="tpu_custom_call", output_to_operand_aliasing={{0}: (9, {})} | custom-call | flops 10000000 | bytes 8388608 | tf_op jit(solution)/shard_map/left_far/pallas_call | solution.py:516
  26.0 0.0 collective-permute-done.2.after_far
  26.0 1.7 %right_far.1 = (f32[2,2,1056,128]{3,2,1,0:T(8,128)S(1)}, f32[4,1024]{1,0:T(4,128)S(1)}) custom-call(s32[4]{0:T(128)S(1)} %get-tuple-element.35.pairing, s32[8]{0:T(128)S(1)} %get-tuple-element.36.offsets, f32[8]{0:T(128)S(1)} %get-tuple-element.37.weights, f32[264,256]{1,0:T(8,128)S(1)} %collective-permute-done.after, ...), custom_call_target="tpu_custom_call", output_to_operand_aliasing={{0}: (9, {})} | custom-call | flops 10000000 | bytes 8388608 | tf_op jit(solution)/shard_map/right_far/pallas_call | solution.py:558
  27.6 1.3 %collective-permute-start.4 = (f32[4,1024]{1,0:T(4,128)S(1)}, f32[4,1024]{1,0:T(4,128)S(1)}, u32[]{:S(2)}, u32[]{:S(2)}) collective-permute-start(f32[4,1024]{1,0:T(4,128)S(1)} %get-tuple-element.67), channel_id=1, source_target_pairs={{0,1},{1,0},{2,3},{3,2},{4,5},{5,4},{6,7},{7,6},{8,9},{9,8},{10,11... | collective-permute-start | bytes 49160 | tf_op jit(solution)/shard_map/ppermute | solution.py:604
  28.9 0.8 %collective-permute-done.4 = f32[4,1024]{1,0:T(4,128)S(1)} collective-permute-done((f32[4,1024]{1,0:T(4,128)S(1)}, f32[4,1024]{1,0:T(4,128)S(1)}, u32[]{:S(2)}, u32[]{:S(2)}) %collective-permute-start.4) | collective-permute-done | bytes 16416 | tf_op jit(solution)/shard_map/ppermute | solution.py:604
  29.8 2.6 %collective-permute-start.5 = (f32[4,1024]{1,0:T(4,128)S(1)}, f32[4,1024]{1,0:T(4,128)S(1)}, u32[]{:S(2)}, u32[]{:S(2)}) collective-permute-start(f32[4,1024]{1,0:T(4,128)S(1)} %add.6), channel_id=1, source_target_pairs={{0,2},{1,3},{2,0},{3,1},{4,6},{5,7},{6,4},{7,5},{8,10},{9,11},{10,... | collective-permute-start | bytes 49160 | tf_op jit(solution)/shard_map/ppermute | solution.py:604
  32.4 1.5 %collective-permute-done.5 = f32[4,1024]{1,0:T(4,128)S(1)} collective-permute-done((f32[4,1024]{1,0:T(4,128)S(1)}, f32[4,1024]{1,0:T(4,128)S(1)}, u32[]{:S(2)}, u32[]{:S(2)}) %collective-permute-start.5) | collective-permute-done | bytes 16416 | tf_op jit(solution)/shard_map/ppermute | solution.py:604
  33.9 0.6 %add.7 = f32[4,1024]{1,0:T(4,128)} add(f32[4,1024]{1,0:T(4,128)S(1)} %add.6, f32[4,1024]{1,0:T(4,128)S(1)} %collective-permute-done.5) | non-fusion elementwise | flops 4096 | bytes 49152 | tf_op jit(solution)/shard_map/add | solution.py:604
  (2 shorter events, 0.0 us)
Async XLA Ops:
  0.6 4.8 %copy-start = (f32[2048,256]{1,0:T(8,128)S(1)}, f32[2048,256]{1,0:T(8,128)}, u32[]{:S(2)}) copy-start(f32[2048,256]{1,0:T(8,128)} %slab.9) | copy-start | bytes 6291460
  2.1 16.8 %collective-permute-start.1 = (f32[288,256]{1,0:T(8,128)S(1)}, f32[288,256]{1,0:T(8,128)S(1)}, u32[]{:S(2)}, u32[]{:S(2)}) collective-permute-start(f32[288,256]{1,0:T(8,128)S(1)} %get-tuple-element.47), channel_id=1, source_target_pairs={{0,4},{4,8},{8,12},{12,16},{16,20},{20,24},{24,28},{28,32},{32,36}... | collective-permute-start | bytes 884744 | tf_op jit(solution)/shard_map/ppermute | solution.py:586
  4.3 20.3 %collective-permute-start.3 = (f32[272,256]{1,0:T(8,128)S(1)}, f32[272,256]{1,0:T(8,128)S(1)}, u32[]{:S(2)}, u32[]{:S(2)}) collective-permute-start(f32[272,256]{1,0:T(8,128)S(1)} %get-tuple-element.61), channel_id=1, source_target_pairs={{0,4},{4,8},{8,12},{12,16},{16,20},{20,24},{24,28},{28,32},{32,36}... | collective-permute-start | bytes 835592 | tf_op jit(solution)/shard_map/ppermute | solution.py:587
  8.3 12.6 %collective-permute-start = (f32[264,256]{1,0:T(8,128)S(1)}, f32[264,256]{1,0:T(8,128)S(1)}, u32[]{:S(2)}, u32[]{:S(2)}) collective-permute-start(f32[264,256]{1,0:T(8,128)S(1)} %get-tuple-element.41), channel_id=1, source_target_pairs={{4,0},{8,4},{12,8},{16,12},{20,16},{24,20},{28,24},{32,28},{36,32}... | collective-permute-start | bytes 811016 | tf_op jit(solution)/shard_map/ppermute | solution.py:589
  12.3 13.6 %collective-permute-start.2 = (f32[264,256]{1,0:T(8,128)S(1)}, f32[264,256]{1,0:T(8,128)S(1)}, u32[]{:S(2)}, u32[]{:S(2)}) collective-permute-start(f32[264,256]{1,0:T(8,128)S(1)} %get-tuple-element.57), channel_id=1, source_target_pairs={{4,0},{8,4},{12,8},{16,12},{20,16},{24,20},{28,24},{32,28},{36,32}... | collective-permute-start | bytes 811016 | tf_op jit(solution)/shard_map/ppermute | solution.py:590
  27.6 2.2 %collective-permute-start.4 = (f32[4,1024]{1,0:T(4,128)S(1)}, f32[4,1024]{1,0:T(4,128)S(1)}, u32[]{:S(2)}, u32[]{:S(2)}) collective-permute-start(f32[4,1024]{1,0:T(4,128)S(1)} %get-tuple-element.67), channel_id=1, source_target_pairs={{0,1},{1,0},{2,3},{3,2},{4,5},{5,4},{6,7},{7,6},{8,9},{9,8},{10,11... | collective-permute-start | bytes 49160 | tf_op jit(solution)/shard_map/ppermute | solution.py:604
  29.8 4.1 %collective-permute-start.5 = (f32[4,1024]{1,0:T(4,128)S(1)}, f32[4,1024]{1,0:T(4,128)S(1)}, u32[]{:S(2)}, u32[]{:S(2)}) collective-permute-start(f32[4,1024]{1,0:T(4,128)S(1)} %add.6), channel_id=1, source_target_pairs={{0,2},{1,3},{2,0},{3,1},{4,6},{5,7},{6,4},{7,5},{8,10},{9,11},{10,... | collective-permute-start | bytes 49160 | tf_op jit(solution)/shard_map/ppermute | solution.py:604

commit v5 on v4

--- a/solution.py
+++ b/solution.py
@@ -422,8 +422,6 @@
         for copy in copies[1:]:
             copy.wait()
 
-    slab = pltpu.with_memory_space_constraint(slab, pltpu.HBM)
-    angles = pltpu.with_memory_space_constraint(angles, pltpu.HBM)
     return pl.pallas_call(
         kernel,
         out_shape=[jax.ShapeDtypeStruct(shape, jnp.float32) for shape in shapes]
@@ -575,6 +573,8 @@
 
 
 def on_device(slab, angles, pairing, band_offsets, band_weights):
+    slab = pltpu.with_memory_space_constraint(slab, pltpu.HBM)
+    angles = pltpu.with_memory_space_constraint(angles, pltpu.HBM)
     count = lax.axis_size("blk")
     onward = [(i, (i + 1) % count) for i in range(count)]
     back = [((i + 1) % count, i) for i in range(count)]

time: 34.6 us -> 34.6 us (level)
  waiting for transfers between devices: 3.9 us -> 3.49 us
    ppermute x1, waiting for transfers between devices: 1.58 us -> 1.17 us  [on_device(): before_far = lax.ppermute(far_tail, 'blk', onward)]
  transfers between devices with their start and end apart: 6 -> 6, of which waited for: 3 -> 3; matrix products, arithmetic and copies ran while one was open for 0% -> 0% of each run, Pallas kernels for 40% -> 41%
where the time goes in v5:
time: 34.6 us; the launch traced here: 34.4 us
  Pallas kernels  17 us (49%)
  starting transfers between devices  12.6 us (36%)
  waiting for transfers between devices  3.49 us (10%)
  between operations  0.72 us (2%)
  other arithmetic  0.62 us (2%)
    pallas_call x1, Pallas kernels, inner_call(): pl.pallas_call(inner_kernel, out_shape=(EVOLVED, STATES, ADJOINT, jax.Sha...  5.51 us
    ppermute x2, starting transfers between devices, on_device(): lax.ppermute(gradient, 'col', [(i, i ^ step) for i in range(columns)])  3.94 us
    ppermute x1, starting transfers between devices, on_device(): after = lax.ppermute(head, 'blk', back)  3.89 us
    pallas_call x1, Pallas kernels, early_call(): pl.pallas_call(early_kernel, out_shape=(STATES, TABLE) + tuple((jax.Shape...  2.7 us
    ppermute x2, waiting for transfers between devices, on_device(): lax.ppermute(gradient, 'col', [(i, i ^ step) for i in range(columns)])  2.31 us
    pallas_call x1, Pallas kernels, left_call(): pl.pallas_call(left_kernel, out_shape=(EVOLVED, STATES, ADJOINT, TABLE, H...  2.14 us
    pallas_call x1, Pallas kernels, right_call(): pl.pallas_call(right_kernel, out_shape=(EVOLVED, STATES, ADJOINT, TABLE,...  2.13 us
    ppermute x1, starting transfers between devices, on_device(): before = lax.ppermute(tail, 'blk', onward)  2.12 us
  transfers between devices with their start and end apart: 6, of which 3 were waited for; matrix products, arithmetic and copies ran while one was open for 0% of the time, Pallas kernels for 41%

profile of v5, /device:TPU:1, one launch (start us, length us, event | category | flops | bytes accessed | tf_op | source)
XLA Modules:
  0.0 34.4 jit_solution(16720668192542128069)
XLA Ops:
  0.6 1.3 %pack.1 = (f32[288,256]{1,0:T(8,128)S(1)}, f32[272,256]{1,0:T(8,128)S(1)}, f32[264,256]{1,0:T(8,128)S(1)}, f32[264,256]{1,0:T(8,128)S(1)}, s32[4]{0:T(128)S(1)},...) custom-call(f32[2048,256]{1,0:T(8,128)} %slab.9, f32[4,1024]{1,0:T(4,128)} %angles.1, s32[4]{0:T(128)} %refs_0_.1, ...), custom_call_target="tpu_custom_call" | custom-call | flops 1000 | bytes 1048576 | tf_op jit(solution)/shard_map/pack/pallas_call | solution.py:425
  2.0 2.1 %collective-permute-start.1 = (f32[288,256]{1,0:T(8,128)S(1)}, f32[288,256]{1,0:T(8,128)S(1)}, u32[]{:S(2)}, u32[]{:S(2)}) collective-permute-start(f32[288,256]{1,0:T(8,128)S(1)} %get-tuple-element.47), channel_id=1, source_target_pairs={{0,4},{4,8},{8,12},{12,16},{16,20},{20,24},{24,28},{28,32},{32,36}... | collective-permute-start | bytes 884744 | tf_op jit(solution)/shard_map/ppermute | solution.py:586
  4.1 1.2 %collective-permute-start.3 = (f32[272,256]{1,0:T(8,128)S(1)}, f32[272,256]{1,0:T(8,128)S(1)}, u32[]{:S(2)}, u32[]{:S(2)}) collective-permute-start(f32[272,256]{1,0:T(8,128)S(1)} %get-tuple-element.61), channel_id=1, source_target_pairs={{0,4},{4,8},{8,12},{12,16},{16,20},{20,24},{24,28},{28,32},{32,36}... | collective-permute-start | bytes 835592 | tf_op jit(solution)/shard_map/ppermute | solution.py:587
  5.3 2.7 %early.1 = (f32[4,2,2,1568,128]{4,3,2,1,0:T(8,128)S(1)}, f32[8,1056,128]{2,1,0:T(8,128)S(1)}, f32[264,256]{1,0:T(8,128)S(1)}, f32[264,256]{1,0:T(8,128)S(1)}) custom-call(s32[4]{0:T(128)S(1)} %get-tuple-element.35.pairing, f32[2048,256]{1,0:T(8,128)} %slab.9, f32[4,1024]{1,0:T(4,128)S(1)} %get-tuple-element.38.angles, ...), custom_call_target="tpu_custom_call", output_to_operand_aliasing={{2}: (3, {}), {3}: (4, {})} | custom-call | flops 12000000 | bytes 8388608 | tf_op jit(solution)/shard_map/early/pallas_call | solution.py:447
  8.0 3.9 %collective-permute-start = (f32[264,256]{1,0:T(8,128)S(1)}, f32[264,256]{1,0:T(8,128)S(1)}, u32[]{:S(2)}, u32[]{:S(2)}) collective-permute-start(f32[264,256]{1,0:T(8,128)S(1)} %get-tuple-element.41), channel_id=1, source_target_pairs={{4,0},{8,4},{12,8},{16,12},{20,16},{24,20},{28,24},{32,28},{36,32}... | collective-permute-start | bytes 811016 | tf_op jit(solution)/shard_map/ppermute | solution.py:589
  11.9 1.4 %collective-permute-start.2 = (f32[264,256]{1,0:T(8,128)S(1)}, f32[264,256]{1,0:T(8,128)S(1)}, u32[]{:S(2)}, u32[]{:S(2)}) collective-permute-start(f32[264,256]{1,0:T(8,128)S(1)} %get-tuple-element.57), channel_id=1, source_target_pairs={{4,0},{8,4},{12,8},{16,12},{20,16},{24,20},{28,24},{32,28},{36,32}... | collective-permute-start | bytes 811016 | tf_op jit(solution)/shard_map/ppermute | solution.py:590
  13.4 5.5 %inner.1 = (f32[2048,256]{1,0:T(8,128)}, f32[4,2,2,1568,128]{4,3,2,1,0:T(8,128)S(1)}, f32[2,2,1056,128]{3,2,1,0:T(8,128)S(1)}, f32[4,512]{1,0:T(4,128)S(1)}) custom-call(s32[4]{0:T(128)S(1)} %get-tuple-element.35.pairing, s32[8]{0:T(128)S(1)} %get-tuple-element.36.offsets, f32[8]{0:T(128)S(1)} %get-tuple-element.37.weights, ...), custom_call_target="tpu_custom_call", output_to_operand_aliasing={{1}: (3, {})} | custom-call | flops 50000000 | bytes 16777216 | tf_op jit(solution)/shard_map/inner/pallas_call | solution.py:473
  18.9 0.0 collective-permute-done.1.before
  18.9 2.1 %left.1 = (f32[2048,256]{1,0:T(8,128)}, f32[4,2,2,1568,128]{4,3,2,1,0:T(8,128)S(1)}, f32[2,2,1056,128]{3,2,1,0:T(8,128)S(1)}, f32[8,1056,128]{2,1,0:T(8,128)S(1)...) custom-call(s32[4]{0:T(128)S(1)} %get-tuple-element.35.pairing, ...), custom_call_target="tpu_custom_call", output_to_operand_aliasing={{0}: (5, {}), {1}: (6, {}), {2}: (7, {}), {3}: (8, {})} | custom-call | flops 15000000 | bytes 8388608 | tf_op jit(solution)/shard_map/left/pallas_call | solution.py:492
  21.1 0.0 collective-permute-done.after
  21.1 2.1 %right.1 = (f32[2048,256]{1,0:T(8,128)}, f32[4,2,2,1568,128]{4,3,2,1,0:T(8,128)S(1)}, f32[2,2,1056,128]{3,2,1,0:T(8,128)S(1)}, f32[8,1056,128]{2,1,0:T(8,128)S(1...) custom-call(s32[4]{0:T(128)S(1)} %get-tuple-element.35.pairing, ...), custom_call_target="tpu_custom_call", output_to_operand_aliasing={{0}: (7, {}), {1}: (8, {}), {2}: (9, {}), {3}: (10, {})} | custom-call | flops 15000000 | bytes 8388608 | tf_op jit(solution)/shard_map/right/pallas_call | solution.py:534
  23.2 1.2 %collective-permute-done.3.before_far = f32[272,256]{1,0:T(8,128)S(1)} collective-permute-done((f32[272,256]{1,0:T(8,128)S(1)}, f32[272,256]{1,0:T(8,128)S(1)}, u32[]{:S(2)}, u32[]{:S(2)}) %collective-permute-start.3) | collective-permute-done | bytes 278560 | tf_op jit(solution)/shard_map/ppermute | solution.py:587
  24.4 1.4 %left_far.1 = (f32[2,2,1056,128]{3,2,1,0:T(8,128)S(1)}, f32[4,896]{1,0:T(4,128)S(1)}) custom-call(s32[4]{0:T(128)S(1)} %get-tuple-element.35.pairing, s32[8]{0:T(128)S(1)} %get-tuple-element.36.offsets, f32[8]{0:T(128)S(1)} %get-tuple-element.37.weights, f32[288,256]{1,0:T(8,128)S(1)} %collective-permute-done.1.before, ...), custom_call_target="tpu_custom_call", output_to_operand_aliasing={{0}: (9, {})} | custom-call | flops 10000000 | bytes 8388608 | tf_op jit(solution)/shard_map/left_far/pallas_call | solution.py:514
  25.8 0.0 collective-permute-done.2.after_far
  25.8 1.7 %right_far.1 = (f32[2,2,1056,128]{3,2,1,0:T(8,128)S(1)}, f32[4,1024]{1,0:T(4,128)S(1)}) custom-call(s32[4]{0:T(128)S(1)} %get-tuple-element.35.pairing, s32[8]{0:T(128)S(1)} %get-tuple-element.36.offsets, f32[8]{0:T(128)S(1)} %get-tuple-element.37.weights, f32[264,256]{1,0:T(8,128)S(1)} %collective-permute-done.after, ...), custom_call_target="tpu_custom_call", output_to_operand_aliasing={{0}: (9, {})} | custom-call | flops 10000000 | bytes 8388608 | tf_op jit(solution)/shard_map/right_far/pallas_call | solution.py:556
  27.5 1.3 %collective-permute-start.4 = (f32[4,1024]{1,0:T(4,128)S(1)}, f32[4,1024]{1,0:T(4,128)S(1)}, u32[]{:S(2)}, u32[]{:S(2)}) collective-permute-start(f32[4,1024]{1,0:T(4,128)S(1)} %get-tuple-element.67), channel_id=1, source_target_pairs={{0,1},{1,0},{2,3},{3,2},{4,5},{5,4},{6,7},{7,6},{8,9},{9,8},{10,11... | collective-permute-start | bytes 49160 | tf_op jit(solution)/shard_map/ppermute | solution.py:604
  28.8 0.8 %collective-permute-done.4 = f32[4,1024]{1,0:T(4,128)S(1)} collective-permute-done((f32[4,1024]{1,0:T(4,128)S(1)}, f32[4,1024]{1,0:T(4,128)S(1)}, u32[]{:S(2)}, u32[]{:S(2)}) %collective-permute-start.4) | collective-permute-done | bytes 16416 | tf_op jit(solution)/shard_map/ppermute | solution.py:604
  29.7 2.6 %collective-permute-start.5 = (f32[4,1024]{1,0:T(4,128)S(1)}, f32[4,1024]{1,0:T(4,128)S(1)}, u32[]{:S(2)}, u32[]{:S(2)}) collective-permute-start(f32[4,1024]{1,0:T(4,128)S(1)} %add.6), channel_id=1, source_target_pairs={{0,2},{1,3},{2,0},{3,1},{4,6},{5,7},{6,4},{7,5},{8,10},{9,11},{10,... | collective-permute-start | bytes 49160 | tf_op jit(solution)/shard_map/ppermute | solution.py:604
  32.3 1.5 %collective-permute-done.5 = f32[4,1024]{1,0:T(4,128)S(1)} collective-permute-done((f32[4,1024]{1,0:T(4,128)S(1)}, f32[4,1024]{1,0:T(4,128)S(1)}, u32[]{:S(2)}, u32[]{:S(2)}) %collective-permute-start.5) | collective-permute-done | bytes 16416 | tf_op jit(solution)/shard_map/ppermute | solution.py:604
  33.8 0.6 %add.7 = f32[4,1024]{1,0:T(4,128)} add(f32[4,1024]{1,0:T(4,128)S(1)} %add.6, f32[4,1024]{1,0:T(4,128)S(1)} %collective-permute-done.5) | non-fusion elementwise | flops 4096 | bytes 49152 | tf_op jit(solution)/shard_map/add | solution.py:604
  (2 shorter events, 0.0 us)
Async XLA Ops:
  2.0 16.9 %collective-permute-start.1 = (f32[288,256]{1,0:T(8,128)S(1)}, f32[288,256]{1,0:T(8,128)S(1)}, u32[]{:S(2)}, u32[]{:S(2)}) collective-permute-start(f32[288,256]{1,0:T(8,128)S(1)} %get-tuple-element.47), channel_id=1, source_target_pairs={{0,4},{4,8},{8,12},{12,16},{16,20},{20,24},{24,28},{28,32},{32,36}... | collective-permute-start | bytes 884744 | tf_op jit(solution)/shard_map/ppermute | solution.py:586
  4.1 20.3 %collective-permute-start.3 = (f32[272,256]{1,0:T(8,128)S(1)}, f32[272,256]{1,0:T(8,128)S(1)}, u32[]{:S(2)}, u32[]{:S(2)}) collective-permute-start(f32[272,256]{1,0:T(8,128)S(1)} %get-tuple-element.61), channel_id=1, source_target_pairs={{0,4},{4,8},{8,12},{12,16},{16,20},{20,24},{24,28},{28,32},{32,36}... | collective-permute-start | bytes 835592 | tf_op jit(solution)/shard_map/ppermute | solution.py:587
  8.0 13.0 %collective-permute-start = (f32[264,256]{1,0:T(8,128)S(1)}, f32[264,256]{1,0:T(8,128)S(1)}, u32[]{:S(2)}, u32[]{:S(2)}) collective-permute-start(f32[264,256]{1,0:T(8,128)S(1)} %get-tuple-element.41), channel_id=1, source_target_pairs={{4,0},{8,4},{12,8},{16,12},{20,16},{24,20},{28,24},{32,28},{36,32}... | collective-permute-start | bytes 811016 | tf_op jit(solution)/shard_map/ppermute | solution.py:589
  11.9 13.9 %collective-permute-start.2 = (f32[264,256]{1,0:T(8,128)S(1)}, f32[264,256]{1,0:T(8,128)S(1)}, u32[]{:S(2)}, u32[]{:S(2)}) collective-permute-start(f32[264,256]{1,0:T(8,128)S(1)} %get-tuple-element.57), channel_id=1, source_target_pairs={{4,0},{8,4},{12,8},{16,12},{20,16},{24,20},{28,24},{32,28},{36,32}... | collective-permute-start | bytes 811016 | tf_op jit(solution)/shard_map/ppermute | solution.py:590
  27.5 2.2 %collective-permute-start.4 = (f32[4,1024]{1,0:T(4,128)S(1)}, f32[4,1024]{1,0:T(4,128)S(1)}, u32[]{:S(2)}, u32[]{:S(2)}) collective-permute-start(f32[4,1024]{1,0:T(4,128)S(1)} %get-tuple-element.67), channel_id=1, source_target_pairs={{0,1},{1,0},{2,3},{3,2},{4,5},{5,4},{6,7},{7,6},{8,9},{9,8},{10,11... | collective-permute-start | bytes 49160 | tf_op jit(solution)/shard_map/ppermute | solution.py:604
  29.7 4.1 %collective-permute-start.5 = (f32[4,1024]{1,0:T(4,128)S(1)}, f32[4,1024]{1,0:T(4,128)S(1)}, u32[]{:S(2)}, u32[]{:S(2)}) collective-permute-start(f32[4,1024]{1,0:T(4,128)S(1)} %add.6), channel_id=1, source_target_pairs={{0,2},{1,3},{2,0},{3,1},{4,6},{5,7},{6,4},{7,5},{8,10},{9,11},{10,... | collective-permute-start | bytes 49160 | tf_op jit(solution)/shard_map/ppermute | solution.py:604

commit v6 on v5

--- a/solution.py
+++ b/solution.py
@@ -599,10 +599,10 @@
     adjoint, rest = left_far_call(*scalars, before, before_far, states, table, left_table, rest, adjoint)
     _, gradient = right_far_call(*scalars, after, after_far, states, table, right_table, rest, adjoint)
     columns = lax.axis_size("col")
-    step = 1
-    while step < columns:
+    step = columns // 2
+    while step:
         gradient = gradient + lax.ppermute(gradient, "col", [(i, i ^ step) for i in range(columns)])
-        step *= 2
+        step //= 2
     return (evolved, gradient)
 
 

time: 34.6 us -> 35.7 us (1.032)
  starting transfers between devices: 12.6 us -> 13.7 us
    ppermute x2, starting transfers between devices: 3.94 us -> 5.09 us  [on_device(): lax.ppermute(gradient, 'col', [(i, i ^ step) for i in range(columns)])]
  transfers between devices with their start and end apart: 6 -> 6, of which waited for: 3 -> 3; matrix products, arithmetic and copies ran while one was open for 0% -> 0% of each run, Pallas kernels for 41% -> 39%
where the time goes in v6:
time: 35.7 us; the launch traced here: 35.5 us
  Pallas kernels  16.9 us (47%)
  starting transfers between devices  13.7 us (38%)
  waiting for transfers between devices  3.52 us (10%)
  between operations  0.72 us (2%)
  other arithmetic  0.62 us (2%)
    pallas_call x1, Pallas kernels, inner_call(): pl.pallas_call(inner_kernel, out_shape=(EVOLVED, STATES, ADJOINT, jax.Sha...  5.47 us
    ppermute x2, starting transfers between devices, on_device(): lax.ppermute(gradient, 'col', [(i, i ^ step) for i in range(columns)])  5.09 us
    ppermute x1, starting transfers between devices, on_device(): after = lax.ppermute(head, 'blk', back)  3.89 us
    pallas_call x1, Pallas kernels, early_call(): pl.pallas_call(early_kernel, out_shape=(STATES, TABLE) + tuple((jax.Shape...  2.7 us
    ppermute x2, waiting for transfers between devices, on_device(): lax.ppermute(gradient, 'col', [(i, i ^ step) for i in range(columns)])  2.31 us
    pallas_call x1, Pallas kernels, right_call(): pl.pallas_call(right_kernel, out_shape=(EVOLVED, STATES, ADJOINT, TABLE,...  2.14 us
    pallas_call x1, Pallas kernels, left_call(): pl.pallas_call(left_kernel, out_shape=(EVOLVED, STATES, ADJOINT, TABLE, H...  2.14 us
    ppermute x1, starting transfers between devices, on_device(): before = lax.ppermute(tail, 'blk', onward)  2.12 us
  transfers between devices with their start and end apart: 6, of which 3 were waited for; matrix products, arithmetic and copies ran while one was open for 0% of the time, Pallas kernels for 39%

profile of v6, /device:TPU:1, one launch (start us, length us, event | category | flops | bytes accessed | tf_op | source)
XLA Modules:
  0.0 35.5 jit_solution(17129747959575629122)
XLA Ops:
  0.6 1.3 %pack.1 = (f32[288,256]{1,0:T(8,128)S(1)}, f32[272,256]{1,0:T(8,128)S(1)}, f32[264,256]{1,0:T(8,128)S(1)}, f32[264,256]{1,0:T(8,128)S(1)}, s32[4]{0:T(128)S(1)},...) custom-call(f32[2048,256]{1,0:T(8,128)} %slab.9, f32[4,1024]{1,0:T(4,128)} %angles.1, s32[4]{0:T(128)} %refs_0_.1, ...), custom_call_target="tpu_custom_call" | custom-call | flops 1000 | bytes 1048576 | tf_op jit(solution)/shard_map/pack/pallas_call | solution.py:425
  2.0 2.1 %collective-permute-start.1 = (f32[288,256]{1,0:T(8,128)S(1)}, f32[288,256]{1,0:T(8,128)S(1)}, u32[]{:S(2)}, u32[]{:S(2)}) collective-permute-start(f32[288,256]{1,0:T(8,128)S(1)} %get-tuple-element.47), channel_id=1, source_target_pairs={{0,4},{4,8},{8,12},{12,16},{16,20},{20,24},{24,28},{28,32},{32,36}... | collective-permute-start | bytes 884744 | tf_op jit(solution)/shard_map/ppermute | solution.py:586
  4.1 1.2 %collective-permute-start.3 = (f32[272,256]{1,0:T(8,128)S(1)}, f32[272,256]{1,0:T(8,128)S(1)}, u32[]{:S(2)}, u32[]{:S(2)}) collective-permute-start(f32[272,256]{1,0:T(8,128)S(1)} %get-tuple-element.61), channel_id=1, source_target_pairs={{0,4},{4,8},{8,12},{12,16},{16,20},{20,24},{24,28},{28,32},{32,36}... | collective-permute-start | bytes 835592 | tf_op jit(solution)/shard_map/ppermute | solution.py:587
  5.3 2.7 %early.1 = (f32[4,2,2,1568,128]{4,3,2,1,0:T(8,128)S(1)}, f32[8,1056,128]{2,1,0:T(8,128)S(1)}, f32[264,256]{1,0:T(8,128)S(1)}, f32[264,256]{1,0:T(8,128)S(1)}) custom-call(s32[4]{0:T(128)S(1)} %get-tuple-element.35.pairing, f32[2048,256]{1,0:T(8,128)} %slab.9, f32[4,1024]{1,0:T(4,128)S(1)} %get-tuple-element.38.angles, ...), custom_call_target="tpu_custom_call", output_to_operand_aliasing={{2}: (3, {}), {3}: (4, {})} | custom-call | flops 12000000 | bytes 8388608 | tf_op jit(solution)/shard_map/early/pallas_call | solution.py:447
  8.0 3.9 %collective-permute-start = (f32[264,256]{1,0:T(8,128)S(1)}, f32[264,256]{1,0:T(8,128)S(1)}, u32[]{:S(2)}, u32[]{:S(2)}) collective-permute-start(f32[264,256]{1,0:T(8,128)S(1)} %get-tuple-element.41), channel_id=1, source_target_pairs={{4,0},{8,4},{12,8},{16,12},{20,16},{24,20},{28,24},{32,28},{36,32}... | collective-permute-start | bytes 811016 | tf_op jit(solution)/shard_map/ppermute | solution.py:589
  11.9 1.4 %collective-permute-start.2 = (f32[264,256]{1,0:T(8,128)S(1)}, f32[264,256]{1,0:T(8,128)S(1)}, u32[]{:S(2)}, u32[]{:S(2)}) collective-permute-start(f32[264,256]{1,0:T(8,128)S(1)} %get-tuple-element.57), channel_id=1, source_target_pairs={{4,0},{8,4},{12,8},{16,12},{20,16},{24,20},{28,24},{32,28},{36,32}... | collective-permute-start | bytes 811016 | tf_op jit(solution)/shard_map/ppermute | solution.py:590
  13.4 5.5 %inner.1 = (f32[2048,256]{1,0:T(8,128)}, f32[4,2,2,1568,128]{4,3,2,1,0:T(8,128)S(1)}, f32[2,2,1056,128]{3,2,1,0:T(8,128)S(1)}, f32[4,512]{1,0:T(4,128)S(1)}) custom-call(s32[4]{0:T(128)S(1)} %get-tuple-element.35.pairing, s32[8]{0:T(128)S(1)} %get-tuple-element.36.offsets, f32[8]{0:T(128)S(1)} %get-tuple-element.37.weights, ...), custom_call_target="tpu_custom_call", output_to_operand_aliasing={{1}: (3, {})} | custom-call | flops 50000000 | bytes 16777216 | tf_op jit(solution)/shard_map/inner/pallas_call | solution.py:473
  18.9 0.0 collective-permute-done.1.before
  18.9 2.1 %left.1 = (f32[2048,256]{1,0:T(8,128)}, f32[4,2,2,1568,128]{4,3,2,1,0:T(8,128)S(1)}, f32[2,2,1056,128]{3,2,1,0:T(8,128)S(1)}, f32[8,1056,128]{2,1,0:T(8,128)S(1)...) custom-call(s32[4]{0:T(128)S(1)} %get-tuple-element.35.pairing, ...), custom_call_target="tpu_custom_call", output_to_operand_aliasing={{0}: (5, {}), {1}: (6, {}), {2}: (7, {}), {3}: (8, {})} | custom-call | flops 15000000 | bytes 8388608 | tf_op jit(solution)/shard_map/left/pallas_call | solution.py:492
  21.0 0.0 collective-permute-done.after
  21.0 2.1 %right.1 = (f32[2048,256]{1,0:T(8,128)}, f32[4,2,2,1568,128]{4,3,2,1,0:T(8,128)S(1)}, f32[2,2,1056,128]{3,2,1,0:T(8,128)S(1)}, f32[8,1056,128]{2,1,0:T(8,128)S(1...) custom-call(s32[4]{0:T(128)S(1)} %get-tuple-element.35.pairing, ...), custom_call_target="tpu_custom_call", output_to_operand_aliasing={{0}: (7, {}), {1}: (8, {}), {2}: (9, {}), {3}: (10, {})} | custom-call | flops 15000000 | bytes 8388608 | tf_op jit(solution)/shard_map/right/pallas_call | solution.py:534
  23.2 1.2 %collective-permute-done.3.before_far = f32[272,256]{1,0:T(8,128)S(1)} collective-permute-done((f32[272,256]{1,0:T(8,128)S(1)}, f32[272,256]{1,0:T(8,128)S(1)}, u32[]{:S(2)}, u32[]{:S(2)}) %collective-permute-start.3) | collective-permute-done | bytes 278560 | tf_op jit(solution)/shard_map/ppermute | solution.py:587
  24.4 1.4 %left_far.1 = (f32[2,2,1056,128]{3,2,1,0:T(8,128)S(1)}, f32[4,896]{1,0:T(4,128)S(1)}) custom-call(s32[4]{0:T(128)S(1)} %get-tuple-element.35.pairing, s32[8]{0:T(128)S(1)} %get-tuple-element.36.offsets, f32[8]{0:T(128)S(1)} %get-tuple-element.37.weights, f32[288,256]{1,0:T(8,128)S(1)} %collective-permute-done.1.before, ...), custom_call_target="tpu_custom_call", output_to_operand_aliasing={{0}: (9, {})} | custom-call | flops 10000000 | bytes 8388608 | tf_op jit(solution)/shard_map/left_far/pallas_call | solution.py:514
  25.8 0.0 collective-permute-done.2.after_far
  25.8 1.7 %right_far.1 = (f32[2,2,1056,128]{3,2,1,0:T(8,128)S(1)}, f32[4,1024]{1,0:T(4,128)S(1)}) custom-call(s32[4]{0:T(128)S(1)} %get-tuple-element.35.pairing, s32[8]{0:T(128)S(1)} %get-tuple-element.36.offsets, f32[8]{0:T(128)S(1)} %get-tuple-element.37.weights, f32[264,256]{1,0:T(8,128)S(1)} %collective-permute-done.after, ...), custom_call_target="tpu_custom_call", output_to_operand_aliasing={{0}: (9, {})} | custom-call | flops 10000000 | bytes 8388608 | tf_op jit(solution)/shard_map/right_far/pallas_call | solution.py:556
  27.5 2.7 %collective-permute-start.4 = (f32[4,1024]{1,0:T(4,128)S(1)}, f32[4,1024]{1,0:T(4,128)S(1)}, u32[]{:S(2)}, u32[]{:S(2)}) collective-permute-start(f32[4,1024]{1,0:T(4,128)S(1)} %get-tuple-element.67), channel_id=1, source_target_pairs={{0,2},{1,3},{2,0},{3,1},{4,6},{5,7},{6,4},{7,5},{8,10},{9,11},{10,... | collective-permute-start | bytes 49160 | tf_op jit(solution)/shard_map/ppermute | solution.py:604
  30.2 1.5 %collective-permute-done.4 = f32[4,1024]{1,0:T(4,128)S(1)} collective-permute-done((f32[4,1024]{1,0:T(4,128)S(1)}, f32[4,1024]{1,0:T(4,128)S(1)}, u32[]{:S(2)}, u32[]{:S(2)}) %collective-permute-start.4) | collective-permute-done | bytes 16416 | tf_op jit(solution)/shard_map/ppermute | solution.py:604
  31.7 2.4 %collective-permute-start.5 = (f32[4,1024]{1,0:T(4,128)S(1)}, f32[4,1024]{1,0:T(4,128)S(1)}, u32[]{:S(2)}, u32[]{:S(2)}) collective-permute-start(f32[4,1024]{1,0:T(4,128)S(1)} %add.6), channel_id=1, source_target_pairs={{0,1},{1,0},{2,3},{3,2},{4,5},{5,4},{6,7},{7,6},{8,9},{9,8},{10,11... | collective-permute-start | bytes 49160 | tf_op jit(solution)/shard_map/ppermute | solution.py:604
  34.0 0.8 %collective-permute-done.5 = f32[4,1024]{1,0:T(4,128)S(1)} collective-permute-done((f32[4,1024]{1,0:T(4,128)S(1)}, f32[4,1024]{1,0:T(4,128)S(1)}, u32[]{:S(2)}, u32[]{:S(2)}) %collective-permute-start.5) | collective-permute-done | bytes 16416 | tf_op jit(solution)/shard_map/ppermute | solution.py:604
  34.9 0.6 %add.7 = f32[4,1024]{1,0:T(4,128)} add(f32[4,1024]{1,0:T(4,128)S(1)} %add.6, f32[4,1024]{1,0:T(4,128)S(1)} %collective-permute-done.5) | non-fusion elementwise | flops 4096 | bytes 49152 | tf_op jit(solution)/shard_map/add | solution.py:604
  (2 shorter events, 0.0 us)
Async XLA Ops:
  2.0 16.9 %collective-permute-start.1 = (f32[288,256]{1,0:T(8,128)S(1)}, f32[288,256]{1,0:T(8,128)S(1)}, u32[]{:S(2)}, u32[]{:S(2)}) collective-permute-start(f32[288,256]{1,0:T(8,128)S(1)} %get-tuple-element.47), channel_id=1, source_target_pairs={{0,4},{4,8},{8,12},{12,16},{16,20},{20,24},{24,28},{28,32},{32,36}... | collective-permute-start | bytes 884744 | tf_op jit(solution)/shard_map/ppermute | solution.py:586
  4.1 20.3 %collective-permute-start.3 = (f32[272,256]{1,0:T(8,128)S(1)}, f32[272,256]{1,0:T(8,128)S(1)}, u32[]{:S(2)}, u32[]{:S(2)}) collective-permute-start(f32[272,256]{1,0:T(8,128)S(1)} %get-tuple-element.61), channel_id=1, source_target_pairs={{0,4},{4,8},{8,12},{12,16},{16,20},{20,24},{24,28},{28,32},{32,36}... | collective-permute-start | bytes 835592 | tf_op jit(solution)/shard_map/ppermute | solution.py:587
  8.0 13.0 %collective-permute-start = (f32[264,256]{1,0:T(8,128)S(1)}, f32[264,256]{1,0:T(8,128)S(1)}, u32[]{:S(2)}, u32[]{:S(2)}) collective-permute-start(f32[264,256]{1,0:T(8,128)S(1)} %get-tuple-element.41), channel_id=1, source_target_pairs={{4,0},{8,4},{12,8},{16,12},{20,16},{24,20},{28,24},{32,28},{36,32}... | collective-permute-start | bytes 811016 | tf_op jit(solution)/shard_map/ppermute | solution.py:589
  11.9 13.9 %collective-permute-start.2 = (f32[264,256]{1,0:T(8,128)S(1)}, f32[264,256]{1,0:T(8,128)S(1)}, u32[]{:S(2)}, u32[]{:S(2)}) collective-permute-start(f32[264,256]{1,0:T(8,128)S(1)} %get-tuple-element.57), channel_id=1, source_target_pairs={{4,0},{8,4},{12,8},{16,12},{20,16},{24,20},{28,24},{32,28},{36,32}... | collective-permute-start | bytes 811016 | tf_op jit(solution)/shard_map/ppermute | solution.py:590
  27.5 4.2 %collective-permute-start.4 = (f32[4,1024]{1,0:T(4,128)S(1)}, f32[4,1024]{1,0:T(4,128)S(1)}, u32[]{:S(2)}, u32[]{:S(2)}) collective-permute-start(f32[4,1024]{1,0:T(4,128)S(1)} %get-tuple-element.67), channel_id=1, source_target_pairs={{0,2},{1,3},{2,0},{3,1},{4,6},{5,7},{6,4},{7,5},{8,10},{9,11},{10,... | collective-permute-start | bytes 49160 | tf_op jit(solution)/shard_map/ppermute | solution.py:604
  31.7 3.2 %collective-permute-start.5 = (f32[4,1024]{1,0:T(4,128)S(1)}, f32[4,1024]{1,0:T(4,128)S(1)}, u32[]{:S(2)}, u32[]{:S(2)}) collective-permute-start(f32[4,1024]{1,0:T(4,128)S(1)} %add.6), channel_id=1, source_target_pairs={{0,1},{1,0},{2,3},{3,2},{4,5},{5,4},{6,7},{7,6},{8,9},{9,8},{10,11... | collective-permute-start | bytes 49160 | tf_op jit(solution)/shard_map/ppermute | solution.py:604
